TPU v7x, 128 devices: a whole 4x4x4 slice. The times are simulated.
128 devices in a mesh: tm: 32 (over z, y, core), head: 4 (over x).
Axes of the slice: x: 4, y: 4, z: 4, core: 2. Of those that a mesh axis runs over, the one named last changes fastest.
Arguments:
- queries: bfloat16 [16384, 1280], P('tm', 'head'), may hold values from -6 to 6
- key_rows: bfloat16 [16384, 1280], P('tm', 'head'), may hold values from -6 to 6
- value_rows: bfloat16 [16384, 1280], P('tm', 'head'), may hold values from -6 to 6
- cotangent: bfloat16 [16384, 1280], P('tm', 'head'), may hold values from -6 to 6
- out_weight: bfloat16 [1280, 1280], P('head'), may hold values from -0.15625 to 0.15625
- segment_units: int32 [64], replicated, may hold values from 1 to 32, as said below
- left_segments: int32 [64], replicated, may hold values from 0 to 4, as said below
Outputs:
- query_grad: bfloat16 [16384, 1280], P('tm', 'head')
- key_grad: bfloat16 [16384, 1280], P('tm', 'head')
- value_grad: bfloat16 [16384, 1280], P('tm', 'head')
- out_weight_grad: float32 [1280, 1280], P('head', 'tm')
Inputs may be any that keep to these rules, and one draw needn't show every extreme that they name: `segment_units`: the segments cover all 16384 frames in order; some segment has exactly 32 units. `left_segments`: some segment has exactly 4.
All inputs are finite; a program needn't handle non-finite values.
Results may differ from a plain program's by a relative error of at most 0.0085.
Values may be sent and summed in bfloat16 or wider, within the bound.
A program may use at most 64 MiB of HBM per device.

v0:
```python
import jax
import jax.numpy as jnp
from jax import lax
from jax.sharding import PartitionSpec as P

HS = 64
UNIT = 16
MOSTU = 32
LEFT_MAX = 4


masked_score = -1e30


def for_sending(shard):
    return jax.tree.map(lambda a: a.astype(jnp.bfloat16) if a.dtype == jnp.float32 else a, shard)


def shifted(shard, axis, by):
    size = lax.axis_size(axis)
    pairs = [(i, i + by) for i in range(size) if 0 <= i + by < size]
    return lax.ppermute(shard, axis, pairs)


def segment_bounds(frames, segment_units, left_segments):
    segment_ends = jnp.cumsum(segment_units) * UNIT
    segment_starts = segment_ends - segment_units * UNIT
    number = jnp.arange(segment_units.shape[0], dtype=jnp.int32)
    owner_segment = jnp.sum(
        (segment_ends[None, :] <= frames[:, None]).astype(jnp.int32), axis=1, dtype=jnp.int32
    )
    match_own = number[None, :] == owner_segment[:, None]
    reach_back = jnp.sum(jnp.where(match_own, left_segments[None, :], 0), axis=1, dtype=jnp.int32)
    upper_end = jnp.sum(jnp.where(match_own, segment_ends[None, :], 0), axis=1, dtype=jnp.int32)
    lowest = jnp.maximum(owner_segment - reach_back, 0)
    lower_end = jnp.sum(
        jnp.where(number[None, :] == lowest[:, None], segment_starts[None, :], 0),
        axis=1,
        dtype=jnp.int32,
    )
    return (lower_end, upper_end)


def touches(lower_end, upper_end, key_first, key_count):
    return jnp.any(
        jnp.maximum(lower_end, key_first) < jnp.minimum(upper_end, key_first + key_count)
    )


def visible_mask(lower_end, upper_end, key_first, key_count):
    key_frames = key_first + jnp.arange(key_count, dtype=jnp.int32)
    return (key_frames[None, :] >= lower_end[:, None]) & (key_frames[None, :] < upper_end[:, None])


def forward_update(
    running, query_part, grad_part, key_heads, value_heads, key_first, lower_end, upper_end
):
    maxima, totals, weighted = running
    visible = visible_mask(lower_end, upper_end, key_first, key_heads.shape[0])[None]
    scores = jnp.einsum(
        "qhd,khd->hqk", query_part, key_heads, preferred_element_type=jnp.float32
    ) * HS ** (-0.5)
    scores = jnp.where(visible, scores, masked_score)
    grad_probs = jnp.einsum(
        "qhd,khd->hqk", grad_part, value_heads, preferred_element_type=jnp.float32
    )
    new_max = jnp.maximum(maxima, jnp.max(scores, axis=2))
    weights = jnp.where(visible, jnp.exp(scores - new_max[:, :, None]), 0.0)
    factor = jnp.exp(maxima - new_max)
    return (
        new_max,
        totals * factor + jnp.sum(weights, axis=2),
        weighted * factor + jnp.sum(weights * grad_probs, axis=2),
    )


def backward_tile(
    query_part,
    grad_part,
    key_heads,
    value_heads,
    key_first,
    lower_end,
    upper_end,
    log_total,
    delta_rows,
    with_query,
    with_keys,
):
    visible = visible_mask(lower_end, upper_end, key_first, key_heads.shape[0])[None]
    scores = jnp.einsum(
        "qhd,khd->hqk", query_part, key_heads, preferred_element_type=jnp.float32
    ) * HS ** (-0.5)
    probs_full = jnp.where(visible, jnp.exp(scores - log_total[:, :, None]), 0.0)
    probs_low = probs_full.astype(jnp.bfloat16)
    grad_probs = jnp.einsum(
        "qhd,khd->hqk", grad_part, value_heads, preferred_element_type=jnp.float32
    )
    dscore = (probs_full * (grad_probs - delta_rows[:, :, None])).astype(jnp.bfloat16)
    results = ()
    if with_query:
        results = results + (
            jnp.einsum("hqk,khd->qhd", probs_low, value_heads, preferred_element_type=jnp.float32),
            jnp.einsum("hqk,khd->qhd", dscore, key_heads, preferred_element_type=jnp.float32),
        )
    if with_keys:
        results = results + (
            jnp.einsum("hqk,qhd->khd", dscore, query_part, preferred_element_type=jnp.float32),
            jnp.einsum("hqk,qhd->khd", probs_low, grad_part, preferred_element_type=jnp.float32),
        )
    return results


def shards(queries, key_rows, value_rows, cotangent, out_weight, segment_units, left_segments):
    frames_dev = queries.shape[0]
    head_count = queries.shape[1] // HS
    tm_count = lax.axis_size("tm")
    tm_place = lax.axis_index("tm")
    reach_depth = min(tm_count - 1, ((LEFT_MAX + 1) * MOSTU * UNIT - UNIT - 1) // frames_dev + 1)
    block_rows = min(512, frames_dev)
    windows = [slice(0, block_rows)]
    own_first = tm_place * frames_dev
    frame_steps = jnp.arange(frames_dev, dtype=jnp.int32)
    lower_own, upper_own = segment_bounds(own_first + frame_steps, segment_units, left_segments)
    full_cotangent = lax.all_gather(cotangent, "head", axis=1, tiled=True)
    grad_out = jnp.einsum(
        "fd,ed->fe", full_cotangent, out_weight, preferred_element_type=jnp.float32
    ).astype(jnp.bfloat16)
    query_heads = queries.reshape(frames_dev, head_count, HS)
    key_heads = key_rows.reshape(frames_dev, head_count, HS)
    value_heads = value_rows.reshape(frames_dev, head_count, HS)
    grad_heads = grad_out.reshape(frames_dev, head_count, HS)

    def advance(blocks):
        return jax.tree.map(
            lambda part, own: part.astype(own.dtype), shifted(for_sending(blocks), "tm", 1), blocks
        )

    def forward_all(running, blocks, key_first):
        updated = []
        for portion, window in enumerate(windows):
            updated.append(
                forward_update(
                    running[portion],
                    query_heads,
                    grad_heads,
                    blocks[0],
                    blocks[1],
                    key_first,
                    lower_own,
                    upper_own,
                )
            )
        return tuple(updated)

    start_stats = tuple(
        (
            (
                jnp.full((head_count, block_rows), masked_score, jnp.float32),
                jnp.zeros((head_count, block_rows), jnp.float32),
                jnp.zeros((head_count, block_rows), jnp.float32),
            )
            for window in windows
        )
    )
    row_stats = forward_all(start_stats, (key_heads, value_heads), own_first)
    stored = None

    def first_turn(offset, loop_state):
        blocks, running, kept_blocks = loop_state
        blocks = advance(blocks)
        key_first = (tm_place - offset) * frames_dev
        flag = touches(lower_own, upper_own, key_first, frames_dev)
        running = lax.cond(
            flag,
            lambda current: forward_all(current, blocks, key_first),
            lambda current: current,
            running,
        )
        return (blocks, running, kept_blocks)

    blocks_last, row_stats, stored = lax.fori_loop(
        1, reach_depth + 1, first_turn, ((key_heads, value_heads), row_stats, stored)
    )
    log_total = jnp.concatenate(
        [part_stats[0] + jnp.log(part_stats[1]) for part_stats in row_stats], axis=1
    )
    delta_rows = jnp.concatenate(
        [part_stats[2] / part_stats[1] for part_stats in row_stats], axis=1
    )

    def fetch_block(blocks):
        return advance(blocks)

    def query_side(accums, blocks, key_first, with_keys):
        out_acc, query_acc, key_acc = accums
        results = backward_tile(
            query_heads,
            grad_heads,
            blocks[0],
            blocks[1],
            key_first,
            lower_own,
            upper_own,
            log_total,
            delta_rows,
            True,
            with_keys,
        )
        out_parts = [out_acc + results[0]]
        query_parts = [query_acc + results[1]]
        if with_keys:
            key_acc = (results[2], results[3])
        return (jnp.concatenate(out_parts, axis=0), jnp.concatenate(query_parts, axis=0), key_acc)

    zero_rows = jnp.zeros((frames_dev, head_count, HS), jnp.float32)
    out_acc, query_acc, own_keys = query_side(
        (zero_rows, zero_rows, (zero_rows, zero_rows)), (key_heads, value_heads), own_first, True
    )

    def second_turn(offset, loop_state):
        blocks, out_acc, query_acc = loop_state
        blocks = fetch_block(blocks)
        key_first = (tm_place - offset) * frames_dev

        def visit(current):
            result = query_side((current[0], current[1], None), blocks, key_first, False)
            return (result[0], result[1])

        flag = touches(lower_own, upper_own, key_first, frames_dev)
        out_acc, query_acc = lax.cond(flag, visit, lambda current: current, (out_acc, query_acc))
        return (blocks, out_acc, query_acc)

    blocks_last, out_acc, query_acc = lax.fori_loop(
        1, reach_depth + 1, second_turn, ((key_heads, value_heads), out_acc, query_acc)
    )

    def key_side(key_acc, visiting, lower_end, upper_end):
        results = backward_tile(
            visiting[0],
            visiting[1],
            key_heads,
            value_heads,
            own_first,
            lower_end,
            upper_end,
            visiting[2],
            visiting[3],
            False,
            True,
        )
        key_acc = (key_acc[0] + results[0], key_acc[1] + results[1])
        return key_acc

    def third_turn(offset, loop_state):
        visiting, key_acc = loop_state
        rows_moved = shifted((visiting[0], visiting[1]), "tm", -1)
        stats_moved = shifted((visiting[2], visiting[3]), "tm", -1)
        visiting = (rows_moved[0], rows_moved[1], stats_moved[0], stats_moved[1])
        first_query = (tm_place + offset) * frames_dev
        lower_seen, upper_seen = segment_bounds(
            first_query + frame_steps, segment_units, left_segments
        )
        flag = touches(lower_seen, upper_seen, own_first, frames_dev)
        key_acc = lax.cond(
            flag,
            lambda current: key_side(current, visiting, lower_seen, upper_seen),
            lambda current: current,
            key_acc,
        )
        return (visiting, key_acc)

    visiting_last, (key_sum, value_sum) = lax.fori_loop(
        1, reach_depth + 1, third_turn, ((query_heads, grad_heads, log_total, delta_rows), own_keys)
    )
    scale_factor = HS ** (-0.5)
    head_width = head_count * HS
    attn_out = out_acc.reshape(frames_dev, head_width).astype(jnp.bfloat16)
    weight_term = jnp.einsum(
        "fe,fd->ed", attn_out, full_cotangent, preferred_element_type=jnp.float32
    )
    out_weight_grad = lax.psum_scatter(weight_term, "tm", scatter_dimension=1, tiled=True)
    query_grad = (query_acc * scale_factor).reshape(frames_dev, head_width).astype(jnp.bfloat16)
    key_grad = (key_sum * scale_factor).reshape(frames_dev, head_width).astype(jnp.bfloat16)
    value_grad = value_sum.reshape(frames_dev, head_width).astype(jnp.bfloat16)
    return (query_grad, key_grad, value_grad, out_weight_grad)


def solution(mesh):
    placed = (
        P("tm", "head"),
        P("tm", "head"),
        P("tm", "head"),
        P("tm", "head"),
        P("head", None),
        P(),
        P(),
    )
    return jax.shard_map(
        shards,
        mesh=mesh,
        in_specs=placed,
        out_specs=(P("tm", "head"), P("tm", "head"), P("tm", "head"), P("head", "tm")),
        check_vma=False,
    )
```

profile of v0, /device:TPU:8, one launch (start us, length us, event | category | flops | bytes accessed | tf_op | source)
XLA Modules:
  0.0 416.8 jit_solution(2538383122414679435)
XLA Ops:
  16.8 4.3 %select_reduce_fusion.3 = (f32[5,512]{1,0:T(8,128)S(1)}, f32[5,512,512]{1,2,0:T(8,128)}) fusion(pred[512,512]{0,1:T(8,128)(4,1)S(1)} %compare_and_fusion.3, bf16[512,5,64]{0,2,1:T(8,128)(2,1)S(1)} %bitcast.72, bf16[512,5,64]{0,2,1:T(8,128)(2,1)} %bitcast.76), kind=kOutput, calls=%fused_computation.67 | convolution fusion | flops 171701760 | bytes 6170624 | tf_op jit(solution)/shard_map/qhd,khd->hqk/dot_general | solution.py:91
  21.1 15.8 %all-gather.2.cloned.1.call-done = bf16[512,1280]{0,1:T(8,128)(2,1)} async-done(((bf16[512,320]{0,1:T(8,128)(2,1)}), bf16[512,1280]{0,1:T(8,128)(2,1)}) %all-gather.2.cloned.1.call-update) | async-done | bytes 1310736 | tf_op jit(solution)/shard_map/all_gather | solution.py:125
  39.5 5.6 %multiply_reduce_fusion.1 = (f32[5,512]{1,0:T(8,128)S(1)}, f32[5,512]{1,0:T(8,128)S(1)}, f32[5,512,512]{1,2,0:T(8,128)}) fusion(f32[5,512,512]{1,2,0:T(8,128)} %get-tuple-element.1045, f32[5,512]{1,0:T(8,128)S(1)} %broadcast_maximum_fusion, pred[512,512]{0,1:T(8,128)(4,1)S(1)} %compare_and_fusion.3, bf16[512,5,64]{0,2,1:T(8,128)(2,1)} %bitcast.8, ...), kind=kOutput, calls=%fused_computation.65 | convolution fusion | flops 176942080 | bytes 11433984 | tf_op jit(solution)/shard_map/qhd,khd->hqk/dot_general | solution.py:64
  45.1 73.9 %while.65 = (s32[]{:T(128)}, bf16[512,5,64]{0,2,1:T(8,128)(2,1)S(1)}, bf16[512,5,64]{0,2,1:T(8,128)(2,1)S(1)}, f32[5,512]{1,0:T(8,128)S(1)}, f32[5,512]{1,0:T(8,...) while((s32[]{:T(128)}, ...), condition=%wide.region_15.16_spmd, body=%wide.region_8.15_spmd.sunk | while | flops 354691072 | bytes 22217100 | solution.py:182
  53.5 3.5 collective-permute-done.1
  57.0 5.5 %conditional.7 = ((f32[5,512]{1,0:T(8,128)S(1)}, f32[5,512]{1,0:T(8,128)S(1)}, f32[5,512]{1,0:T(8,128)S(1)})) conditional(s32[]{:T(128)} %convert_element_type.129, (f32[5,512]{1,0:T(8,128)S(1)}, f32[5,512]{1,0:T(8,128)S(1)}, f32[5,512]{1,0:T(8,128)S(1)}) %tuple.129, (s32[]{:T(128)}, s32[512]{0:T(512)S(1)}, s32[512]{0:T(512)S(1)}, ...), branch_computations={%region_10.10_spmd, %region_11.14_spmd} | conditional | flops 354689024 | bytes 18280484 | solution.py:174
  71.0 3.5 collective-permute-done.1
  74.5 5.5 %conditional.7 = ((f32[5,512]{1,0:T(8,128)S(1)}, f32[5,512]{1,0:T(8,128)S(1)}, f32[5,512]{1,0:T(8,128)S(1)})) conditional(s32[]{:T(128)} %convert_element_type.129, (f32[5,512]{1,0:T(8,128)S(1)}, f32[5,512]{1,0:T(8,128)S(1)}, f32[5,512]{1,0:T(8,128)S(1)}) %tuple.129, (s32[]{:T(128)}, s32[512]{0:T(512)S(1)}, s32[512]{0:T(512)S(1)}, ...), branch_computations={%region_10.10_spmd, %region_11.14_spmd} | conditional | flops 354689024 | bytes 18280484 | solution.py:174
  88.4 3.5 collective-permute-done.1
  94.0 9.0 %collective-permute-start.1 = (bf16[512,5,64]{0,2,1:T(8,128)(2,1)S(1)}, bf16[512,5,64]{0,2,1:T(8,128)(2,1)S(1)}, u32[]{:S(2)}, u32[]{:S(2)}) collective-permute-start(bf16[512,5,64]{0,2,1:T(8,128)(2,1)S(1)} %get-tuple-element.1325), channel_id=1, source_target_pairs={{0,4},{4,8},{8,12},{12,16},{16,20},{20,24},{24,28},{28,32},{32,36}... | collective-permute-start | bytes 983048 | tf_op jit(solution)/shard_map/while/body/eval_jaxpr/ppermute | solution.py:22
  104.4 6.1 %collective-permute-start = (bf16[512,5,64]{0,2,1:T(8,128)(2,1)S(1)}, bf16[512,5,64]{0,2,1:T(8,128)(2,1)S(1)}, u32[]{:S(2)}, u32[]{:S(2)}) collective-permute-start(bf16[512,5,64]{0,2,1:T(8,128)(2,1)S(1)} %get-tuple-element.1324), channel_id=1, source_target_pairs={{0,4},{4,8},{8,12},{12,16},{16,20},{20,24},{24,28},{28,32},{32,36}... | collective-permute-start | bytes 983048 | tf_op jit(solution)/shard_map/while/body/eval_jaxpr/ppermute | solution.py:22
  110.5 4.4 %collective-permute-start.1 = (bf16[512,5,64]{0,2,1:T(8,128)(2,1)S(1)}, bf16[512,5,64]{0,2,1:T(8,128)(2,1)S(1)}, u32[]{:S(2)}, u32[]{:S(2)}) collective-permute-start(bf16[512,5,64]{0,2,1:T(8,128)(2,1)S(1)} %get-tuple-element.1325), channel_id=1, source_target_pairs={{0,4},{4,8},{8,12},{12,16},{16,20},{20,24},{24,28},{28,32},{32,36}... | collective-permute-start | bytes 983048 | tf_op jit(solution)/shard_map/while/body/eval_jaxpr/ppermute | solution.py:22
  119.0 4.7 %convolution_bitcast_fusion.2 = f32[512,5,64]{0,2,1:T(8,128)} fusion(bf16[512,5,64]{0,2,1:T(8,128)(2,1)} %bitcast.8, f32[5,512,512]{1,2,0:T(8,128)} %get-tuple-element.1045, f32[5,512]{1,0:T(8,128)S(1)} %get-tuple-element.1394, pred[512,512]{0,1:T(8,128)(4,1)S(1)} %compare_and_fusion.3), kind=kOutput, calls=%fused_computation.72 | convolution fusion | flops 173015040 | bytes 6498304 | tf_op jit(solution)/shard_map/hqk,qhd->khd/dot_general | solution.py:109
  123.8 5.7 %multiply_convert_fusion.12 = bf16[5,512,512]{1,2,0:T(8,128)(2,1)S(1)} fusion(f32[5,512,512]{1,2,0:T(8,128)} %get-tuple-element.1046, f32[5,512,512]{1,2,0:T(8,128)} %get-tuple-element.1045, f32[5,512]{1,0:T(8,128)S(1)} %get-tuple-element.1395, f32[5,512]{1,0:T(8,128)S(1)} %get-tuple-element.1394, pred[512,512]{0,1:T(8,128)(4,1)S(1)} %compare_and_fusion.3), kind=kLoop, calls=%fused_computation.63 | loop fusion | flops 7864320 | bytes 13389824 | tf_op jit(solution)/shard_map/convert_element_type | solution.py:99
  133.9 116.0 %while.66 = (s32[]{:T(128)}, bf16[512,5,64]{0,2,1:T(8,128)(2,1)}, bf16[512,5,64]{0,2,1:T(8,128)(2,1)}, f32[512,5,64]{0,2,1:T(8,128)}, f32[512,5,64]{0,2,1:T(8,12...) while((s32[]{:T(128)}, bf16[512,5,64]{0,2,1:T(8,128)(2,1)}, ...), condition=%wide.region_20.21_spmd, body=%wide.region_16.20_spmd.sunk | while | flops 685312512 | bytes 25078156 | solution.py:234
  137.4 6.2 %collective-permute-start.3 = (bf16[512,5,64]{0,2,1:T(8,128)(2,1)}, bf16[512,5,64]{0,2,1:T(8,128)(2,1)S(1)}, u32[]{:S(2)}, u32[]{:S(2)}) collective-permute-start(bf16[512,5,64]{0,2,1:T(8,128)(2,1)} %get-tuple-element.1365), channel_id=1, source_target_pairs={{0,4},{4,8},{8,12},{12,16},{16,20},{20,24},{24,28},{28,32},{32,36}... | collective-permute-start | bytes 983048 | tf_op jit(solution)/shard_map/while/body/eval_jaxpr/ppermute | solution.py:22
  146.0 14.3 %conditional.8 = ((f32[512,5,64]{0,2,1:T(8,128)}, f32[512,5,64]{0,2,1:T(8,128)})) conditional(s32[]{:T(128)} %convert_element_type.130, (f32[512,5,64]{0,2,1:T(8,128)}, f32[512,5,64]{0,2,1:T(8,128)}) %tuple.132, (s32[]{:T(128)}, s32[512]{0:T(512)S(1)}, s32[512]{0:T(512)S(1)}, bf16[512,5,64]{0,2,1:T(8,128)(2,1)S(1)}, ...), branch_computations={%region_18.18_spmd, %region_19.19_spmd} | conditional | flops 685310464 | bytes 21141532 | solution.py:231
  149.5 6.1 %fusion.20 = f32[512,5,64]{0,2,1:T(8,128)} fusion(f32[512,5,64]{0,2,1:T(8,128)} %get-tuple-element.759, bf16[512,5,64]{0,2,1:T(8,128)(2,1)S(1)} %get-tuple-element.756, f32[5,512,512]{2,1,0:T(8,128)} %fusion.54, f32[5,512]{1,0:T(8,128)S(1)} %get-tuple-element.761, f32[5,512]{1,0:T(8,128)S(1)} %get-tuple-element.757, ...), kind=kOutput, calls=%fused_computation.24 | convolution fusion | flops 343572480 | bytes 7819264 | tf_op jit(solution)/shard_map/while/body/eval_jaxpr/cond/branch_1_fun/hqk,khd->qhd/dot_general | solution.py:104
  155.6 4.8 %fusion.17 = f32[512,5,64]{0,2,1:T(8,128)} fusion(f32[512,5,64]{0,2,1:T(8,128)} %get-tuple-element.751, bf16[512,5,64]{0,2,1:T(8,128)(2,1)S(1)} %get-tuple-element.758, f32[5,512,512]{2,1,0:T(8,128)} %fusion.54, f32[5,512]{1,0:T(8,128)S(1)} %get-tuple-element.757, pred[512,512]{1,0:T(8,128)(4,1)S(1)} %compare_and_fusion.1), kind=kOutput, calls=%fused_computation.23 | convolution fusion | flops 173178880 | bytes 7153664 | tf_op jit(solution)/shard_map/while/body/eval_jaxpr/cond/branch_1_fun/hqk,khd->qhd/dot_general | solution.py:103
  161.8 8.1 %collective-permute-start.2 = (bf16[512,5,64]{0,2,1:T(8,128)(2,1)}, bf16[512,5,64]{0,2,1:T(8,128)(2,1)S(1)}, u32[]{:S(2)}, u32[]{:S(2)}) collective-permute-start(bf16[512,5,64]{0,2,1:T(8,128)(2,1)} %get-tuple-element.1364), channel_id=1, source_target_pairs={{0,4},{4,8},{8,12},{12,16},{16,20},{20,24},{24,28},{28,32},{32,36}... | collective-permute-start | bytes 983048 | tf_op jit(solution)/shard_map/while/body/eval_jaxpr/ppermute | solution.py:22
  169.9 4.3 %collective-permute-start.3 = (bf16[512,5,64]{0,2,1:T(8,128)(2,1)}, bf16[512,5,64]{0,2,1:T(8,128)(2,1)S(1)}, u32[]{:S(2)}, u32[]{:S(2)}) collective-permute-start(bf16[512,5,64]{0,2,1:T(8,128)(2,1)} %get-tuple-element.1365), channel_id=1, source_target_pairs={{0,4},{4,8},{8,12},{12,16},{16,20},{20,24},{24,28},{28,32},{32,36}... | collective-permute-start | bytes 983048 | tf_op jit(solution)/shard_map/while/body/eval_jaxpr/ppermute | solution.py:22
  178.5 14.3 %conditional.8 = ((f32[512,5,64]{0,2,1:T(8,128)}, f32[512,5,64]{0,2,1:T(8,128)})) conditional(s32[]{:T(128)} %convert_element_type.130, (f32[512,5,64]{0,2,1:T(8,128)}, f32[512,5,64]{0,2,1:T(8,128)}) %tuple.132, (s32[]{:T(128)}, s32[512]{0:T(512)S(1)}, s32[512]{0:T(512)S(1)}, bf16[512,5,64]{0,2,1:T(8,128)(2,1)S(1)}, ...), branch_computations={%region_18.18_spmd, %region_19.19_spmd} | conditional | flops 685310464 | bytes 21141532 | solution.py:231
  181.9 6.1 %fusion.20 = f32[512,5,64]{0,2,1:T(8,128)} fusion(f32[512,5,64]{0,2,1:T(8,128)} %get-tuple-element.759, bf16[512,5,64]{0,2,1:T(8,128)(2,1)S(1)} %get-tuple-element.756, f32[5,512,512]{2,1,0:T(8,128)} %fusion.54, f32[5,512]{1,0:T(8,128)S(1)} %get-tuple-element.761, f32[5,512]{1,0:T(8,128)S(1)} %get-tuple-element.757, ...), kind=kOutput, calls=%fused_computation.24 | convolution fusion | flops 343572480 | bytes 7819264 | tf_op jit(solution)/shard_map/while/body/eval_jaxpr/cond/branch_1_fun/hqk,khd->qhd/dot_general | solution.py:104
  188.0 4.8 %fusion.17 = f32[512,5,64]{0,2,1:T(8,128)} fusion(f32[512,5,64]{0,2,1:T(8,128)} %get-tuple-element.751, bf16[512,5,64]{0,2,1:T(8,128)(2,1)S(1)} %get-tuple-element.758, f32[5,512,512]{2,1,0:T(8,128)} %fusion.54, f32[5,512]{1,0:T(8,128)S(1)} %get-tuple-element.757, pred[512,512]{1,0:T(8,128)(4,1)S(1)} %compare_and_fusion.1), kind=kOutput, calls=%fused_computation.23 | convolution fusion | flops 173178880 | bytes 7153664 | tf_op jit(solution)/shard_map/while/body/eval_jaxpr/cond/branch_1_fun/hqk,khd->qhd/dot_general | solution.py:103
  194.3 4.2 collective-permute-start.2
  198.4 4.3 %collective-permute-start.3 = (bf16[512,5,64]{0,2,1:T(8,128)(2,1)}, bf16[512,5,64]{0,2,1:T(8,128)(2,1)S(1)}, u32[]{:S(2)}, u32[]{:S(2)}) collective-permute-start(bf16[512,5,64]{0,2,1:T(8,128)(2,1)} %get-tuple-element.1365), channel_id=1, source_target_pairs={{0,4},{4,8},{8,12},{12,16},{16,20},{20,24},{24,28},{28,32},{32,36}... | collective-permute-start | bytes 983048 | tf_op jit(solution)/shard_map/while/body/eval_jaxpr/ppermute | solution.py:22
  212.0 18.6 %collective-permute-start.3 = (bf16[512,5,64]{0,2,1:T(8,128)(2,1)}, bf16[512,5,64]{0,2,1:T(8,128)(2,1)S(1)}, u32[]{:S(2)}, u32[]{:S(2)}) collective-permute-start(bf16[512,5,64]{0,2,1:T(8,128)(2,1)} %get-tuple-element.1365), channel_id=1, source_target_pairs={{0,4},{4,8},{8,12},{12,16},{16,20},{20,24},{24,28},{28,32},{32,36}... | collective-permute-start | bytes 983048 | tf_op jit(solution)/shard_map/while/body/eval_jaxpr/ppermute | solution.py:22
  233.5 6.4 %collective-permute-start.2 = (bf16[512,5,64]{0,2,1:T(8,128)(2,1)}, bf16[512,5,64]{0,2,1:T(8,128)(2,1)S(1)}, u32[]{:S(2)}, u32[]{:S(2)}) collective-permute-start(bf16[512,5,64]{0,2,1:T(8,128)(2,1)} %get-tuple-element.1364), channel_id=1, source_target_pairs={{0,4},{4,8},{8,12},{12,16},{16,20},{20,24},{24,28},{28,32},{32,36}... | collective-permute-start | bytes 983048 | tf_op jit(solution)/shard_map/while/body/eval_jaxpr/ppermute | solution.py:22
  239.9 4.3 %collective-permute-start.3 = (bf16[512,5,64]{0,2,1:T(8,128)(2,1)}, bf16[512,5,64]{0,2,1:T(8,128)(2,1)S(1)}, u32[]{:S(2)}, u32[]{:S(2)}) collective-permute-start(bf16[512,5,64]{0,2,1:T(8,128)(2,1)} %get-tuple-element.1365), channel_id=1, source_target_pairs={{0,4},{4,8},{8,12},{12,16},{16,20},{20,24},{24,28},{28,32},{32,36}... | collective-permute-start | bytes 983048 | tf_op jit(solution)/shard_map/while/body/eval_jaxpr/ppermute | solution.py:22
  254.6 150.8 %while.67 = (s32[]{:T(128)}, bf16[512,5,64]{0,2,1:T(8,128)(2,1)S(1)}, bf16[512,5,64]{0,2,1:T(8,128)(2,1)}, f32[5,512]{1,0:T(8,128)S(1)}, f32[5,512]{1,0:T(8,128)...) while((s32[]{:T(128)}, ...), condition=%wide.region_29.30_spmd.clone, body=%wide.region_21.29_spmd.clone.sunk | while | flops 685672704 | bytes 25225964 | solution.py:273
  266.5 13.1 %conditional.9 = ((f32[512,5,64]{0,2,1:T(8,128)S(1)}, f32[512,5,64]{0,2,1:T(8,128)})) conditional(s32[]{:T(128)} %convert_element_type.132, (f32[512,5,64]{0,2,1:T(8,128)S(1)}, f32[512,5,64]{0,2,1:T(8,128)}) %tuple.136, (s32[]{:T(128)}, s32[512]{0:T(512)S(1)}, s32[512]{0:T(512)S(1)}, bf16[512,5,64]{0,2,1:T(8,128)(2,1)S(1)}, ...), branch_computations={%region_27.27_spmd, %region_28.28_spmd} | conditional | flops 685310464 | bytes 21141532 | solution.py:265
  270.0 4.8 %fusion.41 = f32[512,5,64]{0,2,1:T(8,128)S(1)} fusion(f32[512,5,64]{0,2,1:T(8,128)S(1)} %get-tuple-element.777, bf16[512,5,64]{0,2,1:T(8,128)(2,1)S(1)} %get-tuple-element.781, f32[5,512,512]{2,1,0:T(8,128)} %fusion.55, f32[5,512]{1,0:T(8,128)S(1)} %get-tuple-element.786, f32[5,512]{1,0:T(8,128)S(1)} %get-tuple-element.783, ...), kind=kOutput, calls=%fused_computation.44 | convolution fusion | flops 343572480 | bytes 7819264 | tf_op jit(solution)/shard_map/while/body/eval_jaxpr/cond/branch_1_fun/hqk,qhd->khd/dot_general | solution.py:108
  274.8 4.7 %fusion.38 = f32[512,5,64]{0,2,1:T(8,128)} fusion(f32[512,5,64]{0,2,1:T(8,128)} %get-tuple-element.787, bf16[512,5,64]{0,2,1:T(8,128)(2,1)S(1)} %get-tuple-element.784, f32[5,512,512]{2,1,0:T(8,128)} %fusion.55, f32[5,512]{1,0:T(8,128)S(1)} %get-tuple-element.783, pred[512,512]{1,0:T(8,128)(4,1)S(1)} %compare_and_fusion.2), kind=kOutput, calls=%fused_computation.43 | convolution fusion | flops 173178880 | bytes 7153664 | tf_op jit(solution)/shard_map/while/body/eval_jaxpr/cond/branch_1_fun/hqk,qhd->khd/dot_general | solution.py:109
  290.1 12.7 %collective-permute-done.6 = f32[5,512]{1,0:T(8,128)S(1)} collective-permute-done((f32[5,512]{1,0:T(8,128)S(1)}, f32[5,512]{1,0:T(8,128)S(1)}, u32[]{:S(2)}, u32[]{:S(2)}) %collective-permute-start.6) | collective-permute-done | bytes 10272 | tf_op jit(solution)/shard_map/while/body/eval_jaxpr/ppermute | solution.py:22
  304.7 13.3 %conditional.9 = ((f32[512,5,64]{0,2,1:T(8,128)S(1)}, f32[512,5,64]{0,2,1:T(8,128)})) conditional(s32[]{:T(128)} %convert_element_type.132, (f32[512,5,64]{0,2,1:T(8,128)S(1)}, f32[512,5,64]{0,2,1:T(8,128)}) %tuple.136, (s32[]{:T(128)}, s32[512]{0:T(512)S(1)}, s32[512]{0:T(512)S(1)}, bf16[512,5,64]{0,2,1:T(8,128)(2,1)S(1)}, ...), branch_computations={%region_27.27_spmd, %region_28.28_spmd} | conditional | flops 685310464 | bytes 21141532 | solution.py:265
  308.2 4.9 %fusion.41 = f32[512,5,64]{0,2,1:T(8,128)S(1)} fusion(f32[512,5,64]{0,2,1:T(8,128)S(1)} %get-tuple-element.777, bf16[512,5,64]{0,2,1:T(8,128)(2,1)S(1)} %get-tuple-element.781, f32[5,512,512]{2,1,0:T(8,128)} %fusion.55, f32[5,512]{1,0:T(8,128)S(1)} %get-tuple-element.786, f32[5,512]{1,0:T(8,128)S(1)} %get-tuple-element.783, ...), kind=kOutput, calls=%fused_computation.44 | convolution fusion | flops 343572480 | bytes 7819264 | tf_op jit(solution)/shard_map/while/body/eval_jaxpr/cond/branch_1_fun/hqk,qhd->khd/dot_general | solution.py:108
  313.1 4.8 %fusion.38 = f32[512,5,64]{0,2,1:T(8,128)} fusion(f32[512,5,64]{0,2,1:T(8,128)} %get-tuple-element.787, bf16[512,5,64]{0,2,1:T(8,128)(2,1)S(1)} %get-tuple-element.784, f32[5,512,512]{2,1,0:T(8,128)} %fusion.55, f32[5,512]{1,0:T(8,128)S(1)} %get-tuple-element.783, pred[512,512]{1,0:T(8,128)(4,1)S(1)} %compare_and_fusion.2), kind=kOutput, calls=%fused_computation.43 | convolution fusion | flops 173178880 | bytes 7153664 | tf_op jit(solution)/shard_map/while/body/eval_jaxpr/cond/branch_1_fun/hqk,qhd->khd/dot_general | solution.py:109
  331.5 13.1 %conditional.9 = ((f32[512,5,64]{0,2,1:T(8,128)S(1)}, f32[512,5,64]{0,2,1:T(8,128)})) conditional(s32[]{:T(128)} %convert_element_type.132, (f32[512,5,64]{0,2,1:T(8,128)S(1)}, f32[512,5,64]{0,2,1:T(8,128)}) %tuple.136, (s32[]{:T(128)}, s32[512]{0:T(512)S(1)}, s32[512]{0:T(512)S(1)}, bf16[512,5,64]{0,2,1:T(8,128)(2,1)S(1)}, ...), branch_computations={%region_27.27_spmd, %region_28.28_spmd} | conditional | flops 685310464 | bytes 21141532 | solution.py:265
  335.0 4.8 %fusion.41 = f32[512,5,64]{0,2,1:T(8,128)S(1)} fusion(f32[512,5,64]{0,2,1:T(8,128)S(1)} %get-tuple-element.777, bf16[512,5,64]{0,2,1:T(8,128)(2,1)S(1)} %get-tuple-element.781, f32[5,512,512]{2,1,0:T(8,128)} %fusion.55, f32[5,512]{1,0:T(8,128)S(1)} %get-tuple-element.786, f32[5,512]{1,0:T(8,128)S(1)} %get-tuple-element.783, ...), kind=kOutput, calls=%fused_computation.44 | convolution fusion | flops 343572480 | bytes 7819264 | tf_op jit(solution)/shard_map/while/body/eval_jaxpr/cond/branch_1_fun/hqk,qhd->khd/dot_general | solution.py:108
  339.8 4.8 %fusion.38 = f32[512,5,64]{0,2,1:T(8,128)} fusion(f32[512,5,64]{0,2,1:T(8,128)} %get-tuple-element.787, bf16[512,5,64]{0,2,1:T(8,128)(2,1)S(1)} %get-tuple-element.784, f32[5,512,512]{2,1,0:T(8,128)} %fusion.55, f32[5,512]{1,0:T(8,128)S(1)} %get-tuple-element.783, pred[512,512]{1,0:T(8,128)(4,1)S(1)} %compare_and_fusion.2), kind=kOutput, calls=%fused_computation.43 | convolution fusion | flops 173178880 | bytes 7153664 | tf_op jit(solution)/shard_map/while/body/eval_jaxpr/cond/branch_1_fun/hqk,qhd->khd/dot_general | solution.py:109
  354.7 4.9 %collective-permute-done.6 = f32[5,512]{1,0:T(8,128)S(1)} collective-permute-done((f32[5,512]{1,0:T(8,128)S(1)}, f32[5,512]{1,0:T(8,128)S(1)}, u32[]{:S(2)}, u32[]{:S(2)}) %collective-permute-start.6) | collective-permute-done | bytes 10272 | tf_op jit(solution)/shard_map/while/body/eval_jaxpr/ppermute | solution.py:22
  361.5 13.1 %conditional.9 = ((f32[512,5,64]{0,2,1:T(8,128)S(1)}, f32[512,5,64]{0,2,1:T(8,128)})) conditional(s32[]{:T(128)} %convert_element_type.132, (f32[512,5,64]{0,2,1:T(8,128)S(1)}, f32[512,5,64]{0,2,1:T(8,128)}) %tuple.136, (s32[]{:T(128)}, s32[512]{0:T(512)S(1)}, s32[512]{0:T(512)S(1)}, bf16[512,5,64]{0,2,1:T(8,128)(2,1)S(1)}, ...), branch_computations={%region_27.27_spmd, %region_28.28_spmd} | conditional | flops 685310464 | bytes 21141532 | solution.py:265
  365.0 4.8 %fusion.41 = f32[512,5,64]{0,2,1:T(8,128)S(1)} fusion(f32[512,5,64]{0,2,1:T(8,128)S(1)} %get-tuple-element.777, bf16[512,5,64]{0,2,1:T(8,128)(2,1)S(1)} %get-tuple-element.781, f32[5,512,512]{2,1,0:T(8,128)} %fusion.55, f32[5,512]{1,0:T(8,128)S(1)} %get-tuple-element.786, f32[5,512]{1,0:T(8,128)S(1)} %get-tuple-element.783, ...), kind=kOutput, calls=%fused_computation.44 | convolution fusion | flops 343572480 | bytes 7819264 | tf_op jit(solution)/shard_map/while/body/eval_jaxpr/cond/branch_1_fun/hqk,qhd->khd/dot_general | solution.py:108
  369.8 4.7 %fusion.38 = f32[512,5,64]{0,2,1:T(8,128)} fusion(f32[512,5,64]{0,2,1:T(8,128)} %get-tuple-element.787, bf16[512,5,64]{0,2,1:T(8,128)(2,1)S(1)} %get-tuple-element.784, f32[5,512,512]{2,1,0:T(8,128)} %fusion.55, f32[5,512]{1,0:T(8,128)S(1)} %get-tuple-element.783, pred[512,512]{1,0:T(8,128)(4,1)S(1)} %compare_and_fusion.2), kind=kOutput, calls=%fused_computation.43 | convolution fusion | flops 173178880 | bytes 7153664 | tf_op jit(solution)/shard_map/while/body/eval_jaxpr/cond/branch_1_fun/hqk,qhd->khd/dot_general | solution.py:109
  384.7 5.0 %collective-permute-done.6 = f32[5,512]{1,0:T(8,128)S(1)} collective-permute-done((f32[5,512]{1,0:T(8,128)S(1)}, f32[5,512]{1,0:T(8,128)S(1)}, u32[]{:S(2)}, u32[]{:S(2)}) %collective-permute-start.6) | collective-permute-done | bytes 10272 | tf_op jit(solution)/shard_map/while/body/eval_jaxpr/ppermute | solution.py:22
  391.6 13.1 %conditional.9 = ((f32[512,5,64]{0,2,1:T(8,128)S(1)}, f32[512,5,64]{0,2,1:T(8,128)})) conditional(s32[]{:T(128)} %convert_element_type.132, (f32[512,5,64]{0,2,1:T(8,128)S(1)}, f32[512,5,64]{0,2,1:T(8,128)}) %tuple.136, (s32[]{:T(128)}, s32[512]{0:T(512)S(1)}, s32[512]{0:T(512)S(1)}, bf16[512,5,64]{0,2,1:T(8,128)(2,1)S(1)}, ...), branch_computations={%region_27.27_spmd, %region_28.28_spmd} | conditional | flops 685310464 | bytes 21141532 | solution.py:265
  395.1 4.8 %fusion.41 = f32[512,5,64]{0,2,1:T(8,128)S(1)} fusion(f32[512,5,64]{0,2,1:T(8,128)S(1)} %get-tuple-element.777, bf16[512,5,64]{0,2,1:T(8,128)(2,1)S(1)} %get-tuple-element.781, f32[5,512,512]{2,1,0:T(8,128)} %fusion.55, f32[5,512]{1,0:T(8,128)S(1)} %get-tuple-element.786, f32[5,512]{1,0:T(8,128)S(1)} %get-tuple-element.783, ...), kind=kOutput, calls=%fused_computation.44 | convolution fusion | flops 343572480 | bytes 7819264 | tf_op jit(solution)/shard_map/while/body/eval_jaxpr/cond/branch_1_fun/hqk,qhd->khd/dot_general | solution.py:108
  399.9 4.7 %fusion.38 = f32[512,5,64]{0,2,1:T(8,128)} fusion(f32[512,5,64]{0,2,1:T(8,128)} %get-tuple-element.787, bf16[512,5,64]{0,2,1:T(8,128)(2,1)S(1)} %get-tuple-element.784, f32[5,512,512]{2,1,0:T(8,128)} %fusion.55, f32[5,512]{1,0:T(8,128)S(1)} %get-tuple-element.783, pred[512,512]{1,0:T(8,128)(4,1)S(1)} %compare_and_fusion.2), kind=kOutput, calls=%fused_computation.43 | convolution fusion | flops 173178880 | bytes 7153664 | tf_op jit(solution)/shard_map/while/body/eval_jaxpr/cond/branch_1_fun/hqk,qhd->khd/dot_general | solution.py:109
  (244 shorter events, 177.3 us)
Async XLA Ops:
  7.2 29.7 %copy-start = (bf16[320,1280]{1,0:T(8,128)(2,1)S(1)}, bf16[320,1280]{1,0:T(8,128)(2,1)}, u32[]{:S(2)}) copy-start(bf16[320,1280]{1,0:T(8,128)(2,1)} %param.23) | copy-start | bytes 2457604
  7.2 29.7 %all-gather.2.cloned.1.call-start = ((), (), s32[]{:S(2)}) async-start(), calls=%async_computation.1 | async-start | bytes 1638400 | tf_op jit(solution)/shard_map/all_gather | solution.py:125
  8.3 401.6 %reduce-scatter.4.cloned.1.call-start = ((), (), s32[]{:S(2)}) async-start(), calls=%async_computation.2 | async-start | bytes 2027520
  11.0 28.5 %copy-start.2 = (bf16[512,320]{0,1:T(8,128)(2,1)S(1)}, bf16[512,320]{0,1:T(8,128)(2,1)}, u32[]{:S(2)}) copy-start(bf16[512,320]{0,1:T(8,128)(2,1)} %param.21) | copy-start | bytes 983044
  45.1 8.4 %collective-permute-start = (bf16[512,5,64]{0,2,1:T(8,128)(2,1)S(1)}, bf16[512,5,64]{0,2,1:T(8,128)(2,1)S(1)}, u32[]{:S(2)}, u32[]{:S(2)}) collective-permute-start(bf16[512,5,64]{0,2,1:T(8,128)(2,1)S(1)} %get-tuple-element.1324), channel_id=1, source_target_pairs={{0,4},{4,8},{8,12},{12,16},{16,20},{20,24},{24,28},{28,32},{32,36}... | collective-permute-start | bytes 983048 | tf_op jit(solution)/shard_map/while/body/eval_jaxpr/ppermute | solution.py:22
  47.0 10.0 %collective-permute-start.1 = (bf16[512,5,64]{0,2,1:T(8,128)(2,1)S(1)}, bf16[512,5,64]{0,2,1:T(8,128)(2,1)S(1)}, u32[]{:S(2)}, u32[]{:S(2)}) collective-permute-start(bf16[512,5,64]{0,2,1:T(8,128)(2,1)S(1)} %get-tuple-element.1325), channel_id=1, source_target_pairs={{0,4},{4,8},{8,12},{12,16},{16,20},{20,24},{24,28},{28,32},{32,36}... | collective-permute-start | bytes 983048 | tf_op jit(solution)/shard_map/while/body/eval_jaxpr/ppermute | solution.py:22
  62.6 8.4 %collective-permute-start = (bf16[512,5,64]{0,2,1:T(8,128)(2,1)S(1)}, bf16[512,5,64]{0,2,1:T(8,128)(2,1)S(1)}, u32[]{:S(2)}, u32[]{:S(2)}) collective-permute-start(bf16[512,5,64]{0,2,1:T(8,128)(2,1)S(1)} %get-tuple-element.1324), channel_id=1, source_target_pairs={{0,4},{4,8},{8,12},{12,16},{16,20},{20,24},{24,28},{28,32},{32,36}... | collective-permute-start | bytes 983048 | tf_op jit(solution)/shard_map/while/body/eval_jaxpr/ppermute | solution.py:22
  64.5 10.0 %collective-permute-start.1 = (bf16[512,5,64]{0,2,1:T(8,128)(2,1)S(1)}, bf16[512,5,64]{0,2,1:T(8,128)(2,1)S(1)}, u32[]{:S(2)}, u32[]{:S(2)}) collective-permute-start(bf16[512,5,64]{0,2,1:T(8,128)(2,1)S(1)} %get-tuple-element.1325), channel_id=1, source_target_pairs={{0,4},{4,8},{8,12},{12,16},{16,20},{20,24},{24,28},{28,32},{32,36}... | collective-permute-start | bytes 983048 | tf_op jit(solution)/shard_map/while/body/eval_jaxpr/ppermute | solution.py:22
  80.1 8.4 %collective-permute-start = (bf16[512,5,64]{0,2,1:T(8,128)(2,1)S(1)}, bf16[512,5,64]{0,2,1:T(8,128)(2,1)S(1)}, u32[]{:S(2)}, u32[]{:S(2)}) collective-permute-start(bf16[512,5,64]{0,2,1:T(8,128)(2,1)S(1)} %get-tuple-element.1324), channel_id=1, source_target_pairs={{0,4},{4,8},{8,12},{12,16},{16,20},{20,24},{24,28},{28,32},{32,36}... | collective-permute-start | bytes 983048 | tf_op jit(solution)/shard_map/while/body/eval_jaxpr/ppermute | solution.py:22
  82.0 10.0 %collective-permute-start.1 = (bf16[512,5,64]{0,2,1:T(8,128)(2,1)S(1)}, bf16[512,5,64]{0,2,1:T(8,128)(2,1)S(1)}, u32[]{:S(2)}, u32[]{:S(2)}) collective-permute-start(bf16[512,5,64]{0,2,1:T(8,128)(2,1)S(1)} %get-tuple-element.1325), channel_id=1, source_target_pairs={{0,4},{4,8},{8,12},{12,16},{16,20},{20,24},{24,28},{28,32},{32,36}... | collective-permute-start | bytes 983048 | tf_op jit(solution)/shard_map/while/body/eval_jaxpr/ppermute | solution.py:22
  92.0 12.2 %collective-permute-start = (bf16[512,5,64]{0,2,1:T(8,128)(2,1)S(1)}, bf16[512,5,64]{0,2,1:T(8,128)(2,1)S(1)}, u32[]{:S(2)}, u32[]{:S(2)}) collective-permute-start(bf16[512,5,64]{0,2,1:T(8,128)(2,1)S(1)} %get-tuple-element.1324), channel_id=1, source_target_pairs={{0,4},{4,8},{8,12},{12,16},{16,20},{20,24},{24,28},{28,32},{32,36}... | collective-permute-start | bytes 983048 | tf_op jit(solution)/shard_map/while/body/eval_jaxpr/ppermute | solution.py:22
  94.0 10.3 %collective-permute-start.1 = (bf16[512,5,64]{0,2,1:T(8,128)(2,1)S(1)}, bf16[512,5,64]{0,2,1:T(8,128)(2,1)S(1)}, u32[]{:S(2)}, u32[]{:S(2)}) collective-permute-start(bf16[512,5,64]{0,2,1:T(8,128)(2,1)S(1)} %get-tuple-element.1325), channel_id=1, source_target_pairs={{0,4},{4,8},{8,12},{12,16},{16,20},{20,24},{24,28},{28,32},{32,36}... | collective-permute-start | bytes 983048 | tf_op jit(solution)/shard_map/while/body/eval_jaxpr/ppermute | solution.py:22
  104.4 11.9 %collective-permute-start = (bf16[512,5,64]{0,2,1:T(8,128)(2,1)S(1)}, bf16[512,5,64]{0,2,1:T(8,128)(2,1)S(1)}, u32[]{:S(2)}, u32[]{:S(2)}) collective-permute-start(bf16[512,5,64]{0,2,1:T(8,128)(2,1)S(1)} %get-tuple-element.1324), channel_id=1, source_target_pairs={{0,4},{4,8},{8,12},{12,16},{16,20},{20,24},{24,28},{28,32},{32,36}... | collective-permute-start | bytes 983048 | tf_op jit(solution)/shard_map/while/body/eval_jaxpr/ppermute | solution.py:22
  110.5 8.4 %collective-permute-start.1 = (bf16[512,5,64]{0,2,1:T(8,128)(2,1)S(1)}, bf16[512,5,64]{0,2,1:T(8,128)(2,1)S(1)}, u32[]{:S(2)}, u32[]{:S(2)}) collective-permute-start(bf16[512,5,64]{0,2,1:T(8,128)(2,1)S(1)} %get-tuple-element.1325), channel_id=1, source_target_pairs={{0,4},{4,8},{8,12},{12,16},{16,20},{20,24},{24,28},{28,32},{32,36}... | collective-permute-start | bytes 983048 | tf_op jit(solution)/shard_map/while/body/eval_jaxpr/ppermute | solution.py:22
  119.0 12.8 %slice-start = ((s8[5242880]{0:T(1024)(128)(4,1)}), s8[4194304]{0:T(1024)(128)(4,1)S(1)}, s32[]{:S(2)}) async-start(s8[5242880]{0:T(1024)(128)(4,1)} %bitcast.79), calls=%async_computation.3 | async-start | bytes 8388608
  123.8 6.6 %copy-start.1 = (bf16[512,320]{0,1:T(8,128)(2,1)S(1)}, bf16[512,320]{0,1:T(8,128)(2,1)}, u32[]{:S(2)}) copy-start(bf16[512,320]{0,1:T(8,128)(2,1)} %param.20) | copy-start | bytes 983044
  123.8 8.0 %slice-start.1 = ((s8[5242880]{0:T(1024)(128)(4,1)}), s8[1048576]{0:T(1024)(128)(4,1)S(1)}, s32[]{:S(2)}) async-start(s8[5242880]{0:T(1024)(128)(4,1)} %bitcast.79), calls=%async_computation.4 | async-start | bytes 2097152
  133.9 11.0 %collective-permute-start.2 = (bf16[512,5,64]{0,2,1:T(8,128)(2,1)}, bf16[512,5,64]{0,2,1:T(8,128)(2,1)S(1)}, u32[]{:S(2)}, u32[]{:S(2)}) collective-permute-start(bf16[512,5,64]{0,2,1:T(8,128)(2,1)} %get-tuple-element.1364), channel_id=1, source_target_pairs={{0,4},{4,8},{8,12},{12,16},{16,20},{20,24},{24,28},{28,32},{32,36}... | collective-permute-start | bytes 983048 | tf_op jit(solution)/shard_map/while/body/eval_jaxpr/ppermute | solution.py:22
  137.4 8.6 %collective-permute-start.3 = (bf16[512,5,64]{0,2,1:T(8,128)(2,1)}, bf16[512,5,64]{0,2,1:T(8,128)(2,1)S(1)}, u32[]{:S(2)}, u32[]{:S(2)}) collective-permute-start(bf16[512,5,64]{0,2,1:T(8,128)(2,1)} %get-tuple-element.1365), channel_id=1, source_target_pairs={{0,4},{4,8},{8,12},{12,16},{16,20},{20,24},{24,28},{28,32},{32,36}... | collective-permute-start | bytes 983048 | tf_op jit(solution)/shard_map/while/body/eval_jaxpr/ppermute | solution.py:22
  161.8 13.6 %collective-permute-start.2 = (bf16[512,5,64]{0,2,1:T(8,128)(2,1)}, bf16[512,5,64]{0,2,1:T(8,128)(2,1)S(1)}, u32[]{:S(2)}, u32[]{:S(2)}) collective-permute-start(bf16[512,5,64]{0,2,1:T(8,128)(2,1)} %get-tuple-element.1364), channel_id=1, source_target_pairs={{0,4},{4,8},{8,12},{12,16},{16,20},{20,24},{24,28},{28,32},{32,36}... | collective-permute-start | bytes 983048 | tf_op jit(solution)/shard_map/while/body/eval_jaxpr/ppermute | solution.py:22
  169.9 8.6 %collective-permute-start.3 = (bf16[512,5,64]{0,2,1:T(8,128)(2,1)}, bf16[512,5,64]{0,2,1:T(8,128)(2,1)S(1)}, u32[]{:S(2)}, u32[]{:S(2)}) collective-permute-start(bf16[512,5,64]{0,2,1:T(8,128)(2,1)} %get-tuple-element.1365), channel_id=1, source_target_pairs={{0,4},{4,8},{8,12},{12,16},{16,20},{20,24},{24,28},{28,32},{32,36}... | collective-permute-start | bytes 983048 | tf_op jit(solution)/shard_map/while/body/eval_jaxpr/ppermute | solution.py:22
  194.3 9.7 %collective-permute-start.2 = (bf16[512,5,64]{0,2,1:T(8,128)(2,1)}, bf16[512,5,64]{0,2,1:T(8,128)(2,1)S(1)}, u32[]{:S(2)}, u32[]{:S(2)}) collective-permute-start(bf16[512,5,64]{0,2,1:T(8,128)(2,1)} %get-tuple-element.1364), channel_id=1, source_target_pairs={{0,4},{4,8},{8,12},{12,16},{16,20},{20,24},{24,28},{28,32},{32,36}... | collective-permute-start | bytes 983048 | tf_op jit(solution)/shard_map/while/body/eval_jaxpr/ppermute | solution.py:22
  198.4 8.6 %collective-permute-start.3 = (bf16[512,5,64]{0,2,1:T(8,128)(2,1)}, bf16[512,5,64]{0,2,1:T(8,128)(2,1)S(1)}, u32[]{:S(2)}, u32[]{:S(2)}) collective-permute-start(bf16[512,5,64]{0,2,1:T(8,128)(2,1)} %get-tuple-element.1365), channel_id=1, source_target_pairs={{0,4},{4,8},{8,12},{12,16},{16,20},{20,24},{24,28},{28,32},{32,36}... | collective-permute-start | bytes 983048 | tf_op jit(solution)/shard_map/while/body/eval_jaxpr/ppermute | solution.py:22
  208.5 23.4 %collective-permute-start.2 = (bf16[512,5,64]{0,2,1:T(8,128)(2,1)}, bf16[512,5,64]{0,2,1:T(8,128)(2,1)S(1)}, u32[]{:S(2)}, u32[]{:S(2)}) collective-permute-start(bf16[512,5,64]{0,2,1:T(8,128)(2,1)} %get-tuple-element.1364), channel_id=1, source_target_pairs={{0,4},{4,8},{8,12},{12,16},{16,20},{20,24},{24,28},{28,32},{32,36}... | collective-permute-start | bytes 983048 | tf_op jit(solution)/shard_map/while/body/eval_jaxpr/ppermute | solution.py:22
  212.0 20.1 %collective-permute-start.3 = (bf16[512,5,64]{0,2,1:T(8,128)(2,1)}, bf16[512,5,64]{0,2,1:T(8,128)(2,1)S(1)}, u32[]{:S(2)}, u32[]{:S(2)}) collective-permute-start(bf16[512,5,64]{0,2,1:T(8,128)(2,1)} %get-tuple-element.1365), channel_id=1, source_target_pairs={{0,4},{4,8},{8,12},{12,16},{16,20},{20,24},{24,28},{28,32},{32,36}... | collective-permute-start | bytes 983048 | tf_op jit(solution)/shard_map/while/body/eval_jaxpr/ppermute | solution.py:22
  233.5 11.9 %collective-permute-start.2 = (bf16[512,5,64]{0,2,1:T(8,128)(2,1)}, bf16[512,5,64]{0,2,1:T(8,128)(2,1)S(1)}, u32[]{:S(2)}, u32[]{:S(2)}) collective-permute-start(bf16[512,5,64]{0,2,1:T(8,128)(2,1)} %get-tuple-element.1364), channel_id=1, source_target_pairs={{0,4},{4,8},{8,12},{12,16},{16,20},{20,24},{24,28},{28,32},{32,36}... | collective-permute-start | bytes 983048 | tf_op jit(solution)/shard_map/while/body/eval_jaxpr/ppermute | solution.py:22
  239.9 8.6 %collective-permute-start.3 = (bf16[512,5,64]{0,2,1:T(8,128)(2,1)}, bf16[512,5,64]{0,2,1:T(8,128)(2,1)S(1)}, u32[]{:S(2)}, u32[]{:S(2)}) collective-permute-start(bf16[512,5,64]{0,2,1:T(8,128)(2,1)} %get-tuple-element.1365), channel_id=1, source_target_pairs={{0,4},{4,8},{8,12},{12,16},{16,20},{20,24},{24,28},{28,32},{32,36}... | collective-permute-start | bytes 983048 | tf_op jit(solution)/shard_map/while/body/eval_jaxpr/ppermute | solution.py:22
  249.9 4.7 %copy-start.4 = (s32[64]{0:T(128)S(1)}, s32[64]{0:T(128)}, u32[]{:S(2)}) copy-start(s32[64]{0:T(128)} %param.24) | copy-start | bytes 772
  254.6 11.8 %collective-permute-start.4 = (bf16[512,5,64]{0,2,1:T(8,128)(2,1)S(1)}, bf16[512,5,64]{0,2,1:T(8,128)(2,1)S(1)}, u32[]{:S(2)}, u32[]{:S(2)}) collective-permute-start(bf16[512,5,64]{0,2,1:T(8,128)(2,1)S(1)} %get-tuple-element.1409), channel_id=1, source_target_pairs={{4,0},{8,4},{12,8},{16,12},{20,16},{24,20},{28,24},{32,28},{36,32}... | collective-permute-start | bytes 983048 | tf_op jit(solution)/shard_map/while/body/eval_jaxpr/ppermute | solution.py:22
  256.6 9.9 %collective-permute-start.5 = (bf16[512,5,64]{0,2,1:T(8,128)(2,1)}, bf16[512,5,64]{0,2,1:T(8,128)(2,1)S(1)}, u32[]{:S(2)}, u32[]{:S(2)}) collective-permute-start(bf16[512,5,64]{0,2,1:T(8,128)(2,1)} %get-tuple-element.1410), channel_id=1, source_target_pairs={{4,0},{8,4},{12,8},{16,12},{20,16},{24,20},{28,24},{32,28},{36,32}... | collective-permute-start | bytes 983048 | tf_op jit(solution)/shard_map/while/body/eval_jaxpr/ppermute | solution.py:22
  258.5 6.3 %collective-permute-start.6 = (f32[5,512]{1,0:T(8,128)S(1)}, f32[5,512]{1,0:T(8,128)S(1)}, u32[]{:S(2)}, u32[]{:S(2)}) collective-permute-start(f32[5,512]{1,0:T(8,128)S(1)} %get-tuple-element.1411), channel_id=1, source_target_pairs={{4,0},{8,4},{12,8},{16,12},{20,16},{24,20},{28,24},{32,28},{36,32}... | collective-permute-start | bytes 30728 | tf_op jit(solution)/shard_map/while/body/eval_jaxpr/ppermute | solution.py:22
  260.4 6.0 %collective-permute-start.7 = (f32[5,512]{1,0:T(8,128)S(1)}, f32[5,512]{1,0:T(8,128)S(1)}, u32[]{:S(2)}, u32[]{:S(2)}) collective-permute-start(f32[5,512]{1,0:T(8,128)S(1)} %get-tuple-element.1412), channel_id=1, source_target_pairs={{4,0},{8,4},{12,8},{16,12},{20,16},{24,20},{28,24},{32,28},{36,32}... | collective-permute-start | bytes 30728 | tf_op jit(solution)/shard_map/while/body/eval_jaxpr/ppermute | solution.py:22
  280.3 24.4 %collective-permute-start.4 = (bf16[512,5,64]{0,2,1:T(8,128)(2,1)S(1)}, bf16[512,5,64]{0,2,1:T(8,128)(2,1)S(1)}, u32[]{:S(2)}, u32[]{:S(2)}) collective-permute-start(bf16[512,5,64]{0,2,1:T(8,128)(2,1)S(1)} %get-tuple-element.1409), channel_id=1, source_target_pairs={{4,0},{8,4},{12,8},{16,12},{20,16},{24,20},{28,24},{32,28},{36,32}... | collective-permute-start | bytes 983048 | tf_op jit(solution)/shard_map/while/body/eval_jaxpr/ppermute | solution.py:22
  282.6 22.1 %collective-permute-start.5 = (bf16[512,5,64]{0,2,1:T(8,128)(2,1)}, bf16[512,5,64]{0,2,1:T(8,128)(2,1)S(1)}, u32[]{:S(2)}, u32[]{:S(2)}) collective-permute-start(bf16[512,5,64]{0,2,1:T(8,128)(2,1)} %get-tuple-element.1410), channel_id=1, source_target_pairs={{4,0},{8,4},{12,8},{16,12},{20,16},{24,20},{28,24},{32,28},{36,32}... | collective-permute-start | bytes 983048 | tf_op jit(solution)/shard_map/while/body/eval_jaxpr/ppermute | solution.py:22
  284.6 18.2 %collective-permute-start.6 = (f32[5,512]{1,0:T(8,128)S(1)}, f32[5,512]{1,0:T(8,128)S(1)}, u32[]{:S(2)}, u32[]{:S(2)}) collective-permute-start(f32[5,512]{1,0:T(8,128)S(1)} %get-tuple-element.1411), channel_id=1, source_target_pairs={{4,0},{8,4},{12,8},{16,12},{20,16},{24,20},{28,24},{32,28},{36,32}... | collective-permute-start | bytes 30728 | tf_op jit(solution)/shard_map/while/body/eval_jaxpr/ppermute | solution.py:22
  286.5 18.2 %collective-permute-start.7 = (f32[5,512]{1,0:T(8,128)S(1)}, f32[5,512]{1,0:T(8,128)S(1)}, u32[]{:S(2)}, u32[]{:S(2)}) collective-permute-start(f32[5,512]{1,0:T(8,128)S(1)} %get-tuple-element.1412), channel_id=1, source_target_pairs={{4,0},{8,4},{12,8},{16,12},{20,16},{24,20},{28,24},{32,28},{36,32}... | collective-permute-start | bytes 30728 | tf_op jit(solution)/shard_map/while/body/eval_jaxpr/ppermute | solution.py:22
  318.7 12.8 %collective-permute-start.4 = (bf16[512,5,64]{0,2,1:T(8,128)(2,1)S(1)}, bf16[512,5,64]{0,2,1:T(8,128)(2,1)S(1)}, u32[]{:S(2)}, u32[]{:S(2)}) collective-permute-start(bf16[512,5,64]{0,2,1:T(8,128)(2,1)S(1)} %get-tuple-element.1409), channel_id=1, source_target_pairs={{4,0},{8,4},{12,8},{16,12},{20,16},{24,20},{28,24},{32,28},{36,32}... | collective-permute-start | bytes 983048 | tf_op jit(solution)/shard_map/while/body/eval_jaxpr/ppermute | solution.py:22
  320.6 10.8 %collective-permute-start.5 = (bf16[512,5,64]{0,2,1:T(8,128)(2,1)}, bf16[512,5,64]{0,2,1:T(8,128)(2,1)S(1)}, u32[]{:S(2)}, u32[]{:S(2)}) collective-permute-start(bf16[512,5,64]{0,2,1:T(8,128)(2,1)} %get-tuple-element.1410), channel_id=1, source_target_pairs={{4,0},{8,4},{12,8},{16,12},{20,16},{24,20},{28,24},{32,28},{36,32}... | collective-permute-start | bytes 983048 | tf_op jit(solution)/shard_map/while/body/eval_jaxpr/ppermute | solution.py:22
  322.6 7.0 %collective-permute-start.6 = (f32[5,512]{1,0:T(8,128)S(1)}, f32[5,512]{1,0:T(8,128)S(1)}, u32[]{:S(2)}, u32[]{:S(2)}) collective-permute-start(f32[5,512]{1,0:T(8,128)S(1)} %get-tuple-element.1411), channel_id=1, source_target_pairs={{4,0},{8,4},{12,8},{16,12},{20,16},{24,20},{28,24},{32,28},{36,32}... | collective-permute-start | bytes 30728 | tf_op jit(solution)/shard_map/while/body/eval_jaxpr/ppermute | solution.py:22
  324.5 7.0 %collective-permute-start.7 = (f32[5,512]{1,0:T(8,128)S(1)}, f32[5,512]{1,0:T(8,128)S(1)}, u32[]{:S(2)}, u32[]{:S(2)}) collective-permute-start(f32[5,512]{1,0:T(8,128)S(1)} %get-tuple-element.1412), channel_id=1, source_target_pairs={{4,0},{8,4},{12,8},{16,12},{20,16},{24,20},{28,24},{32,28},{36,32}... | collective-permute-start | bytes 30728 | tf_op jit(solution)/shard_map/while/body/eval_jaxpr/ppermute | solution.py:22
  345.4 16.1 %collective-permute-start.4 = (bf16[512,5,64]{0,2,1:T(8,128)(2,1)S(1)}, bf16[512,5,64]{0,2,1:T(8,128)(2,1)S(1)}, u32[]{:S(2)}, u32[]{:S(2)}) collective-permute-start(bf16[512,5,64]{0,2,1:T(8,128)(2,1)S(1)} %get-tuple-element.1409), channel_id=1, source_target_pairs={{4,0},{8,4},{12,8},{16,12},{20,16},{24,20},{28,24},{32,28},{36,32}... | collective-permute-start | bytes 983048 | tf_op jit(solution)/shard_map/while/body/eval_jaxpr/ppermute | solution.py:22
  347.3 14.2 %collective-permute-start.5 = (bf16[512,5,64]{0,2,1:T(8,128)(2,1)}, bf16[512,5,64]{0,2,1:T(8,128)(2,1)S(1)}, u32[]{:S(2)}, u32[]{:S(2)}) collective-permute-start(bf16[512,5,64]{0,2,1:T(8,128)(2,1)} %get-tuple-element.1410), channel_id=1, source_target_pairs={{4,0},{8,4},{12,8},{16,12},{20,16},{24,20},{28,24},{32,28},{36,32}... | collective-permute-start | bytes 983048 | tf_op jit(solution)/shard_map/while/body/eval_jaxpr/ppermute | solution.py:22
  349.2 10.4 %collective-permute-start.6 = (f32[5,512]{1,0:T(8,128)S(1)}, f32[5,512]{1,0:T(8,128)S(1)}, u32[]{:S(2)}, u32[]{:S(2)}) collective-permute-start(f32[5,512]{1,0:T(8,128)S(1)} %get-tuple-element.1411), channel_id=1, source_target_pairs={{4,0},{8,4},{12,8},{16,12},{20,16},{24,20},{28,24},{32,28},{36,32}... | collective-permute-start | bytes 30728 | tf_op jit(solution)/shard_map/while/body/eval_jaxpr/ppermute | solution.py:22
  351.1 10.4 %collective-permute-start.7 = (f32[5,512]{1,0:T(8,128)S(1)}, f32[5,512]{1,0:T(8,128)S(1)}, u32[]{:S(2)}, u32[]{:S(2)}) collective-permute-start(f32[5,512]{1,0:T(8,128)S(1)} %get-tuple-element.1412), channel_id=1, source_target_pairs={{4,0},{8,4},{12,8},{16,12},{20,16},{24,20},{28,24},{32,28},{36,32}... | collective-permute-start | bytes 30728 | tf_op jit(solution)/shard_map/while/body/eval_jaxpr/ppermute | solution.py:22
  375.3 16.3 %collective-permute-start.4 = (bf16[512,5,64]{0,2,1:T(8,128)(2,1)S(1)}, bf16[512,5,64]{0,2,1:T(8,128)(2,1)S(1)}, u32[]{:S(2)}, u32[]{:S(2)}) collective-permute-start(bf16[512,5,64]{0,2,1:T(8,128)(2,1)S(1)} %get-tuple-element.1409), channel_id=1, source_target_pairs={{4,0},{8,4},{12,8},{16,12},{20,16},{24,20},{28,24},{32,28},{36,32}... | collective-permute-start | bytes 983048 | tf_op jit(solution)/shard_map/while/body/eval_jaxpr/ppermute | solution.py:22
  377.2 14.4 %collective-permute-start.5 = (bf16[512,5,64]{0,2,1:T(8,128)(2,1)}, bf16[512,5,64]{0,2,1:T(8,128)(2,1)S(1)}, u32[]{:S(2)}, u32[]{:S(2)}) collective-permute-start(bf16[512,5,64]{0,2,1:T(8,128)(2,1)} %get-tuple-element.1410), channel_id=1, source_target_pairs={{4,0},{8,4},{12,8},{16,12},{20,16},{24,20},{28,24},{32,28},{36,32}... | collective-permute-start | bytes 983048 | tf_op jit(solution)/shard_map/while/body/eval_jaxpr/ppermute | solution.py:22
  379.2 10.5 %collective-permute-start.6 = (f32[5,512]{1,0:T(8,128)S(1)}, f32[5,512]{1,0:T(8,128)S(1)}, u32[]{:S(2)}, u32[]{:S(2)}) collective-permute-start(f32[5,512]{1,0:T(8,128)S(1)} %get-tuple-element.1411), channel_id=1, source_target_pairs={{4,0},{8,4},{12,8},{16,12},{20,16},{24,20},{28,24},{32,28},{36,32}... | collective-permute-start | bytes 30728 | tf_op jit(solution)/shard_map/while/body/eval_jaxpr/ppermute | solution.py:22
  381.1 10.5 %collective-permute-start.7 = (f32[5,512]{1,0:T(8,128)S(1)}, f32[5,512]{1,0:T(8,128)S(1)}, u32[]{:S(2)}, u32[]{:S(2)}) collective-permute-start(f32[5,512]{1,0:T(8,128)S(1)} %get-tuple-element.1412), channel_id=1, source_target_pairs={{4,0},{8,4},{12,8},{16,12},{20,16},{24,20},{28,24},{32,28},{36,32}... | collective-permute-start | bytes 30728 | tf_op jit(solution)/shard_map/while/body/eval_jaxpr/ppermute | solution.py:22
  (1 other events, 4.7 us)
Sparse Core Ops, SparseCore 0:
  9.7 27.1 all-gather.1
  254.7 108.8 reduce-scatter.3
where the time goes:
time: 419 us; the launch traced here: 417 us
  starting transfers between devices  140 us (33%)
  matrix products  125 us (30%)
  waiting for transfers between devices  78.8 us (19%)
  other arithmetic  29.8 us (7%)
  local copies, waits for them, and re-layouts  18.6 us (4%)
  between operations  14.1 us (3%)
  loops' own time  10.6 us (3%)
    ppermute x40, starting transfers between devices, shifted(): return lax.ppermute(shard, axis, pairs)  140 us
    ppermute x40, waiting for transfers between devices, shifted(): return lax.ppermute(shard, axis, pairs)  62.9 us
    dot_general x6, matrix products, backward_tile(): jnp.einsum('hqk,qhd->khd', probs_low, grad_part, preferred_element_type=j...  28.6 us
    dot_general x8, matrix products, backward_tile(): jnp.einsum('qhd,khd->hqk', query_part, key_heads, preferred_element_type=...  26.7 us
    dot_general x6, matrix products, backward_tile(): jnp.einsum('hqk,qhd->khd', dscore, query_part, preferred_element_type=jnp...  25.1 us
    all_gather x1, waiting for transfers between devices, shards(): full_cotangent = lax.all_gather(cotangent, 'head', axis=1, tiled=True)  15.8 us
    dot_general x3, matrix products, backward_tile(): jnp.einsum('hqk,khd->qhd', dscore, key_heads, preferred_element_type=jnp....  13.6 us
    dot_general x3, matrix products, backward_tile(): jnp.einsum('hqk,khd->qhd', probs_low, value_heads, preferred_element_type...  11.7 us
  transfers between devices with their start and end apart: 42, of which 23 were waited for; matrix products, arithmetic and copies ran while one was open for 23% of the time, Pallas kernels for 0%

commit v1 on v0

v1 whole, which is shorter than its diff:
```python
import functools

import jax
import jax.numpy as jnp
from jax import lax
from jax.experimental import pallas as pl
from jax.experimental.pallas import tpu as pltpu
from jax.sharding import PartitionSpec as P

HS = 64
UNIT = 16
MOSTU = 32
LEFT_MAX = 4
BLK = 512
HEADS = 5
WIDTH = HEADS * HS
BACK = 5
CK = 256
PARTS = (BACK + 1) * BLK // CK
HIDDEN = -2e30
LOWEST = -1e30
F32 = jnp.float32
BF16 = jnp.bfloat16


def greet(signal_list):
    barrier = pltpu.get_barrier_semaphore()
    for target in signal_list:
        pl.semaphore_signal(
            barrier, inc=1, device_id=target, device_id_type=pl.DeviceIdType.MESH
        )


def send(src, dst, send_sem, recv_sem, target):
    return pltpu.make_async_remote_copy(
        src_ref=src,
        dst_ref=dst,
        send_sem=send_sem,
        recv_sem=recv_sem,
        device_id=target,
        device_id_type=pl.DeviceIdType.MESH,
    )


def gather_kernel(tm_count, head_count, kv, cot, kv_out, cot_out, own_sem, ssem, rsem, xs, xr):
    t = lax.axis_index("tm")
    x = lax.axis_index("head")
    core = t % 2
    mate = t + 1 - 2 * core

    def later(by):
        return {"tm": (t + by) % tm_count}

    def earlier(by):
        return {"tm": (t + tm_count - by) % tm_count}

    def side(by):
        return {"head": (x + by) % head_count}

    sides = range(1, head_count)
    greet([{"tm": mate}, earlier(2), earlier(4)] + [side(head_count - i) for i in sides])
    barrier = pltpu.get_barrier_semaphore()

    @pl.when(core == 0)
    def _():
        pl.semaphore_signal(
            barrier, inc=1, device_id=earlier(5), device_id_type=pl.DeviceIdType.MESH
        )
        pl.semaphore_wait(barrier, 3 + len(sides))

    @pl.when(core == 1)
    def _():
        pl.semaphore_wait(barrier, 4 + len(sides))

    own = pltpu.make_async_copy(kv, kv_out.at[0], own_sem.at[0])
    own.start()
    own_cot = pltpu.make_async_copy(cot, cot_out.at[x], own_sem.at[1])
    own_cot.start()

    def slot(src, k, target, sent):
        return send(src, kv_out.at[k], ssem.at[sent], rsem.at[k], target)

    across = [
        send(cot, cot_out.at[x], xs.at[i - 1], xr.at[i - 1], side(i)) for i in sides
    ]
    near = slot(kv, 2, later(2), 0)
    far = slot(kv, 4, later(4), 1)
    near.start()
    for copy in across:
        copy.start()
    far.start()

    @pl.when(core == 0)
    def _():
        first = slot(kv, 1, {"tm": mate}, 2)
        first.start()
        near.wait_recv()
        second = slot(kv_out.at[2], 3, {"tm": mate}, 3)
        second.start()
        far.wait_recv()
        third = slot(kv_out.at[4], 5, {"tm": mate}, 4)
        third.start()
        slot(kv, 1, {"tm": mate}, 2).wait_recv()
        slot(kv, 3, {"tm": mate}, 3).wait_recv()
        slot(kv, 5, {"tm": mate}, 4).wait_recv()
        first.wait_send()
        second.wait_send()
        third.wait_send()

    @pl.when(core == 1)
    def _():
        last = slot(kv, 5, later(5), 4)
        last.start()
        near.wait_recv()
        first = slot(kv_out.at[2], 1, {"tm": mate}, 2)
        first.start()
        far.wait_recv()
        second = slot(kv_out.at[4], 3, {"tm": mate}, 3)
        second.start()
        slot(kv, 1, {"tm": mate}, 2).wait_recv()
        slot(kv, 3, {"tm": mate}, 3).wait_recv()
        slot(kv, 5, {"tm": mate}, 4).wait_recv()
        first.wait_send()
        second.wait_send()
        last.wait_send()

    near.wait_send()
    far.wait_send()
    for copy in across:
        copy.wait()
    own.wait()
    own_cot.wait()


def attend_kernel(
    count_ref,
    spans,
    query_info,
    q_ref,
    kv_ref,
    cot_ref,
    w_ref,
    dq_ref,
    dkv_ref,
    wt_ref,
    kvt,
    probs,
    rhs,
    gt,
    rows,
    out_t,
    dq_t,
    m_all,
    m_run,
    l_run,
    delta,
    acc,
):
    used = count_ref[0]
    own_first = count_ref[1]
    grad = jnp.zeros((BLK, WIDTH), F32)
    for x in range(cot_ref.shape[0]):
        grad += lax.dot_general(
            cot_ref[x], w_ref[x], (((1,), (1,)), ((), ())), preferred_element_type=F32
        )
    queries = (q_ref[...].astype(F32) * HS**-0.5).astype(BF16)
    pair = jnp.concatenate([queries, grad.astype(BF16)], axis=1)
    pair_t = pair.T
    seg_row = lax.broadcasted_iota(jnp.int32, (128, BLK), 0)
    bias = jnp.where(
        (seg_row >= query_info[0:1, :]) & (seg_row <= query_info[1:2, :]), 0.0, HIDDEN
    ).astype(BF16)
    blank_t = jnp.zeros((HS, BLK), BF16)
    lane = lax.broadcasted_iota(jnp.int32, (BLK, 128), 1)
    for j in range(2 * HEADS):
        g, half = divmod(j, 2)
        mine = pair_t[HS * j : HS * (j + 1), :]
        both = [mine, blank_t] if half == 0 else [blank_t, mine]
        if j < HEADS:
            rhs[j] = jnp.concatenate(both + [bias], axis=0)
        else:
            gt[j - HEADS] = jnp.concatenate(both, axis=0)
        group = pair[:, 128 * g : 128 * (g + 1)]
        keep = (lane < HS) if half == 0 else (lane >= HS)
        rows[j] = jnp.where(keep, group, jnp.zeros_like(group))
    m_run[...] = jnp.full(m_run.shape, LOWEST, F32)
    l_run[...] = jnp.zeros(l_run.shape, F32)
    out_t[...] = jnp.zeros(out_t.shape, F32)
    dq_t[...] = jnp.zeros(dq_t.shape, F32)

    def place(i):
        return 2 * (i // 2) + 1 - i % 2

    def forward(i, carry):
        c = place(i)
        frames = own_first + BLK - (i + 1) * CK + lax.broadcasted_iota(jnp.int32, (CK, 128), 0)
        hot = ((frames >= spans[0:1, :]) & (frames < spans[1:2, :])).astype(F32).astype(BF16)
        kvt[c] = kv_ref[c].T
        for h in range(HEADS):
            g = h // 2
            left = jnp.concatenate([kv_ref[c, :, 128 * g : 128 * (g + 1)], hot], axis=1)
            s = jnp.dot(left, rhs[h], preferred_element_type=F32)
            m_old = m_run[h : h + 1, :]
            m_new = jnp.maximum(m_old, jnp.max(s, axis=0, keepdims=True))
            p = jnp.exp(s - m_new)
            factor = jnp.exp(m_old - m_new)
            l_run[h : h + 1, :] = l_run[h : h + 1, :] * factor + jnp.sum(p, axis=0, keepdims=True)
            m_run[h : h + 1, :] = m_new
            m_all[c, h : h + 1, :] = m_new
            low = p.astype(BF16)
            probs[c, h] = low
            here = slice(HS * h, HS * (h + 1))
            out_t[here, :] = out_t[here, :] * factor + jnp.dot(
                kvt[c, WIDTH + HS * h : WIDTH + HS * (h + 1), :], low, preferred_element_type=F32
            )
        return carry

    lax.fori_loop(0, used, forward, 0)

    for h in range(HEADS):
        here = slice(HS * h, HS * (h + 1))
        out = out_t[here, :] / l_run[h : h + 1, :]
        out_t[here, :] = out
        own_grad = gt[h, HS * ((h + 1) % 2) : HS * ((h + 1) % 2) + HS, :].astype(F32)
        delta[h : h + 1, :] = jnp.sum(out * own_grad, axis=0, keepdims=True)
        l_run[h : h + 1, :] = m_run[h : h + 1, :] + jnp.log(l_run[h : h + 1, :])

    attn_t = out_t[...].astype(BF16)
    for x in range(cot_ref.shape[0]):
        term = jnp.dot(attn_t, cot_ref[x], preferred_element_type=F32)
        wt_ref[x] = term.T.astype(BF16)

    def backward(i, carry):
        c = place(i)
        for h in range(HEADS):
            g = (h + HEADS) // 2
            grad_p = jnp.dot(
                kv_ref[c, :, 128 * g : 128 * (g + 1)], gt[h], preferred_element_type=F32
            )
            scale = jnp.exp(m_all[c, h : h + 1, :] - l_run[h : h + 1, :])
            p = probs[c, h].astype(F32) * scale
            ds = (p * (grad_p - delta[h : h + 1, :])).astype(BF16)
            here = slice(HS * h, HS * (h + 1))
            dq_t[here, :] += jnp.dot(kvt[c, here, :], ds, preferred_element_type=F32)
            for j, lhs in ((h, ds), (h + HEADS, p.astype(BF16))):
                cols = slice(128 * (j // 2), 128 * (j // 2 + 1))
                part = jnp.dot(lhs, rows[j], preferred_element_type=F32)
                if j in (0, 5, 6, 2, 8):
                    acc[:, cols] = part
                else:
                    acc[:, cols] += part
        dkv_ref[c] = acc[...].astype(BF16)
        return carry

    lax.fori_loop(0, used, backward, 0)

    def clear(i, carry):
        dkv_ref[place(i)] = jnp.zeros(dkv_ref.shape[1:], BF16)
        return carry

    lax.fori_loop(used, PARTS, clear, 0)
    dq_ref[...] = (dq_t[...] * HS**-0.5).T.astype(BF16)


def return_kernel(
    tm_count,
    dkv,
    wt,
    dk_ref,
    dv_ref,
    dw_ref,
    from_mate,
    sums,
    homes,
    edge,
    z_in,
    z_sum,
    y_in,
    ms,
    mr,
    hs,
    hr,
    es,
    er,
    zs,
    zr,
    ys,
    yr,
):
    t = lax.axis_index("tm")
    core = t % 2
    mate = {"tm": t + 1 - 2 * core}
    z = t // 8
    low = t % 8

    def later(by):
        return {"tm": (t + by) % tm_count}

    def earlier(by):
        return {"tm": (t + tm_count - by) % tm_count}

    def z_peer(i):
        return {"tm": (t + 8 * i) % tm_count}

    def y_peer(i):
        return {"tm": 8 * z + (low + i) % 8}

    barrier = pltpu.get_barrier_semaphore()
    greetings = [mate, later(2), later(4)]
    greetings += [z_peer(4 - i) for i in range(1, 4)] + [y_peer(8 - i) for i in range(1, 8)]
    greet(greetings)

    @pl.when(core == 1)
    def _():
        pl.semaphore_signal(
            barrier, inc=1, device_id=later(5), device_id_type=pl.DeviceIdType.MESH
        )
        pl.semaphore_wait(barrier, len(greetings))

    @pl.when(core == 0)
    def _():
        pl.semaphore_wait(barrier, len(greetings) + 1)

    z_copies = [
        send(wt.at[(z + i) % 4], z_in.at[i - 1], zs.at[i - 1], zr.at[i - 1], z_peer(i))
        for i in range(1, 4)
    ]

    to_far = send(dkv.at[3 + 2 * core], from_mate.at[0], ms.at[0], mr.at[0], mate)
    to_near = send(dkv.at[1 + 2 * core], from_mate.at[1], ms.at[1], mr.at[1], mate)
    to_far.start()
    to_near.start()
    on_edge = send(dkv.at[5], edge, es.at[0], er.at[0], earlier(5))
    in_chip = send(dkv.at[1], edge, es.at[0], er.at[0], mate)

    @pl.when(core == 0)
    def _():
        on_edge.start()

    @pl.when(core == 1)
    def _():
        in_chip.start()

    for copy in z_copies:
        copy.start()
    home_copies = []
    for step, copy, kept in ((0, to_far, 4), (1, to_near, 2)):
        copy.wait_recv()
        sums[step] = (dkv[kept].astype(F32) + from_mate[step].astype(F32)).astype(BF16)
        home = send(sums.at[step], homes.at[step], hs.at[step], hr.at[step], earlier(kept))
        home.start()
        home_copies.append(home)

    for copy in z_copies:
        copy.wait_recv()
    z_sum[...] = wt[z].astype(F32)
    for i in range(3):
        z_sum[...] += z_in[i].astype(F32)
    y_copies = [
        send(
            z_sum.at[pl.ds(pl.multiple_of(40 * ((low + i) % 8), 8), 40)],
            y_in.at[i - 1],
            ys.at[i - 1],
            yr.at[i - 1],
            y_peer(i),
        )
        for i in range(1, 8)
    ]
    for copy in y_copies:
        copy.start()
    total = z_sum[pl.ds(pl.multiple_of(40 * low, 8), 40), :]
    for i, copy in enumerate(y_copies):
        copy.wait_recv()
        total = total + y_in[i]
    dw_ref[...] = total

    total = dkv[0].astype(F32)
    for step, copy in enumerate(home_copies):
        copy.wait_recv()
        total = total + homes[step].astype(F32)
    in_chip.wait_recv()
    total = total + edge[...].astype(F32)
    dk_ref[...] = total[:, :WIDTH].astype(BF16)
    dv_ref[...] = total[:, WIDTH:].astype(BF16)

    for copy in z_copies + y_copies + home_copies + [to_far, to_near, in_chip]:
        copy.wait_send()


def shards(queries, key_rows, value_rows, cotangent, out_weight, segment_units, left_segments):
    tm_count = lax.axis_size("tm")
    head_count = lax.axis_size("head")
    t = lax.axis_index("tm")
    any_space = pl.BlockSpec(memory_space=pl.ANY)
    vmem = pl.BlockSpec(memory_space=pltpu.VMEM)
    smem = pl.BlockSpec(memory_space=pltpu.SMEM)

    ends = jnp.cumsum(segment_units) * UNIT
    starts = ends - segment_units * UNIT
    segments = segment_units.shape[0]
    number = jnp.arange(segments, dtype=jnp.int32)
    own_first = t * BLK
    frames = own_first + jnp.arange(BLK, dtype=jnp.int32)
    own_seg = jnp.sum((ends[:, None] <= frames[None, :]).astype(jnp.int32), axis=0)
    reach = jnp.sum(
        jnp.where(number[:, None] == own_seg[None, :], left_segments[:, None], 0), axis=0
    )
    lowest = jnp.maximum(own_seg - reach, 0)
    first_key = jnp.min(
        jnp.where(number[:, None] == lowest[None, :], starts[:, None], tm_count * BLK)
    )
    used = (own_first + BLK - first_key + CK - 1) // CK
    counts = jnp.stack([jnp.minimum(used, PARTS), own_first]).astype(jnp.int32)
    pad = 128 - segments
    spans = jnp.zeros((8, 128), jnp.int32).at[0, :segments].set(starts).at[1, :segments].set(ends)
    query_info = jnp.stack([lowest, own_seg] + [own_seg] * 6).astype(jnp.int32)

    kv = jnp.concatenate([key_rows, value_rows], axis=1)
    dma = pltpu.SemaphoreType.DMA
    kv_all, cot_all = pl.pallas_call(
        functools.partial(gather_kernel, tm_count, head_count),
        out_shape=(
            jax.ShapeDtypeStruct((BACK + 1, BLK, 2 * WIDTH), BF16),
            jax.ShapeDtypeStruct((head_count, BLK, WIDTH), BF16),
        ),
        in_specs=[any_space] * 2,
        out_specs=(any_space, any_space),
        scratch_shapes=[dma((2,)), dma((5,)), dma((6,)), dma((3,)), dma((3,))],
        compiler_params=pltpu.CompilerParams(collective_id=0, has_side_effects=True),
    )(kv, cotangent)

    w_parts = out_weight.reshape(WIDTH, head_count, WIDTH).transpose(1, 0, 2)
    query_grad, dkv, w_term = pl.pallas_call(
        attend_kernel,
        out_shape=(
            jax.ShapeDtypeStruct((BLK, WIDTH), BF16),
            jax.ShapeDtypeStruct((PARTS, CK, 2 * WIDTH), BF16),
            jax.ShapeDtypeStruct((head_count, WIDTH, WIDTH), BF16),
        ),
        in_specs=[smem] + [vmem] * 6,
        out_specs=(vmem, vmem, vmem),
        scratch_shapes=[
            pltpu.VMEM((PARTS, 2 * WIDTH, CK), BF16),
            pltpu.VMEM((PARTS, HEADS, CK, BLK), BF16),
            pltpu.VMEM((HEADS, 256, BLK), BF16),
            pltpu.VMEM((HEADS, 128, BLK), BF16),
            pltpu.VMEM((2 * HEADS, BLK, 128), BF16),
            pltpu.VMEM((WIDTH, BLK), F32),
            pltpu.VMEM((WIDTH, BLK), F32),
            pltpu.VMEM((PARTS, 8, BLK), F32),
            pltpu.VMEM((8, BLK), F32),
            pltpu.VMEM((8, BLK), F32),
            pltpu.VMEM((8, BLK), F32),
            pltpu.VMEM((CK, 2 * WIDTH), F32),
        ],
        compiler_params=pltpu.CompilerParams(vmem_limit_bytes=52 << 20),
    )(
        counts,
        spans,
        query_info,
        queries,
        kv_all.reshape(PARTS, CK, 2 * WIDTH),
        cot_all,
        w_parts,
    )

    key_grad, value_grad, dw_t = pl.pallas_call(
        functools.partial(return_kernel, tm_count),
        out_shape=(
            jax.ShapeDtypeStruct((BLK, WIDTH), BF16),
            jax.ShapeDtypeStruct((BLK, WIDTH), BF16),
            jax.ShapeDtypeStruct((40, WIDTH), F32),
        ),
        in_specs=[vmem] * 2,
        out_specs=(vmem, vmem, vmem),
        scratch_shapes=[
            pltpu.VMEM((2, BLK, 2 * WIDTH), BF16),
            pltpu.VMEM((2, BLK, 2 * WIDTH), BF16),
            pltpu.VMEM((2, BLK, 2 * WIDTH), BF16),
            pltpu.VMEM((BLK, 2 * WIDTH), BF16),
            pltpu.VMEM((3, WIDTH, WIDTH), BF16),
            pltpu.VMEM((WIDTH, WIDTH), F32),
            pltpu.VMEM((7, 40, WIDTH), F32),
        ]
        + [dma((2,))] * 4
        + [dma((1,))] * 2
        + [dma((3,))] * 2
        + [dma((7,))] * 2,
        compiler_params=pltpu.CompilerParams(
            collective_id=1, has_side_effects=True, vmem_limit_bytes=40 << 20
        ),
    )(dkv.reshape(BACK + 1, BLK, 2 * WIDTH), w_term)
    return (query_grad, key_grad, value_grad, dw_t.T)


def solution(mesh):
    placed = (
        P("tm", "head"),
        P("tm", "head"),
        P("tm", "head"),
        P("tm", "head"),
        P("head", None),
        P(),
        P(),
    )
    return jax.shard_map(
        shards,
        mesh=mesh,
        in_specs=placed,
        out_specs=(P("tm", "head"), P("tm", "head"), P("tm", "head"), P("head", "tm")),
        check_vma=False,
    )
```

time: 419 us -> 160 us (0.38)
  the two profiles are of different devices: /device:TPU:8 before, /device:TPU:1 now
where the time goes in v1:
time: 160 us
  Pallas kernels  143 us (89%)
  local copies, waits for them, and re-layouts  12.1 us (8%)
  other arithmetic  3.6 us (2%)
    pallas_call x1, Pallas kernels, shards(): pl.pallas_call(functools.partial(return_kernel, tm_count), out_shape=(jax...  69.8 us
    pallas_call x1, Pallas kernels, shards(): pl.pallas_call(functools.partial(gather_kernel, tm_count, head_count), ou...  49.9 us
    pallas_call x1, Pallas kernels, shards(): pl.pallas_call(attend_kernel, out_shape=(jax.ShapeDtypeStruct((BLK, WIDTH...  23 us
    unnamed x16, local copies, waits for them, and re-layouts  9 us

profile of v1, /device:TPU:1, one launch (start us, length us, event | category | flops | bytes accessed | tf_op | source)
XLA Modules:
  0.0 159.8 jit_solution(9229527517022943083)
XLA Ops:
  0.6 0.0 copy-start.2
  0.7 0.8 copy.28
  1.4 0.1 reduce-window.4
  1.5 0.1 multiply_reduce_fusion
  1.6 0.1 convert_reduce_fusion
  1.8 0.7 multiply_subtract_fusion
  2.4 0.7 select_reduce_fusion.1
  3.2 0.7 select_reduce_fusion
  4.6 0.1 pad_add_fusion.count_ref
  4.7 0.1 scatter.9.spans
  4.9 1.2 copy.33.q_ref
  6.1 0.0 copy-start.3
  6.1 1.2 copy.29
  7.3 0.0 copy-done.2
  7.3 0.0 copy-start.1
  7.3 0.2 copy.30
  7.5 1.1 pad_maximum_fusion.kv
  8.6 0.0 copy-done.3
  8.6 0.9 copy.31.cot
  9.5 0.0 copy-done.1
  9.5 1.1 reshape.116
  10.6 1.1 copy.38
  11.7 49.9 %shard_map.102 = (bf16[6,512,640]{2,1,0:T(8,128)(2,1)}, bf16[4,512,320]{2,1,0:T(8,128)(2,1)}) custom-call(bf16[512,640]{1,0:T(8,128)(2,1)} %pad_maximum_fusion.kv, bf16[512,320]{1,0:T(8,128)(2,1)} %copy.31.cot), custom_call_target="tpu_custom_call" | custom-call | tf_op jit(solution)/shard_map/pallas_call | solution.py:420
  61.6 23.0 %shard_map.103 = (bf16[512,320]{1,0:T(8,128)(2,1)S(1)}, bf16[12,256,640]{2,1,0:T(8,128)(2,1)}, bf16[4,320,320]{2,1,0:T(8,128)(2,1)S(1)}) custom-call(s32[2]{0:T(128)S(1)} %pad_add_fusion.count_ref, s32[8,128]{1,0:T(8,128)S(1)} %scatter.9.spans, s32[8,512]{1,0:T(8,128)S(1)} %stack.11.query_info, bf16[512,320]{1,0:T(8,128)(2,1)S(1)} %copy.33.q_ref, ...), custom_call_target="tpu_custom_call" | custom-call | tf_op jit(solution)/shard_map/pallas_call | solution.py:433
  84.6 0.9 copy.34
  85.5 0.0 copy-start
  85.5 2.1 %copy-done = bf16[12,256,640]{2,1,0:T(8,128)(2,1)S(1)} copy-done((bf16[12,256,640]{2,1,0:T(8,128)(2,1)S(1)}, bf16[12,256,640]{2,1,0:T(8,128)(2,1)}, u32[]{:S(2)}) %copy-start) | copy-done | bytes 3932184
  87.6 69.8 %shard_map.104 = (bf16[512,320]{1,0:T(8,128)(2,1)S(1)}, bf16[512,320]{1,0:T(8,128)(2,1)S(1)}, f32[40,320]{1,0:T(8,128)S(1)}) custom-call(bf16[6,512,640]{2,1,0:T(8,128)(2,1)S(1)} %bitcast.13, bf16[4,320,320]{2,1,0:T(8,128)(2,1)S(1)} %get-tuple-element.40.wt), custom_call_target="tpu_custom_call" | custom-call | tf_op jit(solution)/shard_map/pallas_call | solution.py:467
  157.4 0.9 copy.35
  158.3 0.9 copy.36
  159.2 0.6 copy.41
  (5 shorter events, 0.1 us)
Async XLA Ops:
  0.6 6.7 %copy-start.2 = (bf16[512,320]{0,1:T(8,128)(2,1)S(1)}, bf16[512,320]{0,1:T(8,128)(2,1)}, u32[]{:S(2)}) copy-start(bf16[512,320]{0,1:T(8,128)(2,1)} %param.13) | copy-start | bytes 983044
  6.1 2.5 %copy-start.3 = (bf16[512,320]{0,1:T(8,128)(2,1)S(1)}, bf16[512,320]{0,1:T(8,128)(2,1)}, u32[]{:S(2)}) copy-start(bf16[512,320]{0,1:T(8,128)(2,1)} %param.14) | copy-start | bytes 983044
  7.3 2.2 %copy-start.1 = (bf16[320,1280]{1,0:T(8,128)(2,1)S(1)}, bf16[320,1280]{1,0:T(8,128)(2,1)}, u32[]{:S(2)}) copy-start(bf16[320,1280]{1,0:T(8,128)(2,1)} %param.15) | copy-start | bytes 2457604
  85.5 2.1 %copy-start = (bf16[12,256,640]{2,1,0:T(8,128)(2,1)S(1)}, bf16[12,256,640]{2,1,0:T(8,128)(2,1)}, u32[]{:S(2)}) copy-start(bf16[12,256,640]{2,1,0:T(8,128)(2,1)} %get-tuple-element.39) | copy-start | bytes 11796484

commit v2 on v0

v2 whole, which is shorter than its diff:
```python
import functools

import jax
import jax.numpy as jnp
from jax import lax
from jax.experimental import pallas as pl
from jax.experimental.pallas import tpu as pltpu
from jax.sharding import PartitionSpec as P

HS = 64
UNIT = 16
BLK = 512
HEADS = 5
WIDTH = HEADS * HS
BACK = 5
HALF = BLK // 2
STRIP = 128
HIDDEN = -2e30
LOWEST = -1e30
F32 = jnp.float32
BF16 = jnp.bfloat16
MESH = pl.DeviceIdType.MESH


def kernel(
    tm_count,
    head_count,
    units_ref,
    left_ref,
    q_hbm,
    k_hbm,
    v_hbm,
    cot_hbm,
    w_hbm,
    dq_ref,
    dk_ref,
    dv_ref,
    dw_ref,
    slots,
    relay,
    kv_all,
    probs,
    cot_all,
    w_ref,
    q_ref,
    rhs,
    gt,
    rows,
    square,
    work,
    out_t,
    dq_t,
    m_all,
    m_run,
    l_run,
    delta,
    dkv,
    from_mate,
    sums,
    home_near,
    home_far,
    chain_in,
    relay_back,
    edge,
    wt,
    z_in,
    z_sum,
    y_in,
    local,
    sent,
    got_k,
    got_v,
    got_relay,
    side_sent,
    side_got,
    back_sent,
    back_got,
    z_sent,
    z_got,
    y_sent,
    y_got,
):
    t = lax.axis_index("tm")
    x = lax.axis_index("head")
    core = t % 2
    z = t // 8
    y = (t // 2) % 4
    low = t % 8
    sides = range(1, head_count)

    def at(place):
        return {"tm": (place + tm_count) % tm_count}

    def chip(z_place, y_place):
        return (z_place * 4 + y_place % 4) * 2 + core

    mate = at(t + 1 - 2 * core)
    before, after = chip(z, y + 3), chip(z, y + 1)
    src_four = (t + tm_count - 4) % tm_count
    src_relay = chip(src_four // 8, (src_four // 2) % 4 + 3)
    own_four = (t + 4) % tm_count
    own_relay = chip(own_four // 8, (own_four // 2) % 4 + 1)

    greeted = [mate, at(t - 2), at(after), at(src_relay)]
    greeted += [at(t + 2), at(before), at(own_relay)]
    greeted += [{"head": (x + head_count - i) % head_count} for i in sides]
    greeted += [at(t - 8 * i) for i in range(1, 4)]
    greeted += [at(8 * z + (low + 8 - i) % 8) for i in range(1, 8)]
    barrier = pltpu.get_barrier_semaphore()
    for target in greeted:
        pl.semaphore_signal(barrier, inc=1, device_id=target, device_id_type=MESH)
    edge_source = at(t + 5 * (2 * core - 1))
    pl.semaphore_signal(barrier, inc=1, device_id=edge_source, device_id_type=MESH)

    loads = [
        pltpu.make_async_copy(k_hbm, slots.at[0, 0:WIDTH], local.at[0]),
        pltpu.make_async_copy(v_hbm, slots.at[0, WIDTH : 2 * WIDTH], local.at[1]),
        pltpu.make_async_copy(q_hbm, q_ref, local.at[2]),
        pltpu.make_async_copy(
            cot_hbm, cot_all.at[pl.ds(pl.multiple_of(WIDTH * x, 64), WIDTH)], local.at[3]
        ),
        pltpu.make_async_copy(w_hbm, w_ref, local.at[4]),
    ]
    for load in loads:
        load.start()
    pl.semaphore_wait(barrier, len(greeted) + 1)

    def push(src, dst, send_sem, recv_sem, target):
        return pltpu.make_async_remote_copy(
            src_ref=src,
            dst_ref=dst,
            send_sem=send_sem,
            recv_sem=recv_sem,
            device_id=target,
            device_id_type=MESH,
        )

    def keys(src, slot, number, target):
        return push(src, slots.at[slot, 0:WIDTH], sent.at[number], got_k.at[slot], target)

    def values(src, slot, number, target):
        return push(
            src, slots.at[slot, WIDTH : 2 * WIDTH], sent.at[number], got_v.at[slot], target
        )

    def key_part(slot):
        return slots.at[slot, 0:WIDTH]

    def value_part(slot):
        return slots.at[slot, WIDTH : 2 * WIDTH]

    near_k = keys(k_hbm, 2, 0, at(t + 2))
    near_v = values(v_hbm, 2, 1, at(t + 2))
    relay_first = push(v_hbm, relay, sent.at[2], got_relay.at[0], at(before))
    near_k.start()
    relay_first.start()
    across = [
        push(
            cot_hbm,
            cot_all.at[pl.ds(pl.multiple_of(WIDTH * x, 64), WIDTH)],
            side_sent.at[i - 1],
            side_got.at[i - 1],
            {"head": (x + i) % head_count},
        )
        for i in sides
    ]
    for copy in across:
        copy.start()
    near_v.start()
    direct_slot = 1 + 4 * core
    direct_to = at(t + 1 + 4 * core)
    direct_k = keys(k_hbm, direct_slot, 3, direct_to)
    direct_v = values(v_hbm, direct_slot, 4, direct_to)
    direct_k.start()
    direct_v.start()
    chain_k = keys(key_part(2), 4, 5, at(t + 2))
    relay_second = values(relay, 4, 6, at(after + 4))
    pass_near = 3 - 2 * core
    pass_far = 5 - 2 * core
    pass_near_k = keys(key_part(2), pass_near, 7, mate)
    pass_near_v = values(value_part(2), pass_near, 8, mate)
    pass_far_k = keys(key_part(4), pass_far, 9, mate)
    pass_far_v = values(value_part(4), pass_far, 10, mate)

    segments = units_ref.shape[1]
    units = jnp.broadcast_to(units_ref[...].astype(F32), (8, segments)).astype(BF16)
    lefts = jnp.broadcast_to(left_ref[...].astype(F32), (8, segments)).astype(BF16)
    down = lax.broadcasted_iota(jnp.int32, (segments, 128), 0)
    over = lax.broadcasted_iota(jnp.int32, (segments, 128), 1)
    until = jnp.where(down <= over, 1.0, 0.0).astype(BF16)
    ahead = jnp.where(down < over, 1.0, 0.0).astype(BF16)
    same = jnp.where(down == over, 1.0, 0.0).astype(BF16)
    end_row = jnp.dot(units, until, preferred_element_type=F32)[0:1, :] * UNIT
    start_row = jnp.dot(units, ahead, preferred_element_type=F32)[0:1, :] * UNIT
    columns = (((0,), (1,)), ((), ()))
    end_col = lax.dot_general(until, units, columns, preferred_element_type=F32)[:, 0:1] * UNIT
    left_col = lax.dot_general(same, lefts, columns, preferred_element_type=F32)[:, 0:1]
    frame_row = (t * BLK + lax.broadcasted_iota(jnp.int32, (1, BLK), 1)).astype(F32)
    own_seg = jnp.sum(jnp.where(end_col <= frame_row, 1.0, 0.0), axis=0, keepdims=True)
    seg_down = lax.broadcasted_iota(jnp.int32, (128, BLK), 0).astype(F32)
    reach = jnp.sum(jnp.where(seg_down == own_seg, left_col, 0.0), axis=0, keepdims=True)
    lowest = jnp.maximum(own_seg - reach, 0.0)
    bias = jnp.where((seg_down >= lowest) & (seg_down <= own_seg), 0.0, HIDDEN).astype(BF16)

    blank = jnp.zeros((HS, BLK), BF16)
    lane = lax.broadcasted_iota(jnp.int32, (BLK, 128), 1)

    def spread(j, upright, transposed):
        g, half = divmod(j, 2)
        both = [transposed, blank] if half == 0 else [blank, transposed]
        if j < HEADS:
            rhs[j] = jnp.concatenate(both + [bias], axis=0)
        else:
            gt[j - HEADS] = jnp.concatenate(both, axis=0)
        zeros = jnp.zeros((BLK, HS), BF16)
        pair = [upright, zeros] if half == 0 else [zeros, upright]
        rows[g, BLK * half : BLK * (half + 1), :] = jnp.concatenate(pair, axis=1)

    loads[2].wait()
    queries_t = (q_ref[...].astype(F32) * HS**-0.5).astype(BF16)
    for j in range(HEADS):
        mine = queries_t[HS * j : HS * (j + 1), :]
        spread(j, mine.T, mine)
    m_run[...] = jnp.full(m_run.shape, LOWEST, F32)
    l_run[...] = jnp.zeros(l_run.shape, F32)
    out_t[...] = jnp.zeros(out_t.shape, F32)
    dq_t[...] = jnp.zeros(dq_t.shape, F32)
    loads[0].wait()
    loads[1].wait()

    def wait_slot(slot):
        keys(k_hbm, slot, 0, mate).wait_recv()
        values(v_hbm, slot, 1, mate).wait_recv()

    def near_event():
        relay_first.wait_recv()
        relay_second.start()
        near_k.wait_recv()
        chain_k.start()
        pass_near_k.start()
        near_v.wait_recv()
        pass_near_v.start()

    def forward(step, carry):
        @pl.when(step == 1)
        def _():
            loads[3].wait()
            loads[4].wait()
            for copy in across:
                copy.wait_recv()
            grad_t = jnp.dot(w_ref[...], cot_all[...], preferred_element_type=F32).astype(BF16)
            for j in range(HEADS):
                mine = grad_t[HS * j : HS * (j + 1), :]
                spread(j + HEADS, mine.T, mine)

        swapped = jnp.where(step == 0, 0, jnp.where(step < 3, 3 - step, 8 - step))
        slot = jnp.where(core == 0, swapped, step)

        @pl.when(step == 1 + core)
        def _():
            near_event()

        @pl.when((step == 2 - core) | (step == 3) | (step == 5))
        def _():
            wait_slot(slot)

        @pl.when(step == 4)
        def _():
            keys(k_hbm, 4, 0, mate).wait_recv()
            pass_far_k.start()
            values(v_hbm, 4, 1, mate).wait_recv()
            pass_far_v.start()

        kv_all[slot] = slots[slot].T
        first = ((t + tm_count - slot) % tm_count) * BLK
        frames = (first + lax.broadcasted_iota(jnp.int32, (BLK, 128), 0)).astype(F32)
        hot = jnp.where((frames >= start_row) & (frames < end_row), 1.0, 0.0).astype(BF16)
        tops = []
        for turn in range(HEADS + 1):
            if turn < HEADS:
                g = turn // 2
                lhs = jnp.concatenate([kv_all[slot, :, 128 * g : 128 * (g + 1)], hot], axis=1)
                scores = jnp.dot(lhs, rhs[turn], preferred_element_type=F32)
                square[turn % 2] = scores
                tops.append(jnp.max(scores.reshape(BLK // 8, 8, BLK), axis=0))
            if turn == 0:
                continue
            h = turn - 1
            m_old = m_run[h, 0:1, :]
            m_new = jnp.maximum(m_old, jnp.max(tops[h], axis=0, keepdims=True))
            factor = jnp.exp(m_old - m_new)
            total = l_run[h] * factor
            for r in range(0, BLK, STRIP):
                p = jnp.exp(square[h % 2, r : r + STRIP, :] - m_new)
                total = total + jnp.sum(p.reshape(STRIP // 8, 8, BLK), axis=0)
                probs[slot, h, r : r + STRIP, :] = p.astype(BF16)
            m_run[h, 0:1, :] = m_new
            l_run[h] = total
            m_all[slot, h, 0:1, :] = m_new
            here = slice(HS * h, HS * (h + 1))
            out_t[here, :] = out_t[here, :] * factor + jnp.dot(
                slots[slot, WIDTH + HS * h : WIDTH + HS * (h + 1), :],
                probs[slot, h],
                preferred_element_type=F32,
            )
        return carry

    lax.fori_loop(0, BACK + 1, forward, 0)

    for h in range(HEADS):
        here = slice(HS * h, HS * (h + 1))
        total = jnp.sum(l_run[h], axis=0, keepdims=True)
        out = out_t[here, :] / total
        out_t[here, :] = out
        side = HS * ((h + HEADS) % 2)
        own_grad = gt[h, side : side + HS, :].astype(F32)
        delta[h, 0:1, :] = jnp.sum(out * own_grad, axis=0, keepdims=True)
        l_run[h, 0:1, :] = m_run[h, 0:1, :] + jnp.log(total)

    z_copies = [
        push(
            wt.at[(z + i) % 4], z_in.at[i - 1], z_sent.at[i - 1], z_got.at[i - 1], at(t + 8 * i)
        )
        for i in range(1, 4)
    ]
    y_copies = [
        push(
            z_sum.at[pl.ds(pl.multiple_of(40 * ((low + i) % 8), 8), 40)],
            y_in.at[i - 1],
            y_sent.at[i - 1],
            y_got.at[i - 1],
            at(8 * z + (low + i) % 8),
        )
        for i in range(1, 8)
    ]

    far_slot, near_slot, edge_slot = 3 + 2 * core, 1 + 2 * core, 5 - 4 * core
    to_far = push(dkv.at[far_slot], from_mate.at[0], back_sent.at[0], back_got.at[0], mate)
    to_near = push(dkv.at[near_slot], from_mate.at[1], back_sent.at[1], back_got.at[1], mate)
    chain = push(sums.at[0, 0:HALF], chain_in, back_sent.at[2], back_got.at[2], at(t - 2))
    back_first = push(
        sums.at[0, HALF:BLK], relay_back, back_sent.at[3], back_got.at[3], at(after)
    )
    back_second = push(relay_back, home_far, back_sent.at[4], back_got.at[4], at(before - 4))
    homeward = push(sums.at[1], home_near, back_sent.at[5], back_got.at[5], at(t - 2))
    edge_to = at(t - 5 + 4 * core)
    edge_copy = push(dkv.at[edge_slot], edge, back_sent.at[6], back_got.at[6], edge_to)

    def backward(step, carry):
        crossed = jnp.where(
            step < 2, 3 + step, jnp.where(step < 4, step - 1, jnp.where(step == 4, 5, 0))
        )
        slot = jnp.where(core == 0, crossed, 5 - step)
        for turn in range(HEADS + 1):
            if turn < HEADS:
                g = (turn + HEADS) // 2
                grad_p = jnp.dot(
                    kv_all[slot, :, 128 * g : 128 * (g + 1)], gt[turn], preferred_element_type=F32
                )
                scale = jnp.exp(m_all[slot, turn, 0:1, :] - l_run[turn, 0:1, :])
                shift = delta[turn, 0:1, :]
                ds_at, p_at = BLK * (turn % 2), BLK * ((turn + HEADS) % 2)
                for r in range(0, BLK, STRIP):
                    p = probs[slot, turn, r : r + STRIP, :].astype(F32) * scale
                    ds = p * (grad_p[r : r + STRIP] - shift)
                    work[turn // 2, r : r + STRIP, ds_at : ds_at + BLK] = ds.astype(BF16)
                    work[(turn + HEADS) // 2, r : r + STRIP, p_at : p_at + BLK] = p.astype(BF16)
            if turn == 0:
                continue
            h = turn - 1
            here = slice(HS * h, HS * (h + 1))
            ds_at = BLK * (h % 2)
            dq_t[here, :] += jnp.dot(
                slots[slot, here, :],
                work[h // 2, :, ds_at : ds_at + BLK],
                preferred_element_type=F32,
            )
            for g in ((), (0,), (3,), (1,), (2, 4))[h]:
                dkv[slot, :, 128 * g : 128 * (g + 1)] = jnp.dot(
                    work[g], rows[g], preferred_element_type=F32
                ).astype(BF16)

        @pl.when(step == 0)
        def _():
            to_far.start()

        @pl.when(step == 1)
        def _():
            to_far.wait_recv()
            sums[0] = (dkv[4].astype(F32) + from_mate[0].astype(F32)).astype(BF16)
            chain.start()
            back_first.start()
            attn = out_t[...].T.astype(BF16)
            for part in range(4):
                piece = slice(WIDTH * part, WIDTH * (part + 1))
                term = jnp.dot(cot_all[piece, :], attn, preferred_element_type=F32)
                wt[part] = term.astype(BF16)
            for copy in z_copies:
                copy.start()

        @pl.when(step == 2)
        def _():
            to_near.start()

        @pl.when(step == 3)
        def _():
            to_near.wait_recv()
            both = dkv[2].astype(F32) + from_mate[1].astype(F32)
            chain.wait_recv()
            sums[1, 0:HALF] = (both[0:HALF] + chain_in[...].astype(F32)).astype(BF16)
            sums[1, HALF:BLK] = both[HALF:BLK].astype(BF16)
            homeward.start()
            back_first.wait_recv()
            back_second.start()

        @pl.when(step == 4)
        def _():
            edge_copy.start()
            for copy in z_copies:
                copy.wait_recv()
            z_sum[...] = wt[z].astype(F32)
            for i in range(3):
                z_sum[...] += z_in[i].astype(F32)
            for copy in y_copies:
                copy.start()

        return carry

    lax.fori_loop(0, BACK + 1, backward, 0)

    dq_ref[...] = (dq_t[...] * HS**-0.5).astype(BF16)
    total = z_sum[pl.ds(pl.multiple_of(40 * low, 8), 40), :]
    for i, copy in enumerate(y_copies):
        copy.wait_recv()
        total = total + y_in[i]
    dw_ref[...] = total

    edge_copy.wait_recv()
    homeward.wait_recv()
    back_second.wait_recv()
    for half in range(2):
        part = slice(HALF * half, HALF * (half + 1))
        total = dkv[0, part].astype(F32) + edge[part].astype(F32) + home_near[part].astype(F32)
        if half == 1:
            total = total + home_far[...].astype(F32)
        total_t = total.T.astype(BF16)
        dk_ref[:, part] = total_t[:WIDTH]
        dv_ref[:, part] = total_t[WIDTH:]

    copies = [near_k, near_v, relay_first, direct_k, direct_v, chain_k, relay_second]
    copies += [pass_near_k, pass_near_v, pass_far_k, pass_far_v]
    copies += [to_far, to_near, chain, back_first, back_second, homeward, edge_copy]
    for copy in across + copies + z_copies + y_copies:
        copy.wait_send()


def shards(queries, key_rows, value_rows, cotangent, out_weight, segment_units, left_segments):
    tm_count = lax.axis_size("tm")
    head_count = lax.axis_size("head")
    anywhere = pl.BlockSpec(memory_space=pl.ANY)
    vmem = pl.BlockSpec(memory_space=pltpu.VMEM)
    dma = pltpu.SemaphoreType.DMA
    out_t = jax.ShapeDtypeStruct((WIDTH, BLK), BF16)
    both = 2 * WIDTH
    blocks = BACK + 1
    query_t, key_t, value_t, weight_t = pl.pallas_call(
        functools.partial(kernel, tm_count, head_count),
        out_shape=(out_t, out_t, out_t, jax.ShapeDtypeStruct((40, WIDTH), F32)),
        in_specs=[vmem] * 2 + [anywhere] * 5,
        out_specs=(vmem, vmem, vmem, vmem),
        scratch_shapes=[
            pltpu.VMEM((blocks, both, BLK), BF16),
            pltpu.VMEM((WIDTH, BLK), BF16),
            pltpu.VMEM((blocks, BLK, both), BF16),
            pltpu.VMEM((blocks, HEADS, BLK, BLK), BF16),
            pltpu.VMEM((head_count * WIDTH, BLK), BF16),
            pltpu.VMEM((WIDTH, head_count * WIDTH), BF16),
            pltpu.VMEM((WIDTH, BLK), BF16),
            pltpu.VMEM((HEADS, 256, BLK), BF16),
            pltpu.VMEM((HEADS, 128, BLK), BF16),
            pltpu.VMEM((HEADS, 2 * BLK, 128), BF16),
            pltpu.VMEM((2, BLK, BLK), F32),
            pltpu.VMEM((HEADS, BLK, 2 * BLK), BF16),
            pltpu.VMEM((WIDTH, BLK), F32),
            pltpu.VMEM((WIDTH, BLK), F32),
            pltpu.VMEM((blocks, HEADS, 8, BLK), F32),
            pltpu.VMEM((HEADS, 8, BLK), F32),
            pltpu.VMEM((HEADS, 8, BLK), F32),
            pltpu.VMEM((HEADS, 8, BLK), F32),
            pltpu.VMEM((blocks, BLK, both), BF16),
            pltpu.VMEM((2, BLK, both), BF16),
            pltpu.VMEM((2, BLK, both), BF16),
            pltpu.VMEM((BLK, both), BF16),
            pltpu.VMEM((HALF, both), BF16),
            pltpu.VMEM((HALF, both), BF16),
            pltpu.VMEM((HALF, both), BF16),
            pltpu.VMEM((BLK, both), BF16),
            pltpu.VMEM((4, WIDTH, WIDTH), BF16),
            pltpu.VMEM((3, WIDTH, WIDTH), BF16),
            pltpu.VMEM((WIDTH, WIDTH), F32),
            pltpu.VMEM((7, 40, WIDTH), F32),
            dma((5,)),
            dma((11,)),
            dma((blocks,)),
            dma((blocks,)),
            dma((1,)),
            dma((3,)),
            dma((3,)),
            dma((7,)),
            dma((7,)),
            dma((3,)),
            dma((3,)),
            dma((7,)),
            dma((7,)),
        ],
        compiler_params=pltpu.CompilerParams(
            collective_id=0, has_side_effects=True, vmem_limit_bytes=60 << 20
        ),
    )(
        segment_units.reshape(1, -1),
        left_segments.reshape(1, -1),
        queries.T,
        key_rows.T,
        value_rows.T,
        cotangent.T,
        out_weight,
    )
    return (query_t.T, key_t.T, value_t.T, weight_t.T)


def solution(mesh):
    placed = (
        P("tm", "head"),
        P("tm", "head"),
        P("tm", "head"),
        P("tm", "head"),
        P("head", None),
        P(),
        P(),
    )
    return jax.shard_map(
        shards,
        mesh=mesh,
        in_specs=placed,
        out_specs=(P("tm", "head"), P("tm", "head"), P("tm", "head"), P("head", "tm")),
        check_vma=False,
    )
```

time: 419 us -> 107 us (0.26)
  the two profiles are of different devices: /device:TPU:8 before, /device:TPU:1 now
where the time goes in v2:
time: 107 us
  Pallas kernels  102 us (95%)
  local copies, waits for them, and re-layouts  4.33 us (4%)
    pallas_call x1, Pallas kernels, shards(): pl.pallas_call(functools.partial(kernel, tm_count, head_count), out_shape...  102 us
    unnamed x10, local copies, waits for them, and re-layouts  4.33 us

profile of v2, /device:TPU:1, one launch (start us, length us, event | category | flops | bytes accessed | tf_op | source)
XLA Modules:
  0.0 106.8 jit_solution(15777168834086480080)
XLA Ops:
  0.6 101.8 %shard_map.102 = (bf16[320,512]{1,0:T(8,128)(2,1)}, bf16[320,512]{1,0:T(8,128)(2,1)}, bf16[320,512]{1,0:T(8,128)(2,1)}, f32[40,320]{1,0:T(8,128)}) custom-call(s32[1,64]{1,0:T(1,128)} %bitcast.18, s32[1,64]{1,0:T(1,128)} %bitcast.19, bf16[320,512]{1,0:T(8,128)(2,1)} %bitcast.13, bf16[320,512]{1,0:T(8,128)(2,1)} %bitcast.14, bf16[320,512]{1,0:T(8,128)(2,1)} %bitcast.15, ...), custom_call_target="tpu_custom_call" | custom-call | tf_op jit(solution)/shard_map/pallas_call | solution.py:466
  102.5 0.0 copy-start.1
  102.5 1.8 %copy.15 = bf16[512,320]{0,1:T(8,128)(2,1)} copy(bf16[512,320]{0,1:T(8,128)(2,1)} %bitcast.12) | data formatting | bytes 655360
  104.2 0.0 copy-done.1
  104.3 0.0 copy-start
  104.3 0.7 copy.16
  105.0 0.4 copy-done
  105.3 0.0 copy-start.2
  105.3 0.7 copy.17
  106.1 0.1 copy-done.2
  106.2 0.6 copy.18
Async XLA Ops:
  102.5 1.8 %copy-start.1 = (bf16[320,512]{1,0:T(8,128)(2,1)S(1)}, bf16[320,512]{1,0:T(8,128)(2,1)}, u32[]{:S(2)}) copy-start(bf16[320,512]{1,0:T(8,128)(2,1)} %get-tuple-element.9) | copy-start | bytes 983044
  104.3 1.1 %copy-start = (bf16[320,512]{1,0:T(8,128)(2,1)S(1)}, bf16[320,512]{1,0:T(8,128)(2,1)}, u32[]{:S(2)}) copy-start(bf16[320,512]{1,0:T(8,128)(2,1)} %get-tuple-element.10) | copy-start | bytes 983044
  105.3 0.9 copy-start.2

commit v3 on v2

--- a/solution.py
+++ b/solution.py
@@ -15,6 +15,7 @@
 BACK = 5
 HALF = BLK // 2
 STRIP = 128
+WIDE = 256
 HIDDEN = -2e30
 LOWEST = -1e30
 F32 = jnp.float32
@@ -38,6 +39,7 @@
     dw_ref,
     slots,
     relay,
+    cross,
     kv_all,
     probs,
     cot_all,
@@ -61,6 +63,7 @@
     home_far,
     chain_in,
     relay_back,
+    cross_back,
     edge,
     wt,
     z_in,
@@ -92,17 +95,17 @@
         return {"tm": (place + tm_count) % tm_count}
 
     def chip(z_place, y_place):
-        return (z_place * 4 + y_place % 4) * 2 + core
+        return (((z_place + 4) % 4) * 4 + y_place % 4) * 2 + core
 
     mate = at(t + 1 - 2 * core)
     before, after = chip(z, y + 3), chip(z, y + 1)
-    src_four = (t + tm_count - 4) % tm_count
-    src_relay = chip(src_four // 8, (src_four // 2) % 4 + 3)
-    own_four = (t + 4) % tm_count
-    own_relay = chip(own_four // 8, (own_four // 2) % 4 + 1)
-
-    greeted = [mate, at(t - 2), at(after), at(src_relay)]
-    greeted += [at(t + 2), at(before), at(own_relay)]
+    inner = jnp.where((y == 1) | (y == 2), 1, 0)
+    relay_to = chip(z + jnp.where(y >= 2, 1, 0), y + 3)
+    relay_from = chip(z - inner, y + 1)
+    back_to = chip(z - jnp.where(y < 2, 1, 0), y + 1)
+    back_from = chip(z + inner, y + 3)
+
+    greeted = [at(t - 2), at(t + 2), at(relay_from), at(back_from)]
     greeted += [{"head": (x + head_count - i) % head_count} for i in sides]
     greeted += [at(t - 8 * i) for i in range(1, 4)]
     greeted += [at(8 * z + (low + 8 - i) % 8) for i in range(1, 8)]
@@ -151,7 +154,9 @@
 
     near_k = keys(k_hbm, 2, 0, at(t + 2))
     near_v = values(v_hbm, 2, 1, at(t + 2))
-    relay_first = push(v_hbm, relay, sent.at[2], got_relay.at[0], at(before))
+    over_first = push(v_hbm, cross, sent.at[1], got_relay.at[1], at(t + 8))
+    over_second = values(cross, 2, 11, at(t - 6))
+    relay_first = push(v_hbm, relay, sent.at[2], got_relay.at[0], at(relay_to))
     near_k.start()
     relay_first.start()
     across = [
@@ -166,7 +171,15 @@
     ]
     for copy in across:
         copy.start()
-    near_v.start()
+
+    @pl.when(y < 3)
+    def _():
+        near_v.start()
+
+    @pl.when(y == 3)
+    def _():
+        over_first.start()
+
     direct_slot = 1 + 4 * core
     direct_to = at(t + 1 + 4 * core)
     direct_k = keys(k_hbm, direct_slot, 3, direct_to)
@@ -174,7 +187,7 @@
     direct_k.start()
     direct_v.start()
     chain_k = keys(key_part(2), 4, 5, at(t + 2))
-    relay_second = values(relay, 4, 6, at(after + 4))
+    relay_second = values(relay, 4, 6, at(before))
     pass_near = 3 - 2 * core
     pass_far = 5 - 2 * core
     pass_near_k = keys(key_part(2), pass_near, 7, mate)
@@ -235,6 +248,12 @@
     def near_event():
         relay_first.wait_recv()
         relay_second.start()
+
+        @pl.when(y == 3)
+        def _():
+            over_first.wait_recv()
+            over_second.start()
+
         near_k.wait_recv()
         chain_k.start()
         pass_near_k.start()
@@ -279,30 +298,42 @@
         for turn in range(HEADS + 1):
             if turn < HEADS:
                 g = turn // 2
-                lhs = jnp.concatenate([kv_all[slot, :, 128 * g : 128 * (g + 1)], hot], axis=1)
-                scores = jnp.dot(lhs, rhs[turn], preferred_element_type=F32)
-                square[turn % 2] = scores
-                tops.append(jnp.max(scores.reshape(BLK // 8, 8, BLK), axis=0))
-            if turn == 0:
-                continue
-            h = turn - 1
-            m_old = m_run[h, 0:1, :]
-            m_new = jnp.maximum(m_old, jnp.max(tops[h], axis=0, keepdims=True))
-            factor = jnp.exp(m_old - m_new)
-            total = l_run[h] * factor
-            for r in range(0, BLK, STRIP):
-                p = jnp.exp(square[h % 2, r : r + STRIP, :] - m_new)
-                total = total + jnp.sum(p.reshape(STRIP // 8, 8, BLK), axis=0)
-                probs[slot, h, r : r + STRIP, :] = p.astype(BF16)
-            m_run[h, 0:1, :] = m_new
-            l_run[h] = total
-            m_all[slot, h, 0:1, :] = m_new
-            here = slice(HS * h, HS * (h + 1))
-            out_t[here, :] = out_t[here, :] * factor + jnp.dot(
-                slots[slot, WIDTH + HS * h : WIDTH + HS * (h + 1), :],
-                probs[slot, h],
-                preferred_element_type=F32,
-            )
+                tops.append([None] * (BLK // WIDE))
+            if turn > 0:
+                h = turn - 1
+                m_old = m_run[h, 0:1, :]
+                top = [jnp.max(part, axis=0, keepdims=True) for part in tops[h]]
+                m_new = jnp.maximum(m_old, jnp.concatenate(top, axis=1))
+                factor = jnp.exp(m_old - m_new)
+                m_run[h, 0:1, :] = m_new
+                m_all[slot, h, 0:1, :] = m_new
+            for c in range(BLK // WIDE):
+                cols = slice(WIDE * c, WIDE * (c + 1))
+                if turn > 0:
+                    total = l_run[h, :, cols] * factor[:, cols]
+                for r in range(0, BLK, STRIP):
+                    if turn < HEADS:
+                        lhs = jnp.concatenate(
+                            [kv_all[slot, r : r + STRIP, 128 * g : 128 * (g + 1)], hot[r : r + STRIP]],
+                            axis=1,
+                        )
+                        scores = jnp.dot(lhs, rhs[turn, :, cols], preferred_element_type=F32)
+                        square[turn % 2, r : r + STRIP, cols] = scores
+                        fold = jnp.max(scores.reshape(STRIP // 8, 8, WIDE), axis=0)
+                        seen = tops[turn][c]
+                        tops[turn][c] = fold if seen is None else jnp.maximum(seen, fold)
+                    if turn > 0:
+                        p = jnp.exp(square[h % 2, r : r + STRIP, cols] - m_new[:, cols])
+                        total = total + jnp.sum(p.reshape(STRIP // 8, 8, WIDE), axis=0)
+                        probs[slot, h, r : r + STRIP, cols] = p.astype(BF16)
+                if turn > 0:
+                    l_run[h, :, cols] = total
+                    here = slice(HS * h, HS * (h + 1))
+                    out_t[here, cols] = out_t[here, cols] * factor[:, cols] + jnp.dot(
+                        slots[slot, WIDTH + HS * h : WIDTH + HS * (h + 1), :],
+                        probs[slot, h, :, cols],
+                        preferred_element_type=F32,
+                    )
         return carry
 
     lax.fori_loop(0, BACK + 1, forward, 0)
@@ -323,6 +354,12 @@
         )
         for i in range(1, 4)
     ]
+    attn = out_t[...].T.astype(BF16)
+    for part in range(4):
+        piece = slice(WIDTH * part, WIDTH * (part + 1))
+        wt[part] = jnp.dot(cot_all[piece, :], attn, preferred_element_type=F32).astype(BF16)
+    for copy in z_copies:
+        copy.start()
     y_copies = [
         push(
             z_sum.at[pl.ds(pl.multiple_of(40 * ((low + i) % 8), 8), 40)],
@@ -339,10 +376,19 @@
     to_near = push(dkv.at[near_slot], from_mate.at[1], back_sent.at[1], back_got.at[1], mate)
     chain = push(sums.at[0, 0:HALF], chain_in, back_sent.at[2], back_got.at[2], at(t - 2))
     back_first = push(
-        sums.at[0, HALF:BLK], relay_back, back_sent.at[3], back_got.at[3], at(after)
+        sums.at[0, HALF:BLK], relay_back, back_sent.at[3], back_got.at[3], at(back_to)
     )
-    back_second = push(relay_back, home_far, back_sent.at[4], back_got.at[4], at(before - 4))
-    homeward = push(sums.at[1], home_near, back_sent.at[5], back_got.at[5], at(t - 2))
+    back_second = push(relay_back, home_far, back_sent.at[4], back_got.at[4], at(after))
+    home_a = push(
+        sums.at[1, 0:HALF], home_near.at[0:HALF], back_sent.at[5], back_got.at[5], at(t - 2)
+    )
+    home_b = push(
+        sums.at[1, HALF:BLK], home_near.at[HALF:BLK], back_sent.at[7], back_got.at[7], at(t - 2)
+    )
+    over_back = push(sums.at[1, HALF:BLK], cross_back, back_sent.at[7], back_got.at[8], at(t - 8))
+    over_home = push(
+        cross_back, home_near.at[HALF:BLK], back_sent.at[8], back_got.at[7], at(t + 6)
+    )
     edge_to = at(t - 5 + 4 * core)
     edge_copy = push(dkv.at[edge_slot], edge, back_sent.at[6], back_got.at[6], edge_to)
 
@@ -354,17 +400,24 @@
         for turn in range(HEADS + 1):
             if turn < HEADS:
                 g = (turn + HEADS) // 2
-                grad_p = jnp.dot(
-                    kv_all[slot, :, 128 * g : 128 * (g + 1)], gt[turn], preferred_element_type=F32
-                )
                 scale = jnp.exp(m_all[slot, turn, 0:1, :] - l_run[turn, 0:1, :])
                 shift = delta[turn, 0:1, :]
                 ds_at, p_at = BLK * (turn % 2), BLK * ((turn + HEADS) % 2)
-                for r in range(0, BLK, STRIP):
-                    p = probs[slot, turn, r : r + STRIP, :].astype(F32) * scale
-                    ds = p * (grad_p[r : r + STRIP] - shift)
-                    work[turn // 2, r : r + STRIP, ds_at : ds_at + BLK] = ds.astype(BF16)
-                    work[(turn + HEADS) // 2, r : r + STRIP, p_at : p_at + BLK] = p.astype(BF16)
+                for c in range(0, BLK, WIDE):
+                    cols = slice(c, c + WIDE)
+                    for r in range(0, BLK, STRIP):
+                        down = slice(r, r + STRIP)
+                        grad_p = jnp.dot(
+                            kv_all[slot, down, 128 * g : 128 * (g + 1)],
+                            gt[turn, :, cols],
+                            preferred_element_type=F32,
+                        )
+                        p = probs[slot, turn, down, cols].astype(F32) * scale[:, cols]
+                        ds = p * (grad_p - shift[:, cols])
+                        work[turn // 2, down, ds_at + c : ds_at + c + WIDE] = ds.astype(BF16)
+                        work[(turn + HEADS) // 2, down, p_at + c : p_at + c + WIDE] = p.astype(
+                            BF16
+                        )
             if turn == 0:
                 continue
             h = turn - 1
@@ -376,9 +429,10 @@
                 preferred_element_type=F32,
             )
             for g in ((), (0,), (3,), (1,), (2, 4))[h]:
-                dkv[slot, :, 128 * g : 128 * (g + 1)] = jnp.dot(
-                    work[g], rows[g], preferred_element_type=F32
-                ).astype(BF16)
+                for r in range(0, BLK, HALF):
+                    dkv[slot, r : r + HALF, 128 * g : 128 * (g + 1)] = jnp.dot(
+                        work[g, r : r + HALF, :], rows[g], preferred_element_type=F32
+                    ).astype(BF16)
 
         @pl.when(step == 0)
         def _():
@@ -390,32 +444,10 @@
             sums[0] = (dkv[4].astype(F32) + from_mate[0].astype(F32)).astype(BF16)
             chain.start()
             back_first.start()
-            attn = out_t[...].T.astype(BF16)
-            for part in range(4):
-                piece = slice(WIDTH * part, WIDTH * (part + 1))
-                term = jnp.dot(cot_all[piece, :], attn, preferred_element_type=F32)
-                wt[part] = term.astype(BF16)
-            for copy in z_copies:
-                copy.start()
 
         @pl.when(step == 2)
         def _():
             to_near.start()
-
-        @pl.when(step == 3)
-        def _():
-            to_near.wait_recv()
-            both = dkv[2].astype(F32) + from_mate[1].astype(F32)
-            chain.wait_recv()
-            sums[1, 0:HALF] = (both[0:HALF] + chain_in[...].astype(F32)).astype(BF16)
-            sums[1, HALF:BLK] = both[HALF:BLK].astype(BF16)
-            homeward.start()
-            back_first.wait_recv()
-            back_second.start()
-
-        @pl.when(step == 4)
-        def _():
-            edge_copy.start()
             for copy in z_copies:
                 copy.wait_recv()
             z_sum[...] = wt[z].astype(F32)
@@ -424,6 +456,35 @@
             for copy in y_copies:
                 copy.start()
 
+        @pl.when(step == 3)
+        def _():
+            to_near.wait_recv()
+            both = dkv[2].astype(F32) + from_mate[1].astype(F32)
+            chain.wait_recv()
+            sums[1, 0:HALF] = (both[0:HALF] + chain_in[...].astype(F32)).astype(BF16)
+            sums[1, HALF:BLK] = both[HALF:BLK].astype(BF16)
+            home_a.start()
+
+            @pl.when(y > 0)
+            def _():
+                home_b.start()
+
+            @pl.when(y == 0)
+            def _():
+                over_back.start()
+
+            back_first.wait_recv()
+            back_second.start()
+
+        @pl.when(step == 4)
+        def _():
+            edge_copy.start()
+
+            @pl.when(y == 0)
+            def _():
+                over_back.wait_recv()
+                over_home.start()
+
         return carry
 
     lax.fori_loop(0, BACK + 1, backward, 0)
@@ -436,7 +497,8 @@
     dw_ref[...] = total
 
     edge_copy.wait_recv()
-    homeward.wait_recv()
+    home_a.wait_recv()
+    home_b.wait_recv()
     back_second.wait_recv()
     for half in range(2):
         part = slice(HALF * half, HALF * (half + 1))
@@ -449,9 +511,17 @@
 
     copies = [near_k, near_v, relay_first, direct_k, direct_v, chain_k, relay_second]
     copies += [pass_near_k, pass_near_v, pass_far_k, pass_far_v]
-    copies += [to_far, to_near, chain, back_first, back_second, homeward, edge_copy]
+    copies += [to_far, to_near, chain, back_first, back_second, home_a, home_b, edge_copy]
     for copy in across + copies + z_copies + y_copies:
         copy.wait_send()
+
+    @pl.when(y == 3)
+    def _():
+        over_second.wait_send()
+
+    @pl.when(y == 0)
+    def _():
+        over_home.wait_send()
 
 
 def shards(queries, key_rows, value_rows, cotangent, out_weight, segment_units, left_segments):
@@ -470,6 +540,7 @@
         out_specs=(vmem, vmem, vmem, vmem),
         scratch_shapes=[
             pltpu.VMEM((blocks, both, BLK), BF16),
+            pltpu.VMEM((WIDTH, BLK), BF16),
             pltpu.VMEM((WIDTH, BLK), BF16),
             pltpu.VMEM((blocks, BLK, both), BF16),
             pltpu.VMEM((blocks, HEADS, BLK, BLK), BF16),
@@ -494,20 +565,21 @@
             pltpu.VMEM((HALF, both), BF16),
             pltpu.VMEM((HALF, both), BF16),
             pltpu.VMEM((HALF, both), BF16),
+            pltpu.VMEM((HALF, both), BF16),
             pltpu.VMEM((BLK, both), BF16),
             pltpu.VMEM((4, WIDTH, WIDTH), BF16),
             pltpu.VMEM((3, WIDTH, WIDTH), BF16),
             pltpu.VMEM((WIDTH, WIDTH), F32),
             pltpu.VMEM((7, 40, WIDTH), F32),
             dma((5,)),
-            dma((11,)),
+            dma((12,)),
             dma((blocks,)),
             dma((blocks,)),
-            dma((1,)),
+            dma((2,)),
             dma((3,)),
             dma((3,)),
-            dma((7,)),
-            dma((7,)),
+            dma((9,)),
+            dma((9,)),
             dma((3,)),
             dma((3,)),
             dma((7,)),

time: 107 us -> 90.9 us (0.85)
  Pallas kernels: 102 us -> 85.7 us
    pallas_call x1, Pallas kernels: 102 us -> 85.7 us  [shards(): pl.pallas_call(functools.partial(kernel, tm_count, head_count), out_shape...]
where the time goes in v3:
time: 90.9 us; the launch traced here: 90.7 us
  Pallas kernels  85.7 us (94%)
  local copies, waits for them, and re-layouts  4.33 us (5%)
    pallas_call x1, Pallas kernels, shards(): pl.pallas_call(functools.partial(kernel, tm_count, head_count), out_shape...  85.7 us
    unnamed x10, local copies, waits for them, and re-layouts  4.33 us

profile of v3, /device:TPU:1, one launch (start us, length us, event | category | flops | bytes accessed | tf_op | source)
XLA Modules:
  0.0 90.7 jit_solution(15811380081532831558)
XLA Ops:
  0.6 85.7 %shard_map.102 = (bf16[320,512]{1,0:T(8,128)(2,1)}, bf16[320,512]{1,0:T(8,128)(2,1)}, bf16[320,512]{1,0:T(8,128)(2,1)}, f32[40,320]{1,0:T(8,128)}) custom-call(s32[1,64]{1,0:T(1,128)} %bitcast.18, s32[1,64]{1,0:T(1,128)} %bitcast.19, bf16[320,512]{1,0:T(8,128)(2,1)} %bitcast.13, bf16[320,512]{1,0:T(8,128)(2,1)} %bitcast.14, bf16[320,512]{1,0:T(8,128)(2,1)} %bitcast.15, ...), custom_call_target="tpu_custom_call" | custom-call | tf_op jit(solution)/shard_map/pallas_call | solution.py:536
  86.4 0.0 copy-start.1
  86.4 1.8 %copy.15 = bf16[512,320]{0,1:T(8,128)(2,1)} copy(bf16[512,320]{0,1:T(8,128)(2,1)} %bitcast.12) | data formatting | bytes 655360
  88.1 0.0 copy-done.1
  88.2 0.0 copy-start
  88.2 0.7 copy.16
  88.9 0.4 copy-done
  89.2 0.0 copy-start.2
  89.2 0.7 copy.17
  90.0 0.1 copy-done.2
  90.1 0.6 copy.18
Async XLA Ops:
  86.4 1.8 %copy-start.1 = (bf16[320,512]{1,0:T(8,128)(2,1)S(1)}, bf16[320,512]{1,0:T(8,128)(2,1)}, u32[]{:S(2)}) copy-start(bf16[320,512]{1,0:T(8,128)(2,1)} %get-tuple-element.9) | copy-start | bytes 983044
  88.2 1.1 %copy-start = (bf16[320,512]{1,0:T(8,128)(2,1)S(1)}, bf16[320,512]{1,0:T(8,128)(2,1)}, u32[]{:S(2)}) copy-start(bf16[320,512]{1,0:T(8,128)(2,1)} %get-tuple-element.10) | copy-start | bytes 983044
  89.2 0.9 copy-start.2

commit v4 on v3

--- a/solution.py
+++ b/solution.py
@@ -290,50 +290,50 @@
             values(v_hbm, 4, 1, mate).wait_recv()
             pass_far_v.start()
 
-        kv_all[slot] = slots[slot].T
+        def upright(g):
+            group = slice(128 * g, 128 * (g + 1))
+            kv_all[slot, :, group] = slots[slot, group, :].T
+
         first = ((t + tm_count - slot) % tm_count) * BLK
         frames = (first + lax.broadcasted_iota(jnp.int32, (BLK, 128), 0)).astype(F32)
         hot = jnp.where((frames >= start_row) & (frames < end_row), 1.0, 0.0).astype(BF16)
-        tops = []
-        for turn in range(HEADS + 1):
-            if turn < HEADS:
-                g = turn // 2
-                tops.append([None] * (BLK // WIDE))
-            if turn > 0:
-                h = turn - 1
-                m_old = m_run[h, 0:1, :]
-                top = [jnp.max(part, axis=0, keepdims=True) for part in tops[h]]
-                m_new = jnp.maximum(m_old, jnp.concatenate(top, axis=1))
-                factor = jnp.exp(m_old - m_new)
-                m_run[h, 0:1, :] = m_new
-                m_all[slot, h, 0:1, :] = m_new
-            for c in range(BLK // WIDE):
+        upright(0)
+        pieces = BLK // WIDE
+        units_of = HEADS * pieces
+        top = None
+        for turn in range(units_of + 1):
+            last = top
+            if turn < units_of:
+                h, c = divmod(turn, pieces)
                 cols = slice(WIDE * c, WIDE * (c + 1))
-                if turn > 0:
-                    total = l_run[h, :, cols] * factor[:, cols]
-                for r in range(0, BLK, STRIP):
-                    if turn < HEADS:
-                        lhs = jnp.concatenate(
-                            [kv_all[slot, r : r + STRIP, 128 * g : 128 * (g + 1)], hot[r : r + STRIP]],
-                            axis=1,
-                        )
-                        scores = jnp.dot(lhs, rhs[turn, :, cols], preferred_element_type=F32)
-                        square[turn % 2, r : r + STRIP, cols] = scores
-                        fold = jnp.max(scores.reshape(STRIP // 8, 8, WIDE), axis=0)
-                        seen = tops[turn][c]
-                        tops[turn][c] = fold if seen is None else jnp.maximum(seen, fold)
-                    if turn > 0:
-                        p = jnp.exp(square[h % 2, r : r + STRIP, cols] - m_new[:, cols])
-                        total = total + jnp.sum(p.reshape(STRIP // 8, 8, WIDE), axis=0)
-                        probs[slot, h, r : r + STRIP, cols] = p.astype(BF16)
-                if turn > 0:
-                    l_run[h, :, cols] = total
-                    here = slice(HS * h, HS * (h + 1))
-                    out_t[here, cols] = out_t[here, cols] * factor[:, cols] + jnp.dot(
-                        slots[slot, WIDTH + HS * h : WIDTH + HS * (h + 1), :],
-                        probs[slot, h, :, cols],
-                        preferred_element_type=F32,
-                    )
+                g = h // 2
+                lhs = jnp.concatenate([kv_all[slot, :, 128 * g : 128 * (g + 1)], hot], axis=1)
+                scores = jnp.dot(lhs, rhs[h, :, cols], preferred_element_type=F32)
+                square[turn % 2] = scores
+                top = jnp.max(scores.reshape(BLK // 8, 8, WIDE), axis=0)
+                if turn < HEADS - 1:
+                    upright(turn + 1)
+            if turn == 0:
+                continue
+            h, c = divmod(turn - 1, pieces)
+            cols = slice(WIDE * c, WIDE * (c + 1))
+            m_old = m_run[h, 0:1, cols]
+            m_new = jnp.maximum(m_old, jnp.max(last, axis=0, keepdims=True))
+            factor = jnp.exp(m_old - m_new)
+            m_run[h, 0:1, cols] = m_new
+            m_all[slot, h, 0:1, cols] = m_new
+            total = l_run[h, :, cols] * factor
+            for r in range(0, BLK, STRIP):
+                p = jnp.exp(square[(turn - 1) % 2, r : r + STRIP, :] - m_new)
+                total = total + jnp.sum(p.reshape(STRIP // 8, 8, WIDE), axis=0)
+                probs[slot, h, r : r + STRIP, cols] = p.astype(BF16)
+            l_run[h, :, cols] = total
+            here = slice(HS * h, HS * (h + 1))
+            out_t[here, cols] = out_t[here, cols] * factor + jnp.dot(
+                slots[slot, WIDTH + HS * h : WIDTH + HS * (h + 1), :],
+                probs[slot, h, :, cols],
+                preferred_element_type=F32,
+            )
         return carry
 
     lax.fori_loop(0, BACK + 1, forward, 0)
@@ -397,42 +397,43 @@
             step < 2, 3 + step, jnp.where(step < 4, step - 1, jnp.where(step == 4, 5, 0))
         )
         slot = jnp.where(core == 0, crossed, 5 - step)
-        for turn in range(HEADS + 1):
-            if turn < HEADS:
-                g = (turn + HEADS) // 2
-                scale = jnp.exp(m_all[slot, turn, 0:1, :] - l_run[turn, 0:1, :])
-                shift = delta[turn, 0:1, :]
-                ds_at, p_at = BLK * (turn % 2), BLK * ((turn + HEADS) % 2)
-                for c in range(0, BLK, WIDE):
-                    cols = slice(c, c + WIDE)
-                    for r in range(0, BLK, STRIP):
-                        down = slice(r, r + STRIP)
-                        grad_p = jnp.dot(
-                            kv_all[slot, down, 128 * g : 128 * (g + 1)],
-                            gt[turn, :, cols],
-                            preferred_element_type=F32,
-                        )
-                        p = probs[slot, turn, down, cols].astype(F32) * scale[:, cols]
-                        ds = p * (grad_p - shift[:, cols])
-                        work[turn // 2, down, ds_at + c : ds_at + c + WIDE] = ds.astype(BF16)
-                        work[(turn + HEADS) // 2, down, p_at + c : p_at + c + WIDE] = p.astype(
-                            BF16
-                        )
+        pieces = BLK // WIDE
+        units_of = HEADS * pieces
+        for turn in range(units_of + 1):
+            if turn < units_of:
+                h, c = divmod(turn, pieces)
+                g = (h + HEADS) // 2
+                square[turn % 2] = jnp.dot(
+                    kv_all[slot, :, 128 * g : 128 * (g + 1)],
+                    gt[h, :, WIDE * c : WIDE * (c + 1)],
+                    preferred_element_type=F32,
+                )
             if turn == 0:
                 continue
-            h = turn - 1
+            h, c = divmod(turn - 1, pieces)
+            cols = slice(WIDE * c, WIDE * (c + 1))
+            scale = jnp.exp(m_all[slot, h, 0:1, cols] - l_run[h, 0:1, cols])
+            shift = delta[h, 0:1, cols]
+            ds_at = BLK * (h % 2) + WIDE * c
+            p_at = BLK * ((h + HEADS) % 2) + WIDE * c
+            for r in range(0, BLK, STRIP):
+                down = slice(r, r + STRIP)
+                p = probs[slot, h, down, cols].astype(F32) * scale
+                ds = p * (square[(turn - 1) % 2, down, :] - shift)
+                work[h // 2, down, ds_at : ds_at + WIDE] = ds.astype(BF16)
+                work[(h + HEADS) // 2, down, p_at : p_at + WIDE] = p.astype(BF16)
             here = slice(HS * h, HS * (h + 1))
-            ds_at = BLK * (h % 2)
-            dq_t[here, :] += jnp.dot(
+            dq_t[here, cols] += jnp.dot(
                 slots[slot, here, :],
-                work[h // 2, :, ds_at : ds_at + BLK],
+                work[h // 2, :, ds_at : ds_at + WIDE],
                 preferred_element_type=F32,
             )
+            if c < pieces - 1:
+                continue
             for g in ((), (0,), (3,), (1,), (2, 4))[h]:
-                for r in range(0, BLK, HALF):
-                    dkv[slot, r : r + HALF, 128 * g : 128 * (g + 1)] = jnp.dot(
-                        work[g, r : r + HALF, :], rows[g], preferred_element_type=F32
-                    ).astype(BF16)
+                dkv[slot, :, 128 * g : 128 * (g + 1)] = jnp.dot(
+                    work[g], rows[g], preferred_element_type=F32
+                ).astype(BF16)
 
         @pl.when(step == 0)
         def _():
@@ -550,7 +551,7 @@
             pltpu.VMEM((HEADS, 256, BLK), BF16),
             pltpu.VMEM((HEADS, 128, BLK), BF16),
             pltpu.VMEM((HEADS, 2 * BLK, 128), BF16),
-            pltpu.VMEM((2, BLK, BLK), F32),
+            pltpu.VMEM((2, BLK, WIDE), F32),
             pltpu.VMEM((HEADS, BLK, 2 * BLK), BF16),
             pltpu.VMEM((WIDTH, BLK), F32),
             pltpu.VMEM((WIDTH, BLK), F32),

time: 90.9 us -> 90.9 us (level)
  no operation moved by 1% of the time
where the time goes in v4:
time: 90.9 us; the launch traced here: 90.7 us
  Pallas kernels  85.7 us (94%)
  local copies, waits for them, and re-layouts  4.33 us (5%)
    pallas_call x1, Pallas kernels, shards(): pl.pallas_call(functools.partial(kernel, tm_count, head_count), out_shape...  85.7 us
    unnamed x10, local copies, waits for them, and re-layouts  4.33 us

profile of v4, /device:TPU:1, one launch (start us, length us, event | category | flops | bytes accessed | tf_op | source)
XLA Modules:
  0.0 90.7 jit_solution(5305288435951318415)
XLA Ops:
  0.6 85.7 %shard_map.102 = (bf16[320,512]{1,0:T(8,128)(2,1)}, bf16[320,512]{1,0:T(8,128)(2,1)}, bf16[320,512]{1,0:T(8,128)(2,1)}, f32[40,320]{1,0:T(8,128)}) custom-call(s32[1,64]{1,0:T(1,128)} %bitcast.18, s32[1,64]{1,0:T(1,128)} %bitcast.19, bf16[320,512]{1,0:T(8,128)(2,1)} %bitcast.13, bf16[320,512]{1,0:T(8,128)(2,1)} %bitcast.14, bf16[320,512]{1,0:T(8,128)(2,1)} %bitcast.15, ...), custom_call_target="tpu_custom_call" | custom-call | tf_op jit(solution)/shard_map/pallas_call | solution.py:537
  86.3 0.0 copy-start.1
  86.3 1.8 %copy.15 = bf16[512,320]{0,1:T(8,128)(2,1)} copy(bf16[512,320]{0,1:T(8,128)(2,1)} %bitcast.12) | data formatting | bytes 655360
  88.1 0.0 copy-done.1
  88.1 0.0 copy-start
  88.1 0.7 copy.16
  88.8 0.4 copy-done
  89.2 0.0 copy-start.2
  89.2 0.7 copy.17
  89.9 0.1 copy-done.2
  90.0 0.6 copy.18
Async XLA Ops:
  86.3 1.8 %copy-start.1 = (bf16[320,512]{1,0:T(8,128)(2,1)S(1)}, bf16[320,512]{1,0:T(8,128)(2,1)}, u32[]{:S(2)}) copy-start(bf16[320,512]{1,0:T(8,128)(2,1)} %get-tuple-element.9) | copy-start | bytes 983044
  88.1 1.1 %copy-start = (bf16[320,512]{1,0:T(8,128)(2,1)S(1)}, bf16[320,512]{1,0:T(8,128)(2,1)}, u32[]{:S(2)}) copy-start(bf16[320,512]{1,0:T(8,128)(2,1)} %get-tuple-element.10) | copy-start | bytes 983044
  89.2 0.9 copy-start.2

commit v5 on v4

--- a/solution.py
+++ b/solution.py
@@ -78,6 +78,8 @@
     side_got,
     back_sent,
     back_got,
+    mate_sent,
+    mate_got,
     z_sent,
     z_got,
     y_sent,
@@ -184,8 +186,12 @@
     direct_to = at(t + 1 + 4 * core)
     direct_k = keys(k_hbm, direct_slot, 3, direct_to)
     direct_v = values(v_hbm, direct_slot, 4, direct_to)
-    direct_k.start()
-    direct_v.start()
+
+    @pl.when(core == 0)
+    def _():
+        direct_k.start()
+        direct_v.start()
+
     chain_k = keys(key_part(2), 4, 5, at(t + 2))
     relay_second = values(relay, 4, 6, at(before))
     pass_near = 3 - 2 * core
@@ -249,11 +255,6 @@
         relay_first.wait_recv()
         relay_second.start()
 
-        @pl.when(y == 3)
-        def _():
-            over_first.wait_recv()
-            over_second.start()
-
         near_k.wait_recv()
         chain_k.start()
         pass_near_k.start()
@@ -261,6 +262,16 @@
         pass_near_v.start()
 
     def forward(step, carry):
+        @pl.when((step == 1) & (core == 1))
+        def _():
+            direct_k.start()
+            direct_v.start()
+
+        @pl.when((step == 1) & (y == 3))
+        def _():
+            over_first.wait_recv()
+            over_second.start()
+
         @pl.when(step == 1)
         def _():
             loads[3].wait()
@@ -292,7 +303,9 @@
 
         def upright(g):
             group = slice(128 * g, 128 * (g + 1))
-            kv_all[slot, :, group] = slots[slot, group, :].T
+            turned = slots[slot, group, :].T
+            kv_all[2 * slot, :, group] = turned[0:HALF]
+            kv_all[2 * slot + 1, :, group] = turned[HALF:BLK]
 
         first = ((t + tm_count - slot) % tm_count) * BLK
         frames = (first + lax.broadcasted_iota(jnp.int32, (BLK, 128), 0)).astype(F32)
@@ -307,7 +320,9 @@
                 h, c = divmod(turn, pieces)
                 cols = slice(WIDE * c, WIDE * (c + 1))
                 g = h // 2
-                lhs = jnp.concatenate([kv_all[slot, :, 128 * g : 128 * (g + 1)], hot], axis=1)
+                group = slice(128 * g, 128 * (g + 1))
+                keys_here = [kv_all[2 * slot, :, group], kv_all[2 * slot + 1, :, group]]
+                lhs = jnp.concatenate([jnp.concatenate(keys_here, axis=0), hot], axis=1)
                 scores = jnp.dot(lhs, rhs[h, :, cols], preferred_element_type=F32)
                 square[turn % 2] = scores
                 top = jnp.max(scores.reshape(BLK // 8, 8, WIDE), axis=0)
@@ -326,14 +341,18 @@
             for r in range(0, BLK, STRIP):
                 p = jnp.exp(square[(turn - 1) % 2, r : r + STRIP, :] - m_new)
                 total = total + jnp.sum(p.reshape(STRIP // 8, 8, WIDE), axis=0)
-                probs[slot, h, r : r + STRIP, cols] = p.astype(BF16)
+                half, row = divmod(r, HALF)
+                probs[2 * slot + half, h, row : row + STRIP, cols] = p.astype(BF16)
             l_run[h, :, cols] = total
             here = slice(HS * h, HS * (h + 1))
-            out_t[here, cols] = out_t[here, cols] * factor + jnp.dot(
-                slots[slot, WIDTH + HS * h : WIDTH + HS * (h + 1), :],
-                probs[slot, h, :, cols],
-                preferred_element_type=F32,
-            )
+            added = out_t[here, cols] * factor
+            for half in range(2):
+                added += jnp.dot(
+                    slots[slot, WIDTH + HS * h : WIDTH + HS * (h + 1), half * HALF : (half + 1) * HALF],
+                    probs[2 * slot + half, h, :, cols],
+                    preferred_element_type=F32,
+                )
+            out_t[here, cols] = added
         return carry
 
     lax.fori_loop(0, BACK + 1, forward, 0)
@@ -354,12 +373,6 @@
         )
         for i in range(1, 4)
     ]
-    attn = out_t[...].T.astype(BF16)
-    for part in range(4):
-        piece = slice(WIDTH * part, WIDTH * (part + 1))
-        wt[part] = jnp.dot(cot_all[piece, :], attn, preferred_element_type=F32).astype(BF16)
-    for copy in z_copies:
-        copy.start()
     y_copies = [
         push(
             z_sum.at[pl.ds(pl.multiple_of(40 * ((low + i) % 8), 8), 40)],
@@ -371,40 +384,52 @@
         for i in range(1, 8)
     ]
 
-    far_slot, near_slot, edge_slot = 3 + 2 * core, 1 + 2 * core, 5 - 4 * core
-    to_far = push(dkv.at[far_slot], from_mate.at[0], back_sent.at[0], back_got.at[0], mate)
-    to_near = push(dkv.at[near_slot], from_mate.at[1], back_sent.at[1], back_got.at[1], mate)
-    chain = push(sums.at[0, 0:HALF], chain_in, back_sent.at[2], back_got.at[2], at(t - 2))
-    back_first = push(
-        sums.at[0, HALF:BLK], relay_back, back_sent.at[3], back_got.at[3], at(back_to)
-    )
-    back_second = push(relay_back, home_far, back_sent.at[4], back_got.at[4], at(after))
-    home_a = push(
-        sums.at[1, 0:HALF], home_near.at[0:HALF], back_sent.at[5], back_got.at[5], at(t - 2)
-    )
-    home_b = push(
-        sums.at[1, HALF:BLK], home_near.at[HALF:BLK], back_sent.at[7], back_got.at[7], at(t - 2)
-    )
-    over_back = push(sums.at[1, HALF:BLK], cross_back, back_sent.at[7], back_got.at[8], at(t - 8))
-    over_home = push(
-        cross_back, home_near.at[HALF:BLK], back_sent.at[8], back_got.at[7], at(t + 6)
-    )
-    edge_to = at(t - 5 + 4 * core)
-    edge_copy = push(dkv.at[edge_slot], edge, back_sent.at[6], back_got.at[6], edge_to)
+    def piece(slot, half):
+        return dkv.at[2 * slot + half]
+
+    def to_mate(pair, half):
+        number = 2 * pair + half
+        return push(
+            piece(3 + 2 * core - 2 * pair, half),
+            from_mate.at[number],
+            mate_sent.at[number],
+            mate_got.at[number],
+            mate,
+        )
+
+    mated = [[to_mate(pair, half) for half in range(2)] for pair in range(2)]
+    chain = push(sums.at[0], chain_in, back_sent.at[0], back_got.at[0], at(t - 2))
+    back_first = push(sums.at[1], relay_back, back_sent.at[1], back_got.at[1], at(back_to))
+    back_second = push(relay_back, home_far, back_sent.at[2], back_got.at[2], at(after))
+    home_a = push(sums.at[2], home_near.at[0], back_sent.at[3], back_got.at[3], at(t - 2))
+    home_b = push(sums.at[3], home_near.at[1], back_sent.at[4], back_got.at[4], at(t - 2))
+    over_back = push(sums.at[3], cross_back, back_sent.at[4], back_got.at[5], at(t - 8))
+    over_home = push(cross_back, home_near.at[1], back_sent.at[5], back_got.at[4], at(t + 6))
+    edge_copies = [
+        push(
+            piece(5 - 4 * core, half),
+            edge.at[half],
+            back_sent.at[6 + half],
+            back_got.at[6 + half],
+            at(t - 5 + 4 * core),
+        )
+        for half in range(2)
+    ]
 
     def backward(step, carry):
-        crossed = jnp.where(
-            step < 2, 3 + step, jnp.where(step < 4, step - 1, jnp.where(step == 4, 5, 0))
-        )
-        slot = jnp.where(core == 0, crossed, 5 - step)
+        pair, within = step // 4, step % 4
+        paired = jnp.where(within % 2 == 0, 3 + 2 * core, 4) - 2 * pair
+        slot = jnp.where(step < 8, paired, jnp.where(step < 10, 5 - 4 * core, 0))
+        half = jnp.where(step < 8, within // 2, step % 2)
+        here = 2 * slot + half
         pieces = BLK // WIDE
         units_of = HEADS * pieces
         for turn in range(units_of + 1):
             if turn < units_of:
                 h, c = divmod(turn, pieces)
                 g = (h + HEADS) // 2
-                square[turn % 2] = jnp.dot(
-                    kv_all[slot, :, 128 * g : 128 * (g + 1)],
+                square[turn % 2, 0:HALF] = jnp.dot(
+                    kv_all[here, :, 128 * g : 128 * (g + 1)],
                     gt[h, :, WIDE * c : WIDE * (c + 1)],
                     preferred_element_type=F32,
                 )
@@ -416,39 +441,83 @@
             shift = delta[h, 0:1, cols]
             ds_at = BLK * (h % 2) + WIDE * c
             p_at = BLK * ((h + HEADS) % 2) + WIDE * c
-            for r in range(0, BLK, STRIP):
+            for r in range(0, HALF, STRIP):
                 down = slice(r, r + STRIP)
-                p = probs[slot, h, down, cols].astype(F32) * scale
+                p = probs[here, h, down, cols].astype(F32) * scale
                 ds = p * (square[(turn - 1) % 2, down, :] - shift)
                 work[h // 2, down, ds_at : ds_at + WIDE] = ds.astype(BF16)
                 work[(h + HEADS) // 2, down, p_at : p_at + WIDE] = p.astype(BF16)
-            here = slice(HS * h, HS * (h + 1))
-            dq_t[here, cols] += jnp.dot(
-                slots[slot, here, :],
+            mine = slice(HS * h, HS * (h + 1))
+            dq_t[mine, cols] += jnp.dot(
+                slots[slot, mine, pl.ds(pl.multiple_of(HALF * half, HALF), HALF)],
                 work[h // 2, :, ds_at : ds_at + WIDE],
                 preferred_element_type=F32,
             )
             if c < pieces - 1:
                 continue
             for g in ((), (0,), (3,), (1,), (2, 4))[h]:
-                dkv[slot, :, 128 * g : 128 * (g + 1)] = jnp.dot(
+                dkv[here, :, 128 * g : 128 * (g + 1)] = jnp.dot(
                     work[g], rows[g], preferred_element_type=F32
                 ).astype(BF16)
 
-        @pl.when(step == 0)
-        def _():
-            to_far.start()
+        for j in range(2):
+            for k in range(2):
+
+                @pl.when(step == 4 * j + 2 * k)
+                def _(j=j, k=k):
+                    mated[j][k].start()
+
+        def summed(pair, half):
+            mated[pair][half].wait_recv()
+            kept = dkv[2 * (4 - 2 * pair) + half].astype(F32)
+            return kept + from_mate[2 * pair + half].astype(F32)
 
         @pl.when(step == 1)
         def _():
-            to_far.wait_recv()
-            sums[0] = (dkv[4].astype(F32) + from_mate[0].astype(F32)).astype(BF16)
+            sums[0] = summed(0, 0).astype(BF16)
             chain.start()
+
+        @pl.when(step == 3)
+        def _():
+            sums[1] = summed(0, 1).astype(BF16)
             back_first.start()
-
-        @pl.when(step == 2)
-        def _():
-            to_near.start()
+            attn = out_t[...].T.astype(BF16)
+            for part in range(4):
+                some = slice(WIDTH * part, WIDTH * (part + 1))
+                term = jnp.dot(cot_all[some, :], attn, preferred_element_type=F32)
+                wt[part] = term.astype(BF16)
+            for copy in z_copies:
+                copy.start()
+
+        @pl.when(step == 5)
+        def _():
+            both = summed(1, 0)
+            chain.wait_recv()
+            sums[2] = (both + chain_in[...].astype(F32)).astype(BF16)
+            home_a.start()
+
+        @pl.when(step == 7)
+        def _():
+            sums[3] = summed(1, 1).astype(BF16)
+
+            @pl.when(y > 0)
+            def _():
+                home_b.start()
+
+            @pl.when(y == 0)
+            def _():
+                over_back.start()
+
+            back_first.wait_recv()
+            back_second.start()
+
+        @pl.when(step == 8)
+        def _():
+            edge_copies[0].start()
+
+        @pl.when(step == 9)
+        def _():
+            edge_copies[1].start()
             for copy in z_copies:
                 copy.wait_recv()
             z_sum[...] = wt[z].astype(F32)
@@ -457,38 +526,14 @@
             for copy in y_copies:
                 copy.start()
 
-        @pl.when(step == 3)
-        def _():
-            to_near.wait_recv()
-            both = dkv[2].astype(F32) + from_mate[1].astype(F32)
-            chain.wait_recv()
-            sums[1, 0:HALF] = (both[0:HALF] + chain_in[...].astype(F32)).astype(BF16)
-            sums[1, HALF:BLK] = both[HALF:BLK].astype(BF16)
-            home_a.start()
-
-            @pl.when(y > 0)
-            def _():
-                home_b.start()
-
-            @pl.when(y == 0)
-            def _():
-                over_back.start()
-
-            back_first.wait_recv()
-            back_second.start()
-
-        @pl.when(step == 4)
-        def _():
-            edge_copy.start()
-
-            @pl.when(y == 0)
-            def _():
-                over_back.wait_recv()
-                over_home.start()
+        @pl.when((step == 9) & (y == 0))
+        def _():
+            over_back.wait_recv()
+            over_home.start()
 
         return carry
 
-    lax.fori_loop(0, BACK + 1, backward, 0)
+    lax.fori_loop(0, 2 * (BACK + 1), backward, 0)
 
     dq_ref[...] = (dq_t[...] * HS**-0.5).astype(BF16)
     total = z_sum[pl.ds(pl.multiple_of(40 * low, 8), 40), :]
@@ -497,13 +542,11 @@
         total = total + y_in[i]
     dw_ref[...] = total
 
-    edge_copy.wait_recv()
-    home_a.wait_recv()
-    home_b.wait_recv()
-    back_second.wait_recv()
+    for copy in edge_copies + [home_a, home_b, back_second]:
+        copy.wait_recv()
     for half in range(2):
         part = slice(HALF * half, HALF * (half + 1))
-        total = dkv[0, part].astype(F32) + edge[part].astype(F32) + home_near[part].astype(F32)
+        total = dkv[half].astype(F32) + edge[half].astype(F32) + home_near[half].astype(F32)
         if half == 1:
             total = total + home_far[...].astype(F32)
         total_t = total.T.astype(BF16)
@@ -512,7 +555,8 @@
 
     copies = [near_k, near_v, relay_first, direct_k, direct_v, chain_k, relay_second]
     copies += [pass_near_k, pass_near_v, pass_far_k, pass_far_v]
-    copies += [to_far, to_near, chain, back_first, back_second, home_a, home_b, edge_copy]
+    copies += mated[0] + mated[1] + edge_copies
+    copies += [chain, back_first, back_second, home_a, home_b]
     for copy in across + copies + z_copies + y_copies:
         copy.wait_send()
 
@@ -543,8 +587,8 @@
             pltpu.VMEM((blocks, both, BLK), BF16),
             pltpu.VMEM((WIDTH, BLK), BF16),
             pltpu.VMEM((WIDTH, BLK), BF16),
-            pltpu.VMEM((blocks, BLK, both), BF16),
-            pltpu.VMEM((blocks, HEADS, BLK, BLK), BF16),
+            pltpu.VMEM((2 * blocks, HALF, both), BF16),
+            pltpu.VMEM((2 * blocks, HEADS, HALF, BLK), BF16),
             pltpu.VMEM((head_count * WIDTH, BLK), BF16),
             pltpu.VMEM((WIDTH, head_count * WIDTH), BF16),
             pltpu.VMEM((WIDTH, BLK), BF16),
@@ -552,22 +596,22 @@
             pltpu.VMEM((HEADS, 128, BLK), BF16),
             pltpu.VMEM((HEADS, 2 * BLK, 128), BF16),
             pltpu.VMEM((2, BLK, WIDE), F32),
-            pltpu.VMEM((HEADS, BLK, 2 * BLK), BF16),
+            pltpu.VMEM((HEADS, HALF, 2 * BLK), BF16),
             pltpu.VMEM((WIDTH, BLK), F32),
             pltpu.VMEM((WIDTH, BLK), F32),
             pltpu.VMEM((blocks, HEADS, 8, BLK), F32),
             pltpu.VMEM((HEADS, 8, BLK), F32),
             pltpu.VMEM((HEADS, 8, BLK), F32),
             pltpu.VMEM((HEADS, 8, BLK), F32),
-            pltpu.VMEM((blocks, BLK, both), BF16),
-            pltpu.VMEM((2, BLK, both), BF16),
-            pltpu.VMEM((2, BLK, both), BF16),
-            pltpu.VMEM((BLK, both), BF16),
+            pltpu.VMEM((2 * blocks, HALF, both), BF16),
+            pltpu.VMEM((4, HALF, both), BF16),
+            pltpu.VMEM((4, HALF, both), BF16),
+            pltpu.VMEM((2, HALF, both), BF16),
             pltpu.VMEM((HALF, both), BF16),
             pltpu.VMEM((HALF, both), BF16),
             pltpu.VMEM((HALF, both), BF16),
             pltpu.VMEM((HALF, both), BF16),
-            pltpu.VMEM((BLK, both), BF16),
+            pltpu.VMEM((2, HALF, both), BF16),
             pltpu.VMEM((4, WIDTH, WIDTH), BF16),
             pltpu.VMEM((3, WIDTH, WIDTH), BF16),
             pltpu.VMEM((WIDTH, WIDTH), F32),
@@ -579,8 +623,10 @@
             dma((2,)),
             dma((3,)),
             dma((3,)),
-            dma((9,)),
-            dma((9,)),
+            dma((8,)),
+            dma((8,)),
+            dma((4,)),
+            dma((4,)),
             dma((3,)),
             dma((3,)),
             dma((7,)),

time: 90.9 us -> 93.9 us (1.033)
  Pallas kernels: 85.7 us -> 88.6 us
    pallas_call x1, Pallas kernels: 85.7 us -> 88.6 us  [shards(): pl.pallas_call(functools.partial(kernel, tm_count, head_count), out_shape...]
where the time goes in v5:
time: 93.9 us; the launch traced here: 93.6 us
  Pallas kernels  88.6 us (94%)
  local copies, waits for them, and re-layouts  4.33 us (5%)
    pallas_call x1, Pallas kernels, shards(): pl.pallas_call(functools.partial(kernel, tm_count, head_count), out_shape...  88.6 us
    unnamed x10, local copies, waits for them, and re-layouts  4.33 us

profile of v5, /device:TPU:1, one launch (start us, length us, event | category | flops | bytes accessed | tf_op | source)
XLA Modules:
  0.0 93.6 jit_solution(16781560204481222734)
XLA Ops:
  0.6 88.6 %shard_map.102 = (bf16[320,512]{1,0:T(8,128)(2,1)}, bf16[320,512]{1,0:T(8,128)(2,1)}, bf16[320,512]{1,0:T(8,128)(2,1)}, f32[40,320]{1,0:T(8,128)}) custom-call(s32[1,64]{1,0:T(1,128)} %bitcast.18, s32[1,64]{1,0:T(1,128)} %bitcast.19, bf16[320,512]{1,0:T(8,128)(2,1)} %bitcast.13, bf16[320,512]{1,0:T(8,128)(2,1)} %bitcast.14, bf16[320,512]{1,0:T(8,128)(2,1)} %bitcast.15, ...), custom_call_target="tpu_custom_call" | custom-call | tf_op jit(solution)/shard_map/pallas_call | solution.py:581
  89.2 0.0 copy-start.1
  89.3 1.8 %copy.15 = bf16[512,320]{0,1:T(8,128)(2,1)} copy(bf16[512,320]{0,1:T(8,128)(2,1)} %bitcast.12) | data formatting | bytes 655360
  91.0 0.0 copy-done.1
  91.0 0.0 copy-start
  91.0 0.7 copy.16
  91.7 0.4 copy-done
  92.1 0.0 copy-start.2
  92.1 0.7 copy.17
  92.8 0.1 copy-done.2
  93.0 0.6 copy.18
Async XLA Ops:
  89.2 1.8 %copy-start.1 = (bf16[320,512]{1,0:T(8,128)(2,1)S(1)}, bf16[320,512]{1,0:T(8,128)(2,1)}, u32[]{:S(2)}) copy-start(bf16[320,512]{1,0:T(8,128)(2,1)} %get-tuple-element.9) | copy-start | bytes 983044
  91.0 1.1 %copy-start = (bf16[320,512]{1,0:T(8,128)(2,1)S(1)}, bf16[320,512]{1,0:T(8,128)(2,1)}, u32[]{:S(2)}) copy-start(bf16[320,512]{1,0:T(8,128)(2,1)} %get-tuple-element.10) | copy-start | bytes 983044
  92.1 0.9 copy-start.2

commit v6 on v5

--- a/solution.py
+++ b/solution.py
@@ -14,6 +14,7 @@
 WIDTH = HEADS * HS
 BACK = 5
 HALF = BLK // 2
+WEIGHT_WIDTH = 384
 STRIP = 128
 WIDE = 256
 HIDDEN = -2e30
@@ -481,7 +482,9 @@
         def _():
             sums[1] = summed(0, 1).astype(BF16)
             back_first.start()
-            attn = out_t[...].T.astype(BF16)
+            attn = jnp.concatenate(
+                [out_t[...].T.astype(BF16), jnp.zeros((BLK, WEIGHT_WIDTH - WIDTH), BF16)], axis=1
+            )
             for part in range(4):
                 some = slice(WIDTH * part, WIDTH * (part + 1))
                 term = jnp.dot(cot_all[some, :], attn, preferred_element_type=F32)
@@ -540,7 +543,7 @@
     for i, copy in enumerate(y_copies):
         copy.wait_recv()
         total = total + y_in[i]
-    dw_ref[...] = total
+    dw_ref[...] = total[:, :WIDTH]
 
     for copy in edge_copies + [home_a, home_b, back_second]:
         copy.wait_recv()
@@ -612,10 +615,10 @@
             pltpu.VMEM((HALF, both), BF16),
             pltpu.VMEM((HALF, both), BF16),
             pltpu.VMEM((2, HALF, both), BF16),
-            pltpu.VMEM((4, WIDTH, WIDTH), BF16),
-            pltpu.VMEM((3, WIDTH, WIDTH), BF16),
-            pltpu.VMEM((WIDTH, WIDTH), F32),
-            pltpu.VMEM((7, 40, WIDTH), F32),
+            pltpu.VMEM((4, WIDTH, WEIGHT_WIDTH), BF16),
+            pltpu.VMEM((3, WIDTH, WEIGHT_WIDTH), BF16),
+            pltpu.VMEM((WIDTH, WEIGHT_WIDTH), F32),
+            pltpu.VMEM((7, 40, WEIGHT_WIDTH), F32),
             dma((5,)),
             dma((12,)),
             dma((blocks,)),

time: 93.9 us -> 93.8 us (level)
  no operation moved by 1% of the time
where the time goes in v6:
time: 93.8 us; the launch traced here: 93.6 us
  Pallas kernels  88.6 us (94%)
  local copies, waits for them, and re-layouts  4.33 us (5%)
    pallas_call x1, Pallas kernels, shards(): pl.pallas_call(functools.partial(kernel, tm_count, head_count), out_shape...  88.6 us
    unnamed x10, local copies, waits for them, and re-layouts  4.33 us

profile of v6, /device:TPU:1, one launch (start us, length us, event | category | flops | bytes accessed | tf_op | source)
XLA Modules:
  0.0 93.6 jit_solution(7553140269167361708)
XLA Ops:
  0.6 88.6 %shard_map.102 = (bf16[320,512]{1,0:T(8,128)(2,1)}, bf16[320,512]{1,0:T(8,128)(2,1)}, bf16[320,512]{1,0:T(8,128)(2,1)}, f32[40,320]{1,0:T(8,128)}) custom-call(s32[1,64]{1,0:T(1,128)} %bitcast.18, s32[1,64]{1,0:T(1,128)} %bitcast.19, bf16[320,512]{1,0:T(8,128)(2,1)} %bitcast.13, bf16[320,512]{1,0:T(8,128)(2,1)} %bitcast.14, bf16[320,512]{1,0:T(8,128)(2,1)} %bitcast.15, ...), custom_call_target="tpu_custom_call" | custom-call | tf_op jit(solution)/shard_map/pallas_call | solution.py:584
  89.2 0.0 copy-start.1
  89.2 1.8 %copy.15 = bf16[512,320]{0,1:T(8,128)(2,1)} copy(bf16[512,320]{0,1:T(8,128)(2,1)} %bitcast.12) | data formatting | bytes 655360
  91.0 0.0 copy-done.1
  91.0 0.0 copy-start
  91.0 0.7 copy.16
  91.7 0.4 copy-done
  92.1 0.0 copy-start.2
  92.1 0.7 copy.17
  92.8 0.1 copy-done.2
  92.9 0.6 copy.18
Async XLA Ops:
  89.2 1.8 %copy-start.1 = (bf16[320,512]{1,0:T(8,128)(2,1)S(1)}, bf16[320,512]{1,0:T(8,128)(2,1)}, u32[]{:S(2)}) copy-start(bf16[320,512]{1,0:T(8,128)(2,1)} %get-tuple-element.9) | copy-start | bytes 983044
  91.0 1.1 %copy-start = (bf16[320,512]{1,0:T(8,128)(2,1)S(1)}, bf16[320,512]{1,0:T(8,128)(2,1)}, u32[]{:S(2)}) copy-start(bf16[320,512]{1,0:T(8,128)(2,1)} %get-tuple-element.10) | copy-start | bytes 983044
  92.1 0.9 copy-start.2

commit v7 on v6

--- a/solution.py
+++ b/solution.py
@@ -69,6 +69,7 @@
     wt,
     z_in,
     z_sum,
+    z_out,
     y_in,
     local,
     sent,
@@ -92,7 +93,6 @@
     z = t // 8
     y = (t // 2) % 4
     low = t % 8
-    sides = range(1, head_count)
 
     def at(place):
         return {"tm": (place + tm_count) % tm_count}
@@ -109,7 +109,7 @@
     back_from = chip(z + inner, y + 3)
 
     greeted = [at(t - 2), at(t + 2), at(relay_from), at(back_from)]
-    greeted += [{"head": (x + head_count - i) % head_count} for i in sides]
+    greeted += [{"head": (x + head_count + by) % head_count} for by in (-1, 1)]
     greeted += [at(t - 8 * i) for i in range(1, 4)]
     greeted += [at(8 * z + (low + 8 - i) % 8) for i in range(1, 8)]
     barrier = pltpu.get_barrier_semaphore()
@@ -162,17 +162,20 @@
     relay_first = push(v_hbm, relay, sent.at[2], got_relay.at[0], at(relay_to))
     near_k.start()
     relay_first.start()
-    across = [
-        push(
-            cot_hbm,
-            cot_all.at[pl.ds(pl.multiple_of(WIDTH * x, 64), WIDTH)],
-            side_sent.at[i - 1],
-            side_got.at[i - 1],
-            {"head": (x + i) % head_count},
-        )
-        for i in sides
-    ]
-    for copy in across:
+    def cot_rows(place, first, count):
+        start = WIDTH * (place % head_count) + first
+        return cot_all.at[pl.ds(pl.multiple_of(start, 32), count)]
+
+    def aside(src, rows_there, number, by):
+        place = {"head": (x + head_count + by) % head_count}
+        return push(src, rows_there, side_sent.at[number], side_got.at[number], place)
+
+    own_cot = cot_rows(x, 0, WIDTH)
+    upper = cot_rows(x + head_count - 1, 0, WIDTH // 2)
+    lower = cot_rows(x + 1, WIDTH // 2, WIDTH // 2)
+    beside = [aside(cot_hbm, own_cot, 0, 1), aside(cot_hbm, own_cot, 1, -1)]
+    opposite = [aside(upper, upper, 2, 1), aside(lower, lower, 3, -1)]
+    for copy in beside:
         copy.start()
 
     @pl.when(y < 3)
@@ -259,6 +262,9 @@
         near_k.wait_recv()
         chain_k.start()
         pass_near_k.start()
+        for arrived, onward in zip(beside, opposite):
+            arrived.wait_recv()
+            onward.start()
         near_v.wait_recv()
         pass_near_v.start()
 
@@ -273,27 +279,27 @@
             over_first.wait_recv()
             over_second.start()
 
-        @pl.when(step == 1)
+        swapped = jnp.where(step == 0, 0, jnp.where(step < 3, 3 - step, 8 - step))
+        slot = jnp.where(core == 0, swapped, step)
+
+        @pl.when(step == 1 + core)
+        def _():
+            near_event()
+
+        @pl.when((step == 2 - core) | (step == 3) | (step == 5))
+        def _():
+            wait_slot(slot)
+
+        @pl.when(step == 4)
         def _():
             loads[3].wait()
             loads[4].wait()
-            for copy in across:
+            for copy in opposite:
                 copy.wait_recv()
             grad_t = jnp.dot(w_ref[...], cot_all[...], preferred_element_type=F32).astype(BF16)
             for j in range(HEADS):
                 mine = grad_t[HS * j : HS * (j + 1), :]
                 spread(j + HEADS, mine.T, mine)
-
-        swapped = jnp.where(step == 0, 0, jnp.where(step < 3, 3 - step, 8 - step))
-        slot = jnp.where(core == 0, swapped, step)
-
-        @pl.when(step == 1 + core)
-        def _():
-            near_event()
-
-        @pl.when((step == 2 - core) | (step == 3) | (step == 5))
-        def _():
-            wait_slot(slot)
 
         @pl.when(step == 4)
         def _():
@@ -376,7 +382,7 @@
     ]
     y_copies = [
         push(
-            z_sum.at[pl.ds(pl.multiple_of(40 * ((low + i) % 8), 8), 40)],
+            z_out.at[(low + i) % 8],
             y_in.at[i - 1],
             y_sent.at[i - 1],
             y_got.at[i - 1],
@@ -477,11 +483,6 @@
         def _():
             sums[0] = summed(0, 0).astype(BF16)
             chain.start()
-
-        @pl.when(step == 3)
-        def _():
-            sums[1] = summed(0, 1).astype(BF16)
-            back_first.start()
             attn = jnp.concatenate(
                 [out_t[...].T.astype(BF16), jnp.zeros((BLK, WEIGHT_WIDTH - WIDTH), BF16)], axis=1
             )
@@ -492,6 +493,11 @@
             for copy in z_copies:
                 copy.start()
 
+        @pl.when(step == 3)
+        def _():
+            sums[1] = summed(0, 1).astype(BF16)
+            back_first.start()
+
         @pl.when(step == 5)
         def _():
             both = summed(1, 0)
@@ -499,35 +505,42 @@
             sums[2] = (both + chain_in[...].astype(F32)).astype(BF16)
             home_a.start()
 
-        @pl.when(step == 7)
-        def _():
-            sums[3] = summed(1, 1).astype(BF16)
-
-            @pl.when(y > 0)
-            def _():
-                home_b.start()
-
-            @pl.when(y == 0)
-            def _():
-                over_back.start()
-
-            back_first.wait_recv()
-            back_second.start()
-
-        @pl.when(step == 8)
-        def _():
-            edge_copies[0].start()
-
-        @pl.when(step == 9)
-        def _():
-            edge_copies[1].start()
+        @pl.when(step == 6)
+        def _():
             for copy in z_copies:
                 copy.wait_recv()
             z_sum[...] = wt[z].astype(F32)
             for i in range(3):
                 z_sum[...] += z_in[i].astype(F32)
+            for i in range(8):
+                block = z_sum[40 * i : 40 * (i + 1), :]
+                rest = jnp.zeros((8, WEIGHT_WIDTH), F32)
+                z_out[i] = jnp.concatenate([block, rest], axis=0).astype(BF16)
             for copy in y_copies:
                 copy.start()
+
+        @pl.when(step == 7)
+        def _():
+            sums[3] = summed(1, 1).astype(BF16)
+
+            @pl.when(y > 0)
+            def _():
+                home_b.start()
+
+            @pl.when(y == 0)
+            def _():
+                over_back.start()
+
+            back_first.wait_recv()
+            back_second.start()
+
+        @pl.when(step == 8)
+        def _():
+            edge_copies[0].start()
+
+        @pl.when(step == 9)
+        def _():
+            edge_copies[1].start()
 
         @pl.when((step == 9) & (y == 0))
         def _():
@@ -542,7 +555,7 @@
     total = z_sum[pl.ds(pl.multiple_of(40 * low, 8), 40), :]
     for i, copy in enumerate(y_copies):
         copy.wait_recv()
-        total = total + y_in[i]
+        total = total + y_in[i].astype(F32)[0:40]
     dw_ref[...] = total[:, :WIDTH]
 
     for copy in edge_copies + [home_a, home_b, back_second]:
@@ -560,7 +573,7 @@
     copies += [pass_near_k, pass_near_v, pass_far_k, pass_far_v]
     copies += mated[0] + mated[1] + edge_copies
     copies += [chain, back_first, back_second, home_a, home_b]
-    for copy in across + copies + z_copies + y_copies:
+    for copy in beside + opposite + copies + z_copies + y_copies:
         copy.wait_send()
 
     @pl.when(y == 3)
@@ -618,14 +631,15 @@
             pltpu.VMEM((4, WIDTH, WEIGHT_WIDTH), BF16),
             pltpu.VMEM((3, WIDTH, WEIGHT_WIDTH), BF16),
             pltpu.VMEM((WIDTH, WEIGHT_WIDTH), F32),
-            pltpu.VMEM((7, 40, WEIGHT_WIDTH), F32),
+            pltpu.VMEM((8, 48, WEIGHT_WIDTH), BF16),
+            pltpu.VMEM((7, 48, WEIGHT_WIDTH), BF16),
             dma((5,)),
             dma((12,)),
             dma((blocks,)),
             dma((blocks,)),
             dma((2,)),
-            dma((3,)),
-            dma((3,)),
+            dma((4,)),
+            dma((4,)),
             dma((8,)),
             dma((8,)),
             dma((4,)),

time: 93.8 us -> 96.1 us (1.025)
  Pallas kernels: 88.6 us -> 90.9 us
    pallas_call x1, Pallas kernels: 88.6 us -> 90.9 us  [shards(): pl.pallas_call(functools.partial(kernel, tm_count, head_count), out_shape...]
where the time goes in v7:
time: 96.1 us; the launch traced here: 95.9 us
  Pallas kernels  90.9 us (95%)
  local copies, waits for them, and re-layouts  4.33 us (5%)
    pallas_call x1, Pallas kernels, shards(): pl.pallas_call(functools.partial(kernel, tm_count, head_count), out_shape...  90.9 us
    unnamed x10, local copies, waits for them, and re-layouts  4.33 us

profile of v7, /device:TPU:1, one launch (start us, length us, event | category | flops | bytes accessed | tf_op | source)
XLA Modules:
  0.0 95.9 jit_solution(10903849691632292035)
XLA Ops:
  0.6 90.9 %shard_map.102 = (bf16[320,512]{1,0:T(8,128)(2,1)}, bf16[320,512]{1,0:T(8,128)(2,1)}, bf16[320,512]{1,0:T(8,128)(2,1)}, f32[40,320]{1,0:T(8,128)}) custom-call(s32[1,64]{1,0:T(1,128)} %bitcast.18, s32[1,64]{1,0:T(1,128)} %bitcast.19, bf16[320,512]{1,0:T(8,128)(2,1)} %bitcast.13, bf16[320,512]{1,0:T(8,128)(2,1)} %bitcast.14, bf16[320,512]{1,0:T(8,128)(2,1)} %bitcast.15, ...), custom_call_target="tpu_custom_call" | custom-call | tf_op jit(solution)/shard_map/pallas_call | solution.py:597
  91.6 0.0 copy-start.1
  91.6 1.8 %copy.15 = bf16[512,320]{0,1:T(8,128)(2,1)} copy(bf16[512,320]{0,1:T(8,128)(2,1)} %bitcast.12) | data formatting | bytes 655360
  93.3 0.0 copy-done.1
  93.3 0.0 copy-start
  93.3 0.7 copy.16
  94.1 0.4 copy-done
  94.4 0.0 copy-start.2
  94.4 0.7 copy.17
  95.1 0.1 copy-done.2
  95.3 0.6 copy.18
Async XLA Ops:
  91.6 1.8 %copy-start.1 = (bf16[320,512]{1,0:T(8,128)(2,1)S(1)}, bf16[320,512]{1,0:T(8,128)(2,1)}, u32[]{:S(2)}) copy-start(bf16[320,512]{1,0:T(8,128)(2,1)} %get-tuple-element.9) | copy-start | bytes 983044
  93.3 1.1 %copy-start = (bf16[320,512]{1,0:T(8,128)(2,1)S(1)}, bf16[320,512]{1,0:T(8,128)(2,1)}, u32[]{:S(2)}) copy-start(bf16[320,512]{1,0:T(8,128)(2,1)} %get-tuple-element.10) | copy-start | bytes 983044
  94.4 0.9 copy-start.2

commit v8 on v4

--- a/solution.py
+++ b/solution.py
@@ -14,6 +14,7 @@
 WIDTH = HEADS * HS
 BACK = 5
 HALF = BLK // 2
+WEIGHT_WIDTH = 384
 STRIP = 128
 WIDE = 256
 HIDDEN = -2e30
@@ -68,6 +69,7 @@
     wt,
     z_in,
     z_sum,
+    z_out,
     y_in,
     local,
     sent,
@@ -89,7 +91,6 @@
     z = t // 8
     y = (t // 2) % 4
     low = t % 8
-    sides = range(1, head_count)
 
     def at(place):
         return {"tm": (place + tm_count) % tm_count}
@@ -106,7 +107,7 @@
     back_from = chip(z + inner, y + 3)
 
     greeted = [at(t - 2), at(t + 2), at(relay_from), at(back_from)]
-    greeted += [{"head": (x + head_count - i) % head_count} for i in sides]
+    greeted += [{"head": (x + head_count + by) % head_count} for by in (-1, 1)]
     greeted += [at(t - 8 * i) for i in range(1, 4)]
     greeted += [at(8 * z + (low + 8 - i) % 8) for i in range(1, 8)]
     barrier = pltpu.get_barrier_semaphore()
@@ -159,17 +160,20 @@
     relay_first = push(v_hbm, relay, sent.at[2], got_relay.at[0], at(relay_to))
     near_k.start()
     relay_first.start()
-    across = [
-        push(
-            cot_hbm,
-            cot_all.at[pl.ds(pl.multiple_of(WIDTH * x, 64), WIDTH)],
-            side_sent.at[i - 1],
-            side_got.at[i - 1],
-            {"head": (x + i) % head_count},
-        )
-        for i in sides
-    ]
-    for copy in across:
+    def cot_rows(place, first, count):
+        start = WIDTH * (place % head_count) + first
+        return cot_all.at[pl.ds(pl.multiple_of(start, 32), count)]
+
+    def aside(src, rows_there, number, by):
+        place = {"head": (x + head_count + by) % head_count}
+        return push(src, rows_there, side_sent.at[number], side_got.at[number], place)
+
+    own_cot = cot_rows(x, 0, WIDTH)
+    upper = cot_rows(x + head_count - 1, 0, WIDTH // 2)
+    lower = cot_rows(x + 1, WIDTH // 2, WIDTH // 2)
+    beside = [aside(cot_hbm, own_cot, 0, 1), aside(cot_hbm, own_cot, 1, -1)]
+    opposite = [aside(upper, upper, 2, 1), aside(lower, lower, 3, -1)]
+    for copy in beside:
         copy.start()
 
     @pl.when(y < 3)
@@ -184,8 +188,12 @@
     direct_to = at(t + 1 + 4 * core)
     direct_k = keys(k_hbm, direct_slot, 3, direct_to)
     direct_v = values(v_hbm, direct_slot, 4, direct_to)
-    direct_k.start()
-    direct_v.start()
+
+    @pl.when(core == 0)
+    def _():
+        direct_k.start()
+        direct_v.start()
+
     chain_k = keys(key_part(2), 4, 5, at(t + 2))
     relay_second = values(relay, 4, 6, at(before))
     pass_near = 3 - 2 * core
@@ -249,39 +257,47 @@
         relay_first.wait_recv()
         relay_second.start()
 
-        @pl.when(y == 3)
-        def _():
-            over_first.wait_recv()
-            over_second.start()
-
         near_k.wait_recv()
         chain_k.start()
         pass_near_k.start()
+        for arrived, onward in zip(beside, opposite):
+            arrived.wait_recv()
+            onward.start()
         near_v.wait_recv()
         pass_near_v.start()
 
     def forward(step, carry):
-        @pl.when(step == 1)
+        @pl.when((step == 1) & (core == 1))
+        def _():
+            direct_k.start()
+            direct_v.start()
+
+        @pl.when((step == 1) & (y == 3))
+        def _():
+            over_first.wait_recv()
+            over_second.start()
+
+        swapped = jnp.where(step == 0, 0, jnp.where(step < 3, 3 - step, 8 - step))
+        slot = jnp.where(core == 0, swapped, step)
+
+        @pl.when(step == 1 + core)
+        def _():
+            near_event()
+
+        @pl.when((step == 2 - core) | (step == 3) | (step == 5))
+        def _():
+            wait_slot(slot)
+
+        @pl.when(step == 4)
         def _():
             loads[3].wait()
             loads[4].wait()
-            for copy in across:
+            for copy in opposite:
                 copy.wait_recv()
             grad_t = jnp.dot(w_ref[...], cot_all[...], preferred_element_type=F32).astype(BF16)
             for j in range(HEADS):
                 mine = grad_t[HS * j : HS * (j + 1), :]
                 spread(j + HEADS, mine.T, mine)
-
-        swapped = jnp.where(step == 0, 0, jnp.where(step < 3, 3 - step, 8 - step))
-        slot = jnp.where(core == 0, swapped, step)
-
-        @pl.when(step == 1 + core)
-        def _():
-            near_event()
-
-        @pl.when((step == 2 - core) | (step == 3) | (step == 5))
-        def _():
-            wait_slot(slot)
 
         @pl.when(step == 4)
         def _():
@@ -354,7 +370,9 @@
         )
         for i in range(1, 4)
     ]
-    attn = out_t[...].T.astype(BF16)
+    attn = jnp.concatenate(
+        [out_t[...].T.astype(BF16), jnp.zeros((BLK, WEIGHT_WIDTH - WIDTH), BF16)], axis=1
+    )
     for part in range(4):
         piece = slice(WIDTH * part, WIDTH * (part + 1))
         wt[part] = jnp.dot(cot_all[piece, :], attn, preferred_element_type=F32).astype(BF16)
@@ -362,7 +380,7 @@
         copy.start()
     y_copies = [
         push(
-            z_sum.at[pl.ds(pl.multiple_of(40 * ((low + i) % 8), 8), 40)],
+            z_out.at[(low + i) % 8],
             y_in.at[i - 1],
             y_sent.at[i - 1],
             y_got.at[i - 1],
@@ -449,13 +467,6 @@
         @pl.when(step == 2)
         def _():
             to_near.start()
-            for copy in z_copies:
-                copy.wait_recv()
-            z_sum[...] = wt[z].astype(F32)
-            for i in range(3):
-                z_sum[...] += z_in[i].astype(F32)
-            for copy in y_copies:
-                copy.start()
 
         @pl.when(step == 3)
         def _():
@@ -476,6 +487,17 @@
 
             back_first.wait_recv()
             back_second.start()
+            for copy in z_copies:
+                copy.wait_recv()
+            z_sum[...] = wt[z].astype(F32)
+            for i in range(3):
+                z_sum[...] += z_in[i].astype(F32)
+            for i in range(8):
+                block = z_sum[40 * i : 40 * (i + 1), :]
+                rest = jnp.zeros((8, WEIGHT_WIDTH), F32)
+                z_out[i] = jnp.concatenate([block, rest], axis=0).astype(BF16)
+            for copy in y_copies:
+                copy.start()
 
         @pl.when(step == 4)
         def _():
@@ -494,8 +516,8 @@
     total = z_sum[pl.ds(pl.multiple_of(40 * low, 8), 40), :]
     for i, copy in enumerate(y_copies):
         copy.wait_recv()
-        total = total + y_in[i]
-    dw_ref[...] = total
+        total = total + y_in[i].astype(F32)[0:40]
+    dw_ref[...] = total[:, :WIDTH]
 
     edge_copy.wait_recv()
     home_a.wait_recv()
@@ -513,7 +535,7 @@
     copies = [near_k, near_v, relay_first, direct_k, direct_v, chain_k, relay_second]
     copies += [pass_near_k, pass_near_v, pass_far_k, pass_far_v]
     copies += [to_far, to_near, chain, back_first, back_second, home_a, home_b, edge_copy]
-    for copy in across + copies + z_copies + y_copies:
+    for copy in beside + opposite + copies + z_copies + y_copies:
         copy.wait_send()
 
     @pl.when(y == 3)
@@ -568,17 +590,18 @@
             pltpu.VMEM((HALF, both), BF16),
             pltpu.VMEM((HALF, both), BF16),
             pltpu.VMEM((BLK, both), BF16),
-            pltpu.VMEM((4, WIDTH, WIDTH), BF16),
-            pltpu.VMEM((3, WIDTH, WIDTH), BF16),
-            pltpu.VMEM((WIDTH, WIDTH), F32),
-            pltpu.VMEM((7, 40, WIDTH), F32),
+            pltpu.VMEM((4, WIDTH, WEIGHT_WIDTH), BF16),
+            pltpu.VMEM((3, WIDTH, WEIGHT_WIDTH), BF16),
+            pltpu.VMEM((WIDTH, WEIGHT_WIDTH), F32),
+            pltpu.VMEM((8, 48, WEIGHT_WIDTH), BF16),
+            pltpu.VMEM((7, 48, WEIGHT_WIDTH), BF16),
             dma((5,)),
             dma((12,)),
             dma((blocks,)),
             dma((blocks,)),
             dma((2,)),
-            dma((3,)),
-            dma((3,)),
+            dma((4,)),
+            dma((4,)),
             dma((9,)),
             dma((9,)),
             dma((3,)),

time: 90.9 us -> 91.9 us (1.011)
  the two profiles are of different devices: /device:TPU:1 before, /device:TPU:33 now
where the time goes in v8:
time: 91.9 us; the launch traced here: 91.7 us
  Pallas kernels  86.7 us (94%)
  local copies, waits for them, and re-layouts  4.33 us (5%)
    pallas_call x1, Pallas kernels, shards(): pl.pallas_call(functools.partial(kernel, tm_count, head_count), out_shape...  86.7 us
    unnamed x10, local copies, waits for them, and re-layouts  4.33 us

profile of v8, /device:TPU:33, one launch (start us, length us, event | category | flops | bytes accessed | tf_op | source)
XLA Modules:
  0.0 91.7 jit_solution(1869742940813915128)
XLA Ops:
  0.6 86.7 %shard_map.102 = (bf16[320,512]{1,0:T(8,128)(2,1)}, bf16[320,512]{1,0:T(8,128)(2,1)}, bf16[320,512]{1,0:T(8,128)(2,1)}, f32[40,320]{1,0:T(8,128)}) custom-call(s32[1,64]{1,0:T(1,128)} %bitcast.18, s32[1,64]{1,0:T(1,128)} %bitcast.19, bf16[320,512]{1,0:T(8,128)(2,1)} %bitcast.13, bf16[320,512]{1,0:T(8,128)(2,1)} %bitcast.14, bf16[320,512]{1,0:T(8,128)(2,1)} %bitcast.15, ...), custom_call_target="tpu_custom_call" | custom-call | tf_op jit(solution)/shard_map/pallas_call | solution.py:559
  87.4 0.0 copy-start.1
  87.4 1.8 %copy.15 = bf16[512,320]{0,1:T(8,128)(2,1)} copy(bf16[512,320]{0,1:T(8,128)(2,1)} %bitcast.12) | data formatting | bytes 655360
  89.1 0.0 copy-done.1
  89.1 0.0 copy-start
  89.1 0.7 copy.16
  89.9 0.4 copy-done
  90.2 0.0 copy-start.2
  90.2 0.7 copy.17
  91.0 0.1 copy-done.2
  91.1 0.6 copy.18
Async XLA Ops:
  87.4 1.8 %copy-start.1 = (bf16[320,512]{1,0:T(8,128)(2,1)S(1)}, bf16[320,512]{1,0:T(8,128)(2,1)}, u32[]{:S(2)}) copy-start(bf16[320,512]{1,0:T(8,128)(2,1)} %get-tuple-element.9) | copy-start | bytes 983044
  89.1 1.1 %copy-start = (bf16[320,512]{1,0:T(8,128)(2,1)S(1)}, bf16[320,512]{1,0:T(8,128)(2,1)}, u32[]{:S(2)}) copy-start(bf16[320,512]{1,0:T(8,128)(2,1)} %get-tuple-element.10) | copy-start | bytes 983044
  90.2 0.9 copy-start.2

commit v9 on v8

--- a/solution.py
+++ b/solution.py
@@ -35,9 +35,11 @@
     cot_hbm,
     w_hbm,
     dq_ref,
-    dk_ref,
-    dv_ref,
     dw_ref,
+    own_ref,
+    home_near,
+    home_far,
+    edge,
     slots,
     relay,
     cross,
@@ -60,16 +62,15 @@
     dkv,
     from_mate,
     sums,
-    home_near,
-    home_far,
     chain_in,
     relay_back,
     cross_back,
-    edge,
     wt,
     z_in,
     z_sum,
-    z_out,
+    pair_out,
+    pair_in,
+    y_out,
     y_in,
     local,
     sent,
@@ -82,6 +83,8 @@
     back_got,
     z_sent,
     z_got,
+    pair_sent,
+    pair_got,
     y_sent,
     y_got,
 ):
@@ -378,16 +381,22 @@
         wt[part] = jnp.dot(cot_all[piece, :], attn, preferred_element_type=F32).astype(BF16)
     for copy in z_copies:
         copy.start()
+    pair_copy = push(pair_out, pair_in, pair_sent.at[0], pair_got.at[0], mate)
     y_copies = [
         push(
-            z_out.at[(low + i) % 8],
+            y_out.at[(y + i) % 4],
             y_in.at[i - 1],
             y_sent.at[i - 1],
             y_got.at[i - 1],
-            at(8 * z + (low + i) % 8),
+            at(chip(z, y + i)),
         )
-        for i in range(1, 8)
+        for i in range(1, 4)
     ]
+
+    def weight_rows(ring_place, parity):
+        first = pl.multiple_of(80 * ring_place + 40 * parity, 8)
+        block = z_sum[pl.ds(first, 40), :]
+        return jnp.concatenate([block, jnp.zeros((8, WEIGHT_WIDTH), F32)], axis=0)
 
     far_slot, near_slot, edge_slot = 3 + 2 * core, 1 + 2 * core, 5 - 4 * core
     to_far = push(dkv.at[far_slot], from_mate.at[0], back_sent.at[0], back_got.at[0], mate)
@@ -492,16 +501,18 @@
             z_sum[...] = wt[z].astype(F32)
             for i in range(3):
                 z_sum[...] += z_in[i].astype(F32)
-            for i in range(8):
-                block = z_sum[40 * i : 40 * (i + 1), :]
-                rest = jnp.zeros((8, WEIGHT_WIDTH), F32)
-                z_out[i] = jnp.concatenate([block, rest], axis=0).astype(BF16)
+            for i in range(4):
+                pair_out[i] = weight_rows(i, 1 - core).astype(BF16)
+            pair_copy.start()
+
+        @pl.when(step == 4)
+        def _():
+            edge_copy.start()
+            pair_copy.wait_recv()
+            for i in range(4):
+                y_out[i] = (weight_rows(i, core) + pair_in[i].astype(F32)).astype(BF16)
             for copy in y_copies:
                 copy.start()
-
-        @pl.when(step == 4)
-        def _():
-            edge_copy.start()
 
             @pl.when(y == 0)
             def _():
@@ -512,39 +523,46 @@
 
     lax.fori_loop(0, BACK + 1, backward, 0)
 
+    keep = pltpu.make_async_copy(dkv.at[0], own_ref, local.at[0])
+    keep.start()
     dq_ref[...] = (dq_t[...] * HS**-0.5).astype(BF16)
-    total = z_sum[pl.ds(pl.multiple_of(40 * low, 8), 40), :]
+    total = weight_rows(y, core) + pair_in[y].astype(F32)
     for i, copy in enumerate(y_copies):
         copy.wait_recv()
-        total = total + y_in[i].astype(F32)[0:40]
-    dw_ref[...] = total[:, :WIDTH]
-
-    edge_copy.wait_recv()
-    home_a.wait_recv()
-    home_b.wait_recv()
-    back_second.wait_recv()
+        total = total + y_in[i].astype(F32)
+    dw_ref[...] = total
+    for copy in [edge_copy, home_a, home_b, back_second, keep]:
+        if copy is keep:
+            copy.wait()
+        else:
+            copy.wait_recv()
+
+    copies = [near_k, near_v, relay_first, direct_k, direct_v, chain_k, relay_second]
+    copies += [pass_near_k, pass_near_v, pass_far_k, pass_far_v]
+    copies += [to_far, to_near, chain, back_first, back_second, home_a, home_b, edge_copy]
+    for copy in beside + opposite + copies + z_copies + y_copies + [pair_copy]:
+        copy.wait_send()
+
+    @pl.when(y == 3)
+    def _():
+        over_second.wait_send()
+
+    @pl.when(y == 0)
+    def _():
+        over_home.wait_send()
+
+
+def finish_kernel(dq, dw, own, near, far, edge, dq_ref, dk_ref, dv_ref, dw_ref):
+    dq_ref[...] = dq[...]
+    dw_ref[...] = dw[0:40, :WIDTH]
     for half in range(2):
         part = slice(HALF * half, HALF * (half + 1))
-        total = dkv[0, part].astype(F32) + edge[part].astype(F32) + home_near[part].astype(F32)
+        total = own[part].astype(F32) + edge[part].astype(F32) + near[part].astype(F32)
         if half == 1:
-            total = total + home_far[...].astype(F32)
+            total = total + far[...].astype(F32)
         total_t = total.T.astype(BF16)
         dk_ref[:, part] = total_t[:WIDTH]
         dv_ref[:, part] = total_t[WIDTH:]
-
-    copies = [near_k, near_v, relay_first, direct_k, direct_v, chain_k, relay_second]
-    copies += [pass_near_k, pass_near_v, pass_far_k, pass_far_v]
-    copies += [to_far, to_near, chain, back_first, back_second, home_a, home_b, edge_copy]
-    for copy in beside + opposite + copies + z_copies + y_copies:
-        copy.wait_send()
-
-    @pl.when(y == 3)
-    def _():
-        over_second.wait_send()
-
-    @pl.when(y == 0)
-    def _():
-        over_home.wait_send()
 
 
 def shards(queries, key_rows, value_rows, cotangent, out_weight, segment_units, left_segments):
@@ -556,11 +574,19 @@
     out_t = jax.ShapeDtypeStruct((WIDTH, BLK), BF16)
     both = 2 * WIDTH
     blocks = BACK + 1
-    query_t, key_t, value_t, weight_t = pl.pallas_call(
+    block = jax.ShapeDtypeStruct((BLK, both), BF16)
+    pieces = pl.pallas_call(
         functools.partial(kernel, tm_count, head_count),
-        out_shape=(out_t, out_t, out_t, jax.ShapeDtypeStruct((40, WIDTH), F32)),
+        out_shape=(
+            out_t,
+            jax.ShapeDtypeStruct((48, WEIGHT_WIDTH), F32),
+            block,
+            block,
+            jax.ShapeDtypeStruct((HALF, both), BF16),
+            block,
+        ),
         in_specs=[vmem] * 2 + [anywhere] * 5,
-        out_specs=(vmem, vmem, vmem, vmem),
+        out_specs=(vmem, vmem, anywhere, anywhere, anywhere, anywhere),
         scratch_shapes=[
             pltpu.VMEM((blocks, both, BLK), BF16),
             pltpu.VMEM((WIDTH, BLK), BF16),
@@ -584,17 +610,16 @@
             pltpu.VMEM((blocks, BLK, both), BF16),
             pltpu.VMEM((2, BLK, both), BF16),
             pltpu.VMEM((2, BLK, both), BF16),
-            pltpu.VMEM((BLK, both), BF16),
             pltpu.VMEM((HALF, both), BF16),
             pltpu.VMEM((HALF, both), BF16),
             pltpu.VMEM((HALF, both), BF16),
-            pltpu.VMEM((HALF, both), BF16),
-            pltpu.VMEM((BLK, both), BF16),
             pltpu.VMEM((4, WIDTH, WEIGHT_WIDTH), BF16),
             pltpu.VMEM((3, WIDTH, WEIGHT_WIDTH), BF16),
             pltpu.VMEM((WIDTH, WEIGHT_WIDTH), F32),
-            pltpu.VMEM((8, 48, WEIGHT_WIDTH), BF16),
-            pltpu.VMEM((7, 48, WEIGHT_WIDTH), BF16),
+            pltpu.VMEM((4, 48, WEIGHT_WIDTH), BF16),
+            pltpu.VMEM((4, 48, WEIGHT_WIDTH), BF16),
+            pltpu.VMEM((4, 48, WEIGHT_WIDTH), BF16),
+            pltpu.VMEM((3, 48, WEIGHT_WIDTH), BF16),
             dma((5,)),
             dma((12,)),
             dma((blocks,)),
@@ -606,8 +631,10 @@
             dma((9,)),
             dma((3,)),
             dma((3,)),
-            dma((7,)),
-            dma((7,)),
+            dma((1,)),
+            dma((1,)),
+            dma((3,)),
+            dma((3,)),
         ],
         compiler_params=pltpu.CompilerParams(
             collective_id=0, has_side_effects=True, vmem_limit_bytes=60 << 20
@@ -621,6 +648,13 @@
         cotangent.T,
         out_weight,
     )
+    query_t, key_t, value_t, weight_t = pl.pallas_call(
+        finish_kernel,
+        out_shape=(out_t, out_t, out_t, jax.ShapeDtypeStruct((40, WIDTH), F32)),
+        in_specs=[vmem] * 6,
+        out_specs=(vmem, vmem, vmem, vmem),
+        compiler_params=pltpu.CompilerParams(vmem_limit_bytes=24 << 20),
+    )(*pieces)
     return (query_t.T, key_t.T, value_t.T, weight_t.T)
 
 

time: 91.9 us -> 95.6 us (1.040)
  the two profiles are of different devices: /device:TPU:33 before, /device:TPU:1 now
where the time goes in v9:
time: 95.6 us; the launch traced here: 95.2 us
  Pallas kernels  88.5 us (93%)
  local copies, waits for them, and re-layouts  6.08 us (6%)
    pallas_call x1, Pallas kernels, shards(): pl.pallas_call(functools.partial(kernel, tm_count, head_count), out_shape...  87.2 us
    unnamed x12, local copies, waits for them, and re-layouts  6.08 us

profile of v9, /device:TPU:1, one launch (start us, length us, event | category | flops | bytes accessed | tf_op | source)
XLA Modules:
  0.0 95.2 jit_solution(11869895717004680032)
XLA Ops:
  0.6 87.2 %shard_map.102 = (bf16[320,512]{1,0:T(8,128)(2,1)}, f32[48,384]{1,0:T(8,128)}, bf16[512,640]{1,0:T(8,128)(2,1)}, bf16[512,640]{1,0:T(8,128)(2,1)}, bf16[256,640]{1,0:T(8,128)(2,1)}, /*index=5*/bf16[512,640]{1,0:T(8,128)(2,1)}) custom-call(s32[1,64]{1,0:T(1,128)} %bitcast.14, s32[1,64]{1,0:T(1,128)} %bitcast.15, bf16[320,512]{1,0:T(8,128)(2,1)} %bitcast.10, ...), custom_call_target="tpu_custom_call" | custom-call | tf_op jit(solution)/shard_map/pallas_call | solution.py:578
  87.8 0.0 copy-start
  87.8 1.1 %copy-done = bf16[512,640]{1,0:T(8,128)(2,1)S(1)} copy-done((bf16[512,640]{1,0:T(8,128)(2,1)S(1)}, bf16[512,640]{1,0:T(8,128)(2,1)}, u32[]{:S(2)}) %copy-start) | copy-done | bytes 655384
  88.9 0.0 copy-start.1
  88.9 1.1 %copy-done.1 = bf16[512,640]{1,0:T(8,128)(2,1)S(1)} copy-done((bf16[512,640]{1,0:T(8,128)(2,1)S(1)}, bf16[512,640]{1,0:T(8,128)(2,1)}, u32[]{:S(2)}) %copy-start.1) | copy-done | bytes 655384
  90.0 0.0 copy-start.2
  90.0 1.1 %copy-done.2 = bf16[512,640]{1,0:T(8,128)(2,1)S(1)} copy-done((bf16[512,640]{1,0:T(8,128)(2,1)S(1)}, bf16[512,640]{1,0:T(8,128)(2,1)}, u32[]{:S(2)}) %copy-start.2) | copy-done | bytes 655384
  91.1 0.0 copy-start.3
  91.1 1.0 %copy-done.3 = bf16[320,512]{1,0:T(8,128)(2,1)S(1)} copy-done((bf16[320,512]{1,0:T(8,128)(2,1)S(1)}, bf16[320,512]{1,0:T(8,128)(2,1)}, u32[]{:S(2)}) %copy-start.3) | copy-done | bytes 327704
  92.1 0.0 copy-start.4
  92.1 1.0 %copy-done.4 = bf16[256,640]{1,0:T(8,128)(2,1)S(1)} copy-done((bf16[256,640]{1,0:T(8,128)(2,1)S(1)}, bf16[256,640]{1,0:T(8,128)(2,1)}, u32[]{:S(2)}) %copy-start.4) | copy-done | bytes 327704
  93.0 0.0 copy-start.5
  93.0 0.9 copy-done.5
  93.9 1.3 %shard_map.103 = (bf16[320,512]{1,0:T(8,128)(2,1)}, bf16[320,512]{1,0:T(8,128)(2,1)}, bf16[320,512]{1,0:T(8,128)(2,1)}, f32[40,320]{1,0:T(8,128)}) custom-call(bf16[320,512]{1,0:T(8,128)(2,1)S(1)} %copy-done.3, f32[48,384]{1,0:T(8,128)S(1)} %copy-done.5, bf16[512,640]{1,0:T(8,128)(2,1)S(1)} %copy-done, bf16[512,640]{1,0:T(8,128)(2,1)S(1)} %copy-done.1, ...), custom_call_target="tpu_custom_call" | custom-call | tf_op jit(solution)/shard_map/pallas_call | solution.py:651
Async XLA Ops:
  87.8 1.1 %copy-start = (bf16[512,640]{1,0:T(8,128)(2,1)S(1)}, bf16[512,640]{1,0:T(8,128)(2,1)}, u32[]{:S(2)}) copy-start(bf16[512,640]{1,0:T(8,128)(2,1)} %get-tuple-element.16.own) | copy-start | bytes 1966084
  88.9 1.1 %copy-start.1 = (bf16[512,640]{1,0:T(8,128)(2,1)S(1)}, bf16[512,640]{1,0:T(8,128)(2,1)}, u32[]{:S(2)}) copy-start(bf16[512,640]{1,0:T(8,128)(2,1)} %get-tuple-element.17.near) | copy-start | bytes 1966084
  90.0 1.1 %copy-start.2 = (bf16[512,640]{1,0:T(8,128)(2,1)S(1)}, bf16[512,640]{1,0:T(8,128)(2,1)}, u32[]{:S(2)}) copy-start(bf16[512,640]{1,0:T(8,128)(2,1)} %get-tuple-element.19.edge) | copy-start | bytes 1966084
  91.1 1.0 %copy-start.3 = (bf16[320,512]{1,0:T(8,128)(2,1)S(1)}, bf16[320,512]{1,0:T(8,128)(2,1)}, u32[]{:S(2)}) copy-start(bf16[320,512]{1,0:T(8,128)(2,1)} %get-tuple-element.14.dq) | copy-start | bytes 983044
  92.1 1.0 %copy-start.4 = (bf16[256,640]{1,0:T(8,128)(2,1)S(1)}, bf16[256,640]{1,0:T(8,128)(2,1)}, u32[]{:S(2)}) copy-start(bf16[256,640]{1,0:T(8,128)(2,1)} %get-tuple-element.18.far) | copy-start | bytes 983044
  93.0 0.9 copy-start.5

commit v10 on v9

--- a/solution.py
+++ b/solution.py
@@ -480,11 +480,8 @@
         @pl.when(step == 3)
         def _():
             to_near.wait_recv()
-            both = dkv[2].astype(F32) + from_mate[1].astype(F32)
-            chain.wait_recv()
-            sums[1, 0:HALF] = (both[0:HALF] + chain_in[...].astype(F32)).astype(BF16)
-            sums[1, HALF:BLK] = both[HALF:BLK].astype(BF16)
-            home_a.start()
+            both = dkv[2, HALF:BLK].astype(F32) + from_mate[1, HALF:BLK].astype(F32)
+            sums[1, HALF:BLK] = both.astype(BF16)
 
             @pl.when(y > 0)
             def _():
@@ -508,6 +505,10 @@
         @pl.when(step == 4)
         def _():
             edge_copy.start()
+            chain.wait_recv()
+            near = dkv[2, 0:HALF].astype(F32) + from_mate[1, 0:HALF].astype(F32)
+            sums[1, 0:HALF] = (near + chain_in[...].astype(F32)).astype(BF16)
+            home_a.start()
             pair_copy.wait_recv()
             for i in range(4):
                 y_out[i] = (weight_rows(i, core) + pair_in[i].astype(F32)).astype(BF16)
@@ -530,7 +531,7 @@
     for i, copy in enumerate(y_copies):
         copy.wait_recv()
         total = total + y_in[i].astype(F32)
-    dw_ref[...] = total
+    dw_ref[...] = total[0:40, :WIDTH]
     for copy in [edge_copy, home_a, home_b, back_second, keep]:
         if copy is keep:
             copy.wait()
@@ -552,17 +553,25 @@
         over_home.wait_send()
 
 
-def finish_kernel(dq, dw, own, near, far, edge, dq_ref, dk_ref, dv_ref, dw_ref):
-    dq_ref[...] = dq[...]
-    dw_ref[...] = dw[0:40, :WIDTH]
+def finish_kernel(
+    dq, dw, own, near, far, edge, dq_ref, dk_ref, dv_ref, dw_ref, own_v, near_v, far_v, edge_v, sems
+):
+    pairs = ((own, own_v), (edge, edge_v), (near, near_v), (far, far_v), (dq, dq_ref), (dw, dw_ref))
+    copies = [pltpu.make_async_copy(src, dst, sems.at[i]) for i, (src, dst) in enumerate(pairs)]
+    for copy in copies:
+        copy.start()
+    for copy in copies[:4]:
+        copy.wait()
     for half in range(2):
         part = slice(HALF * half, HALF * (half + 1))
-        total = own[part].astype(F32) + edge[part].astype(F32) + near[part].astype(F32)
+        total = own_v[part].astype(F32) + edge_v[part].astype(F32) + near_v[part].astype(F32)
         if half == 1:
-            total = total + far[...].astype(F32)
+            total = total + far_v[...].astype(F32)
         total_t = total.T.astype(BF16)
         dk_ref[:, part] = total_t[:WIDTH]
         dv_ref[:, part] = total_t[WIDTH:]
+    for copy in copies[4:]:
+        copy.wait()
 
 
 def shards(queries, key_rows, value_rows, cotangent, out_weight, segment_units, left_segments):
@@ -579,7 +588,7 @@
         functools.partial(kernel, tm_count, head_count),
         out_shape=(
             out_t,
-            jax.ShapeDtypeStruct((48, WEIGHT_WIDTH), F32),
+            jax.ShapeDtypeStruct((40, WIDTH), F32),
             block,
             block,
             jax.ShapeDtypeStruct((HALF, both), BF16),
@@ -651,9 +660,16 @@
     query_t, key_t, value_t, weight_t = pl.pallas_call(
         finish_kernel,
         out_shape=(out_t, out_t, out_t, jax.ShapeDtypeStruct((40, WIDTH), F32)),
-        in_specs=[vmem] * 6,
+        in_specs=[anywhere] * 6,
         out_specs=(vmem, vmem, vmem, vmem),
-        compiler_params=pltpu.CompilerParams(vmem_limit_bytes=24 << 20),
+        scratch_shapes=[
+            pltpu.VMEM((BLK, both), BF16),
+            pltpu.VMEM((BLK, both), BF16),
+            pltpu.VMEM((HALF, both), BF16),
+            pltpu.VMEM((BLK, both), BF16),
+            dma((6,)),
+        ],
+        compiler_params=pltpu.CompilerParams(vmem_limit_bytes=60 << 20),
     )(*pieces)
     return (query_t.T, key_t.T, value_t.T, weight_t.T)
 

time: 95.6 us -> 80.8 us (0.85)
  the two profiles are of different devices: /device:TPU:1 before, /device:TPU:0 now
where the time goes in v10:
time: 80.8 us; the launch traced here: 80.6 us
  Pallas kernels  80 us (99%)
    pallas_call x1, Pallas kernels, shards(): pl.pallas_call(functools.partial(kernel, tm_count, head_count), out_shape...  77 us
    pallas_call x1, Pallas kernels, shards(): pl.pallas_call(finish_kernel, out_shape=(out_t, out_t, out_t, jax.ShapeDt...  2.95 us

profile of v10, /device:TPU:0, one launch (start us, length us, event | category | flops | bytes accessed | tf_op | source)
XLA Modules:
  0.0 80.6 jit_solution(17108958332637207538)
XLA Ops:
  0.6 77.0 %shard_map.102 = (bf16[320,512]{1,0:T(8,128)(2,1)}, f32[40,320]{1,0:T(8,128)}, bf16[512,640]{1,0:T(8,128)(2,1)}, bf16[512,640]{1,0:T(8,128)(2,1)}, bf16[256,640]{1,0:T(8,128)(2,1)}, /*index=5*/bf16[512,640]{1,0:T(8,128)(2,1)}) custom-call(s32[1,64]{1,0:T(1,128)} %bitcast.14, s32[1,64]{1,0:T(1,128)} %bitcast.15, bf16[320,512]{1,0:T(8,128)(2,1)} %bitcast.10, ...), custom_call_target="tpu_custom_call" | custom-call | tf_op jit(solution)/shard_map/pallas_call | solution.py:587
  77.7 2.9 %shard_map.103 = (bf16[320,512]{1,0:T(8,128)(2,1)}, bf16[320,512]{1,0:T(8,128)(2,1)}, bf16[320,512]{1,0:T(8,128)(2,1)}, f32[40,320]{1,0:T(8,128)}) custom-call(bf16[320,512]{1,0:T(8,128)(2,1)} %get-tuple-element.14.dq, f32[40,320]{1,0:T(8,128)} %get-tuple-element.15.dw, bf16[512,640]{1,0:T(8,128)(2,1)} %get-tuple-element.16.own, ...), custom_call_target="tpu_custom_call" | custom-call | tf_op jit(solution)/shard_map/pallas_call | solution.py:660

commit v11 on v10

--- a/solution.py
+++ b/solution.py
@@ -16,7 +16,7 @@
 HALF = BLK // 2
 WEIGHT_WIDTH = 384
 STRIP = 128
-WIDE = 256
+WIDE = 512
 HIDDEN = -2e30
 LOWEST = -1e30
 F32 = jnp.float32
@@ -320,6 +320,7 @@
         pieces = BLK // WIDE
         units_of = HEADS * pieces
         top = None
+        late = []
         for turn in range(units_of + 1):
             last = top
             if turn < units_of:
@@ -347,12 +348,16 @@
                 total = total + jnp.sum(p.reshape(STRIP // 8, 8, WIDE), axis=0)
                 probs[slot, h, r : r + STRIP, cols] = p.astype(BF16)
             l_run[h, :, cols] = total
-            here = slice(HS * h, HS * (h + 1))
-            out_t[here, cols] = out_t[here, cols] * factor + jnp.dot(
-                slots[slot, WIDTH + HS * h : WIDTH + HS * (h + 1), :],
-                probs[slot, h, :, cols],
-                preferred_element_type=F32,
-            )
+            late.append((h, cols, factor))
+            if turn < 2:
+                continue
+            for h, cols, factor in late[-2:] if turn == units_of else late[-2:-1]:
+                here = slice(HS * h, HS * (h + 1))
+                out_t[here, cols] = out_t[here, cols] * factor + jnp.dot(
+                    slots[slot, WIDTH + HS * h : WIDTH + HS * (h + 1), :],
+                    probs[slot, h, :, cols],
+                    preferred_element_type=F32,
+                )
         return carry
 
     lax.fori_loop(0, BACK + 1, forward, 0)
@@ -426,6 +431,7 @@
         slot = jnp.where(core == 0, crossed, 5 - step)
         pieces = BLK // WIDE
         units_of = HEADS * pieces
+        done = []
         for turn in range(units_of + 1):
             if turn < units_of:
                 h, c = divmod(turn, pieces)
@@ -449,18 +455,21 @@
                 ds = p * (square[(turn - 1) % 2, down, :] - shift)
                 work[h // 2, down, ds_at : ds_at + WIDE] = ds.astype(BF16)
                 work[(h + HEADS) // 2, down, p_at : p_at + WIDE] = p.astype(BF16)
-            here = slice(HS * h, HS * (h + 1))
-            dq_t[here, cols] += jnp.dot(
-                slots[slot, here, :],
-                work[h // 2, :, ds_at : ds_at + WIDE],
-                preferred_element_type=F32,
-            )
-            if c < pieces - 1:
+            done.append(h)
+            if turn < 2:
                 continue
-            for g in ((), (0,), (3,), (1,), (2, 4))[h]:
-                dkv[slot, :, 128 * g : 128 * (g + 1)] = jnp.dot(
-                    work[g], rows[g], preferred_element_type=F32
-                ).astype(BF16)
+            for h in done[-2:] if turn == units_of else done[-2:-1]:
+                here = slice(HS * h, HS * (h + 1))
+                dq_t[here, :] += jnp.dot(
+                    slots[slot, here, :],
+                    work[h // 2, :, BLK * (h % 2) : BLK * (h % 2 + 1)],
+                    preferred_element_type=F32,
+                )
+                for g in ((), (0,), (3,), (1,), (2, 4))[h]:
+                    dkv[slot, :, 128 * g : 128 * (g + 1)] = (
+                        jnp.dot(work[g, :, 0:BLK], rows[g, 0:BLK], preferred_element_type=F32)
+                        + jnp.dot(work[g, :, BLK:], rows[g, BLK:], preferred_element_type=F32)
+                    ).astype(BF16)
 
         @pl.when(step == 0)
         def _():
@@ -554,23 +563,38 @@
 
 
 def finish_kernel(
-    dq, dw, own, near, far, edge, dq_ref, dk_ref, dv_ref, dw_ref, own_v, near_v, far_v, edge_v, sems
+    dq, dw, own, near, far, edge, dq_ref, dk_ref, dv_ref, dw_ref, held, far_v, done, sems, out_sems
 ):
-    pairs = ((own, own_v), (edge, edge_v), (near, near_v), (far, far_v), (dq, dq_ref), (dw, dw_ref))
-    copies = [pltpu.make_async_copy(src, dst, sems.at[i]) for i, (src, dst) in enumerate(pairs)]
-    for copy in copies:
+    through = [
+        pltpu.make_async_copy(dq, dq_ref, out_sems.at[0]),
+        pltpu.make_async_copy(dw, dw_ref, out_sems.at[1]),
+    ]
+    halves = [slice(HALF * half, HALF * (half + 1)) for half in range(2)]
+    loads = [
+        [
+            pltpu.make_async_copy(src.at[part], held.at[i, part], sems.at[3 * half + i])
+            for i, src in enumerate((own, edge, near))
+        ]
+        for half, part in enumerate(halves)
+    ]
+    loads[1].append(pltpu.make_async_copy(far, far_v, sems.at[6]))
+    for copy in loads[0] + loads[1] + through:
         copy.start()
-    for copy in copies[:4]:
-        copy.wait()
-    for half in range(2):
-        part = slice(HALF * half, HALF * (half + 1))
-        total = own_v[part].astype(F32) + edge_v[part].astype(F32) + near_v[part].astype(F32)
+    for half, part in enumerate(halves):
+        for copy in loads[half]:
+            copy.wait()
+        total = held[0, part].astype(F32) + held[1, part].astype(F32) + held[2, part].astype(F32)
         if half == 1:
             total = total + far_v[...].astype(F32)
-        total_t = total.T.astype(BF16)
-        dk_ref[:, part] = total_t[:WIDTH]
-        dv_ref[:, part] = total_t[WIDTH:]
-    for copy in copies[4:]:
+        done[:, part] = total.T.astype(BF16)
+        for i, dst in enumerate((dk_ref, dv_ref)):
+            rows = slice(WIDTH * i, WIDTH * (i + 1))
+            copy = pltpu.make_async_copy(
+                done.at[rows, part], dst.at[:, part], out_sems.at[2 + 2 * half + i]
+            )
+            copy.start()
+            through.append(copy)
+    for copy in through:
         copy.wait()
 
 
@@ -661,12 +685,12 @@
         finish_kernel,
         out_shape=(out_t, out_t, out_t, jax.ShapeDtypeStruct((40, WIDTH), F32)),
         in_specs=[anywhere] * 6,
-        out_specs=(vmem, vmem, vmem, vmem),
+        out_specs=(anywhere, anywhere, anywhere, anywhere),
         scratch_shapes=[
-            pltpu.VMEM((BLK, both), BF16),
-            pltpu.VMEM((BLK, both), BF16),
+            pltpu.VMEM((3, BLK, both), BF16),
             pltpu.VMEM((HALF, both), BF16),
-            pltpu.VMEM((BLK, both), BF16),
+            pltpu.VMEM((both, BLK), BF16),
+            dma((7,)),
             dma((6,)),
         ],
         compiler_params=pltpu.CompilerParams(vmem_limit_bytes=60 << 20),

time: 80.8 us -> 88.5 us (1.095)
  Pallas kernels: 80 us -> 87.7 us
    pallas_call x1, Pallas kernels: 2.95 us -> 13 us  [shards(): pl.pallas_call(finish_kernel, out_shape=(out_t, out_t, out_t, jax.ShapeDt...]
    pallas_call x1, Pallas kernels: 77 us -> 74.7 us  [shards(): pl.pallas_call(functools.partial(kernel, tm_count, head_count), out_shape...]
where the time goes in v11:
time: 88.5 us; the launch traced here: 88.3 us
  Pallas kernels  87.7 us (99%)
    pallas_call x1, Pallas kernels, shards(): pl.pallas_call(functools.partial(kernel, tm_count, head_count), out_shape...  74.7 us
    pallas_call x1, Pallas kernels, shards(): pl.pallas_call(finish_kernel, out_shape=(out_t, out_t, out_t, jax.ShapeDt...  13 us

profile of v11, /device:TPU:0, one launch (start us, length us, event | category | flops | bytes accessed | tf_op | source)
XLA Modules:
  0.0 88.3 jit_solution(6250534944808996648)
XLA Ops:
  0.6 74.7 %shard_map.102 = (bf16[320,512]{1,0:T(8,128)(2,1)}, f32[40,320]{1,0:T(8,128)}, bf16[512,640]{1,0:T(8,128)(2,1)}, bf16[512,640]{1,0:T(8,128)(2,1)}, bf16[256,640]{1,0:T(8,128)(2,1)}, /*index=5*/bf16[512,640]{1,0:T(8,128)(2,1)}) custom-call(s32[1,64]{1,0:T(1,128)} %bitcast.14, s32[1,64]{1,0:T(1,128)} %bitcast.15, bf16[320,512]{1,0:T(8,128)(2,1)} %bitcast.10, ...), custom_call_target="tpu_custom_call" | custom-call | tf_op jit(solution)/shard_map/pallas_call | solution.py:611
  75.3 13.0 %shard_map.103 = (bf16[320,512]{1,0:T(8,128)(2,1)}, bf16[320,512]{1,0:T(8,128)(2,1)}, bf16[320,512]{1,0:T(8,128)(2,1)}, f32[40,320]{1,0:T(8,128)}) custom-call(bf16[320,512]{1,0:T(8,128)(2,1)} %get-tuple-element.14.dq, f32[40,320]{1,0:T(8,128)} %get-tuple-element.15.dw, bf16[512,640]{1,0:T(8,128)(2,1)} %get-tuple-element.16.own, ...), custom_call_target="tpu_custom_call" | custom-call | tf_op jit(solution)/shard_map/pallas_call | solution.py:684

commit v12 on v11

--- a/solution.py
+++ b/solution.py
@@ -478,9 +478,10 @@
         @pl.when(step == 1)
         def _():
             to_far.wait_recv()
-            sums[0] = (dkv[4].astype(F32) + from_mate[0].astype(F32)).astype(BF16)
-            chain.start()
-            back_first.start()
+            for part, copy in ((slice(0, HALF), chain), (slice(HALF, BLK), back_first)):
+                both = dkv[4, part].astype(F32) + from_mate[0, part].astype(F32)
+                sums[0, part] = both.astype(BF16)
+                copy.start()
 
         @pl.when(step == 2)
         def _():
@@ -563,12 +564,8 @@
 
 
 def finish_kernel(
-    dq, dw, own, near, far, edge, dq_ref, dk_ref, dv_ref, dw_ref, held, far_v, done, sems, out_sems
+    dq, dw, own, near, far, edge, dq_ref, dk_ref, dv_ref, dw_ref, held, far_v, sems
 ):
-    through = [
-        pltpu.make_async_copy(dq, dq_ref, out_sems.at[0]),
-        pltpu.make_async_copy(dw, dw_ref, out_sems.at[1]),
-    ]
     halves = [slice(HALF * half, HALF * (half + 1)) for half in range(2)]
     loads = [
         [
@@ -578,6 +575,10 @@
         for half, part in enumerate(halves)
     ]
     loads[1].append(pltpu.make_async_copy(far, far_v, sems.at[6]))
+    through = [
+        pltpu.make_async_copy(dq, dq_ref, sems.at[7]),
+        pltpu.make_async_copy(dw, dw_ref, sems.at[8]),
+    ]
     for copy in loads[0] + loads[1] + through:
         copy.start()
     for half, part in enumerate(halves):
@@ -586,14 +587,9 @@
         total = held[0, part].astype(F32) + held[1, part].astype(F32) + held[2, part].astype(F32)
         if half == 1:
             total = total + far_v[...].astype(F32)
-        done[:, part] = total.T.astype(BF16)
-        for i, dst in enumerate((dk_ref, dv_ref)):
-            rows = slice(WIDTH * i, WIDTH * (i + 1))
-            copy = pltpu.make_async_copy(
-                done.at[rows, part], dst.at[:, part], out_sems.at[2 + 2 * half + i]
-            )
-            copy.start()
-            through.append(copy)
+        total_t = total.T.astype(BF16)
+        dk_ref[:, part] = total_t[:WIDTH]
+        dv_ref[:, part] = total_t[WIDTH:]
     for copy in through:
         copy.wait()
 
@@ -685,13 +681,11 @@
         finish_kernel,
         out_shape=(out_t, out_t, out_t, jax.ShapeDtypeStruct((40, WIDTH), F32)),
         in_specs=[anywhere] * 6,
-        out_specs=(anywhere, anywhere, anywhere, anywhere),
+        out_specs=(vmem, vmem, vmem, vmem),
         scratch_shapes=[
             pltpu.VMEM((3, BLK, both), BF16),
             pltpu.VMEM((HALF, both), BF16),
-            pltpu.VMEM((both, BLK), BF16),
-            dma((7,)),
-            dma((6,)),
+            dma((9,)),
         ],
         compiler_params=pltpu.CompilerParams(vmem_limit_bytes=60 << 20),
     )(*pieces)

time: 88.5 us -> 78.3 us (0.88)
  Pallas kernels: 87.7 us -> 77.5 us
    pallas_call x1, Pallas kernels: 13 us -> 2.83 us  [shards(): pl.pallas_call(finish_kernel, out_shape=(out_t, out_t, out_t, jax.ShapeDt...]
where the time goes in v12:
time: 78.3 us; the launch traced here: 78.2 us
  Pallas kernels  77.5 us (99%)
    pallas_call x1, Pallas kernels, shards(): pl.pallas_call(functools.partial(kernel, tm_count, head_count), out_shape...  74.7 us
    pallas_call x1, Pallas kernels, shards(): pl.pallas_call(finish_kernel, out_shape=(out_t, out_t, out_t, jax.ShapeDt...  2.83 us

profile of v12, /device:TPU:0, one launch (start us, length us, event | category | flops | bytes accessed | tf_op | source)
XLA Modules:
  0.0 78.2 jit_solution(14390604695819610205)
XLA Ops:
  0.6 74.7 %shard_map.102 = (bf16[320,512]{1,0:T(8,128)(2,1)}, f32[40,320]{1,0:T(8,128)}, bf16[512,640]{1,0:T(8,128)(2,1)}, bf16[512,640]{1,0:T(8,128)(2,1)}, bf16[256,640]{1,0:T(8,128)(2,1)}, /*index=5*/bf16[512,640]{1,0:T(8,128)(2,1)}) custom-call(s32[1,64]{1,0:T(1,128)} %bitcast.14, s32[1,64]{1,0:T(1,128)} %bitcast.15, bf16[320,512]{1,0:T(8,128)(2,1)} %bitcast.10, ...), custom_call_target="tpu_custom_call" | custom-call | tf_op jit(solution)/shard_map/pallas_call | solution.py:607
  75.3 2.8 %shard_map.103 = (bf16[320,512]{1,0:T(8,128)(2,1)}, bf16[320,512]{1,0:T(8,128)(2,1)}, bf16[320,512]{1,0:T(8,128)(2,1)}, f32[40,320]{1,0:T(8,128)}) custom-call(bf16[320,512]{1,0:T(8,128)(2,1)} %get-tuple-element.14.dq, f32[40,320]{1,0:T(8,128)} %get-tuple-element.15.dw, bf16[512,640]{1,0:T(8,128)(2,1)} %get-tuple-element.16.own, ...), custom_call_target="tpu_custom_call" | custom-call | tf_op jit(solution)/shard_map/pallas_call | solution.py:680

commit v13 on v12

--- a/solution.py
+++ b/solution.py
@@ -70,6 +70,7 @@
     z_sum,
     pair_out,
     pair_in,
+    z_out,
     y_out,
     y_in,
     local,
@@ -372,21 +373,13 @@
         delta[h, 0:1, :] = jnp.sum(out * own_grad, axis=0, keepdims=True)
         l_run[h, 0:1, :] = m_run[h, 0:1, :] + jnp.log(total)
 
+    pair_copy = push(pair_out, pair_in, pair_sent.at[0], pair_got.at[0], mate)
     z_copies = [
         push(
-            wt.at[(z + i) % 4], z_in.at[i - 1], z_sent.at[i - 1], z_got.at[i - 1], at(t + 8 * i)
+            z_out.at[(z + i) % 4], z_in.at[i - 1], z_sent.at[i - 1], z_got.at[i - 1], at(t + 8 * i)
         )
         for i in range(1, 4)
     ]
-    attn = jnp.concatenate(
-        [out_t[...].T.astype(BF16), jnp.zeros((BLK, WEIGHT_WIDTH - WIDTH), BF16)], axis=1
-    )
-    for part in range(4):
-        piece = slice(WIDTH * part, WIDTH * (part + 1))
-        wt[part] = jnp.dot(cot_all[piece, :], attn, preferred_element_type=F32).astype(BF16)
-    for copy in z_copies:
-        copy.start()
-    pair_copy = push(pair_out, pair_in, pair_sent.at[0], pair_got.at[0], mate)
     y_copies = [
         push(
             y_out.at[(y + i) % 4],
@@ -398,9 +391,9 @@
         for i in range(1, 4)
     ]
 
-    def weight_rows(ring_place, parity):
+    def weight_rows(quarter, ring_place, parity):
         first = pl.multiple_of(80 * ring_place + 40 * parity, 8)
-        block = z_sum[pl.ds(first, 40), :]
+        block = wt[quarter, pl.ds(first, 40), :]
         return jnp.concatenate([block, jnp.zeros((8, WEIGHT_WIDTH), F32)], axis=0)
 
     far_slot, near_slot, edge_slot = 3 + 2 * core, 1 + 2 * core, 5 - 4 * core
@@ -503,13 +496,15 @@
 
             back_first.wait_recv()
             back_second.start()
-            for copy in z_copies:
-                copy.wait_recv()
-            z_sum[...] = wt[z].astype(F32)
-            for i in range(3):
-                z_sum[...] += z_in[i].astype(F32)
-            for i in range(4):
-                pair_out[i] = weight_rows(i, 1 - core).astype(BF16)
+            attn = jnp.concatenate(
+                [out_t[...].T.astype(BF16), jnp.zeros((BLK, WEIGHT_WIDTH - WIDTH), BF16)], axis=1
+            )
+            for part in range(4):
+                piece = slice(WIDTH * part, WIDTH * (part + 1))
+                wt[part] = jnp.dot(cot_all[piece, :], attn, preferred_element_type=F32)
+            for part in range(4):
+                for i in range(4):
+                    pair_out[part, i] = weight_rows(part, i, 1 - core).astype(BF16)
             pair_copy.start()
 
         @pl.when(step == 4)
@@ -520,9 +515,11 @@
             sums[1, 0:HALF] = (near + chain_in[...].astype(F32)).astype(BF16)
             home_a.start()
             pair_copy.wait_recv()
-            for i in range(4):
-                y_out[i] = (weight_rows(i, core) + pair_in[i].astype(F32)).astype(BF16)
-            for copy in y_copies:
+            for part in range(4):
+                for i in range(4):
+                    both = weight_rows(part, i, core) + pair_in[part, i].astype(F32)
+                    z_out[part, i] = both.astype(BF16)
+            for copy in z_copies:
                 copy.start()
 
             @pl.when(y == 0)
@@ -537,7 +534,15 @@
     keep = pltpu.make_async_copy(dkv.at[0], own_ref, local.at[0])
     keep.start()
     dq_ref[...] = (dq_t[...] * HS**-0.5).astype(BF16)
-    total = weight_rows(y, core) + pair_in[y].astype(F32)
+    for copy in z_copies:
+        copy.wait_recv()
+    z_sum[...] = z_out[z].astype(F32)
+    for i in range(3):
+        z_sum[...] += z_in[i].astype(F32)
+    y_out[...] = z_sum[...].astype(BF16)
+    for copy in y_copies:
+        copy.start()
+    total = z_sum[y]
     for i, copy in enumerate(y_copies):
         copy.wait_recv()
         total = total + y_in[i].astype(F32)
@@ -642,11 +647,12 @@
             pltpu.VMEM((HALF, both), BF16),
             pltpu.VMEM((HALF, both), BF16),
             pltpu.VMEM((HALF, both), BF16),
-            pltpu.VMEM((4, WIDTH, WEIGHT_WIDTH), BF16),
-            pltpu.VMEM((3, WIDTH, WEIGHT_WIDTH), BF16),
-            pltpu.VMEM((WIDTH, WEIGHT_WIDTH), F32),
-            pltpu.VMEM((4, 48, WEIGHT_WIDTH), BF16),
-            pltpu.VMEM((4, 48, WEIGHT_WIDTH), BF16),
+            pltpu.VMEM((4, WIDTH, WEIGHT_WIDTH), F32),
+            pltpu.VMEM((3, 4, 48, WEIGHT_WIDTH), BF16),
+            pltpu.VMEM((4, 48, WEIGHT_WIDTH), F32),
+            pltpu.VMEM((4, 4, 48, WEIGHT_WIDTH), BF16),
+            pltpu.VMEM((4, 4, 48, WEIGHT_WIDTH), BF16),
+            pltpu.VMEM((4, 4, 48, WEIGHT_WIDTH), BF16),
             pltpu.VMEM((4, 48, WEIGHT_WIDTH), BF16),
             pltpu.VMEM((3, 48, WEIGHT_WIDTH), BF16),
             dma((5,)),

time: 78.3 us -> 84.2 us (1.075)
  the two profiles are of different devices: /device:TPU:0 before, /device:TPU:64 now
where the time goes in v13:
time: 84.2 us; the launch traced here: 84.1 us
  Pallas kernels  83.4 us (99%)
    pallas_call x1, Pallas kernels, shards(): pl.pallas_call(functools.partial(kernel, tm_count, head_count), out_shape...  80.6 us
    pallas_call x1, Pallas kernels, shards(): pl.pallas_call(finish_kernel, out_shape=(out_t, out_t, out_t, jax.ShapeDt...  2.83 us

profile of v13, /device:TPU:64, one launch (start us, length us, event | category | flops | bytes accessed | tf_op | source)
XLA Modules:
  0.0 84.1 jit_solution(6225024867356314404)
XLA Ops:
  0.6 80.6 %shard_map.102 = (bf16[320,512]{1,0:T(8,128)(2,1)}, f32[40,320]{1,0:T(8,128)}, bf16[512,640]{1,0:T(8,128)(2,1)}, bf16[512,640]{1,0:T(8,128)(2,1)}, bf16[256,640]{1,0:T(8,128)(2,1)}, /*index=5*/bf16[512,640]{1,0:T(8,128)(2,1)}) custom-call(s32[1,64]{1,0:T(1,128)} %bitcast.14, s32[1,64]{1,0:T(1,128)} %bitcast.15, bf16[320,512]{1,0:T(8,128)(2,1)} %bitcast.10, ...), custom_call_target="tpu_custom_call" | custom-call | tf_op jit(solution)/shard_map/pallas_call | solution.py:612
  81.2 2.8 %shard_map.103 = (bf16[320,512]{1,0:T(8,128)(2,1)}, bf16[320,512]{1,0:T(8,128)(2,1)}, bf16[320,512]{1,0:T(8,128)(2,1)}, f32[40,320]{1,0:T(8,128)}) custom-call(bf16[320,512]{1,0:T(8,128)(2,1)} %get-tuple-element.14.dq, f32[40,320]{1,0:T(8,128)} %get-tuple-element.15.dw, bf16[512,640]{1,0:T(8,128)(2,1)} %get-tuple-element.16.own, ...), custom_call_target="tpu_custom_call" | custom-call | tf_op jit(solution)/shard_map/pallas_call | solution.py:686

commit v14 on v12

--- a/solution.py
+++ b/solution.py
@@ -486,23 +486,6 @@
         @pl.when(step == 2)
         def _():
             to_near.start()
-
-        @pl.when(step == 3)
-        def _():
-            to_near.wait_recv()
-            both = dkv[2, HALF:BLK].astype(F32) + from_mate[1, HALF:BLK].astype(F32)
-            sums[1, HALF:BLK] = both.astype(BF16)
-
-            @pl.when(y > 0)
-            def _():
-                home_b.start()
-
-            @pl.when(y == 0)
-            def _():
-                over_back.start()
-
-            back_first.wait_recv()
-            back_second.start()
             for copy in z_copies:
                 copy.wait_recv()
             z_sum[...] = wt[z].astype(F32)
@@ -512,6 +495,28 @@
                 pair_out[i] = weight_rows(i, 1 - core).astype(BF16)
             pair_copy.start()
 
+        @pl.when(step == 3)
+        def _():
+            to_near.wait_recv()
+            both = dkv[2, HALF:BLK].astype(F32) + from_mate[1, HALF:BLK].astype(F32)
+            sums[1, HALF:BLK] = both.astype(BF16)
+
+            @pl.when(y > 0)
+            def _():
+                home_b.start()
+
+            @pl.when(y == 0)
+            def _():
+                over_back.start()
+
+            back_first.wait_recv()
+            back_second.start()
+            pair_copy.wait_recv()
+            for i in range(4):
+                y_out[i] = (weight_rows(i, core) + pair_in[i].astype(F32)).astype(BF16)
+            for copy in y_copies:
+                copy.start()
+
         @pl.when(step == 4)
         def _():
             edge_copy.start()
@@ -519,11 +524,6 @@
             near = dkv[2, 0:HALF].astype(F32) + from_mate[1, 0:HALF].astype(F32)
             sums[1, 0:HALF] = (near + chain_in[...].astype(F32)).astype(BF16)
             home_a.start()
-            pair_copy.wait_recv()
-            for i in range(4):
-                y_out[i] = (weight_rows(i, core) + pair_in[i].astype(F32)).astype(BF16)
-            for copy in y_copies:
-                copy.start()
 
             @pl.when(y == 0)
             def _():

time: 78.3 us -> 82 us (1.047)
  the two profiles are of different devices: /device:TPU:0 before, /device:TPU:1 now
where the time goes in v14:
time: 82 us; the launch traced here: 81.8 us
  Pallas kernels  81.2 us (99%)
    pallas_call x1, Pallas kernels, shards(): pl.pallas_call(functools.partial(kernel, tm_count, head_count), out_shape...  78.4 us
    pallas_call x1, Pallas kernels, shards(): pl.pallas_call(finish_kernel, out_shape=(out_t, out_t, out_t, jax.ShapeDt...  2.83 us

profile of v14, /device:TPU:1, one launch (start us, length us, event | category | flops | bytes accessed | tf_op | source)
XLA Modules:
  0.0 81.8 jit_solution(12001221040675762175)
XLA Ops:
  0.6 78.4 %shard_map.102 = (bf16[320,512]{1,0:T(8,128)(2,1)}, f32[40,320]{1,0:T(8,128)}, bf16[512,640]{1,0:T(8,128)(2,1)}, bf16[512,640]{1,0:T(8,128)(2,1)}, bf16[256,640]{1,0:T(8,128)(2,1)}, /*index=5*/bf16[512,640]{1,0:T(8,128)(2,1)}) custom-call(s32[1,64]{1,0:T(1,128)} %bitcast.14, s32[1,64]{1,0:T(1,128)} %bitcast.15, bf16[320,512]{1,0:T(8,128)(2,1)} %bitcast.10, ...), custom_call_target="tpu_custom_call" | custom-call | tf_op jit(solution)/shard_map/pallas_call | solution.py:607
  79.0 2.8 %shard_map.103 = (bf16[320,512]{1,0:T(8,128)(2,1)}, bf16[320,512]{1,0:T(8,128)(2,1)}, bf16[320,512]{1,0:T(8,128)(2,1)}, f32[40,320]{1,0:T(8,128)}) custom-call(bf16[320,512]{1,0:T(8,128)(2,1)} %get-tuple-element.14.dq, f32[40,320]{1,0:T(8,128)} %get-tuple-element.15.dw, bf16[512,640]{1,0:T(8,128)(2,1)} %get-tuple-element.16.own, ...), custom_call_target="tpu_custom_call" | custom-call | tf_op jit(solution)/shard_map/pallas_call | solution.py:680
